TPU v7x, 32 devices: a whole 2x2x4 slice. The times are simulated.
32 devices in a mesh: gz: 4 (over y, core), gy: 8 (over z, x).
Axes of the slice: x: 2, y: 2, z: 4, core: 2. Of those that a mesh axis runs over, the one named last changes fastest.
Arguments:
- input_field: float32 [32, 16, 64, 256], P(None, 'gz', 'gy'), may hold values from -6 to 6
- pre_activation: float32 [32, 16, 64, 256], P(None, 'gz', 'gy'), may hold values from -8 to 8
- cotangent: float32 [32, 16, 64, 256], P(None, 'gz', 'gy'), may hold values from -6 to 6
- spectral_weights: float32 [2, 16, 32, 32, 32, 32], P(None, None, 'gz', 'gy'), may hold values from -4.2426405 to 4.2426405
- mix_weights: float32 [32, 32], replicated, may hold values from -1 to 1
- coefficients: float32 [5, 32], replicated, may hold values from -3 to 3
Outputs:
- grad_input: float32 [32, 16, 64, 256], P(None, 'gz', 'gy')
- grad_spectral: float32 [2, 16, 32, 32, 32, 32], P(None, None, 'gz', 'gy')
- grad_mix: float32 [32, 32], replicated
- grad_coef: float32 [5, 32], replicated
All inputs are finite; a program needn't handle non-finite values.
Results may differ from a plain program's by a relative error of at most 0.00013.
Values sent between devices are 32-bit elements; how exact they have to be, the bound alone decides.
No kernel may reach another device: no remote copies, remote signals or barrier semaphores. Data moves between devices by JAX's collectives and lax.ppermute only.
A program may use at most 192 MiB of HBM per device.

v0:
```python
import functools
import math

import jax
import jax.numpy as jnp
import numpy as np
from jax import lax
from jax.experimental import pallas as pl
from jax.experimental.pallas import tpu as pltpu
from jax.sharding import PartitionSpec as P

PRECISION = lax.Precision.HIGH
MIB = 1 << 20
SUB = 8
LANES = 128


def dot(left, right, dims=((1,), (0,)), precision=PRECISION):
    return lax.dot_general(
        left, right, (dims, ((), ())), precision=precision, preferred_element_type=jnp.float32
    )


def call(body, outs, operands, limit_mib, flops, bytes_accessed, scratch=(), **grid):
    return pl.pallas_call(
        body,
        out_shape=outs,
        scratch_shapes=list(scratch),
        compiler_params=pltpu.CompilerParams(vmem_limit_bytes=limit_mib * MIB),
        cost_estimate=pl.CostEstimate(
            flops=flops, bytes_accessed=bytes_accessed, transcendentals=0
        ),
        **grid,
    )(*operands)


def f32(*shape):
    return jax.ShapeDtypeStruct(shape, jnp.float32)


def mode_numbers(number):
    positions = np.arange(number)
    return np.where(positions < number // 2, positions, positions - number)


def angles(cells, modes):
    product = np.mod(np.arange(cells)[:, None] * mode_numbers(modes)[None, :], cells)
    return product * (2.0 * math.pi / cells)


def table_x(cells, modes):
    theta = angles(cells, modes)
    pair = np.stack([np.cos(theta), -np.sin(theta)], axis=2)
    return pair.reshape(cells, 2 * modes).astype(np.float32)


def wide_columns(table):
    spare = -table.shape[1] % LANES
    return np.pad(table, ((0, 0), (0, spare)))


def table_rows(cells, modes):
    theta = angles(cells, modes).T
    cos, sin = np.cos(theta), np.sin(theta)
    return np.block([[cos, sin], [-sin, cos]]).astype(np.float32)


def order_z(groups, depth):
    part, cell = np.meshgrid(np.arange(2), np.arange(groups * depth), indexing="ij")
    index = (part * groups * depth + cell).reshape(2, groups, depth)
    return index.transpose(1, 0, 2).reshape(-1)


def gelu_slope(values):
    normal_cdf = 0.5 * (1.0 + lax.erf(values * 0.7071067811865476))
    return normal_cdf + values * jnp.exp(-0.5 * values * values) * 0.3989422804014327


def x_kernel(sizes, in_ref, pre_ref, cot_ref, tab_ref, slope_ref, send_ref, ylast_ref, yfirst_ref,
             zlast_ref, zfirst_ref, work_ref, half_ref):
    C, zl, yl, dests, kr = sizes
    slope = cot_ref[...] * gelu_slope(pre_ref[...])
    slope_ref[...] = slope
    for f in range(2):
        field = in_ref[...] if f == 0 else slope
        work_ref[f] = dot(field, tab_ref[...])
        for y in range(yl):
            rows = [work_ref[f, pl.ds(z * yl + y, C, stride=zl * yl), :] for z in range(zl)]
            turned = jnp.concatenate(rows, axis=0).T
            for d in range(dests):
                send_ref[pl.ds(((d * 2 + f) * yl + y) * kr, kr), :] = turned[d * kr : (d + 1) * kr]
    for half in range(slope_ref.shape[1] // LANES):
        cut = pl.ds(half * LANES, LANES)
        half_ref[...] = slope[:, half * LANES : (half + 1) * LANES]
        for z in range(zl):
            to = pl.ds(z * C, C)
            ylast_ref[to, cut] = half_ref[pl.ds(z * yl + yl - 1, C, stride=zl * yl), :]
            yfirst_ref[to, cut] = half_ref[pl.ds(z * yl, C, stride=zl * yl), :]
    for c in range(C):
        zlast_ref[pl.ds(c * yl, yl), :] = slope_ref[pl.ds((c * zl + zl - 1) * yl, yl), :]
        zfirst_ref[pl.ds(c * yl, yl), :] = slope_ref[pl.ds(c * zl * yl, yl), :]


def widen(values, lanes):
    spare = lanes - values.shape[1]
    if spare == 0:
        return values
    return jnp.concatenate([values, jnp.zeros((values.shape[0], spare), jnp.float32)], axis=1)


def y_kernel(sizes, recv_ref, tab_ref, send_ref):
    C, zl, kxl, ky, kyl, yl, sources = sizes
    kr = 2 * kxl
    lanes = zl * C
    pieces = []
    for kx in range(kxl):
        for f in range(2):
            pieces.append(
                jnp.concatenate(
                    [
                        recv_ref[pl.ds((s * 2 + f) * yl * kr + kx * 2 + r, yl, stride=kr), :]
                        for r in range(2)
                        for s in range(sources)
                    ],
                    axis=0,
                )
            )
    out = dot(tab_ref[...], jnp.concatenate(pieces, axis=1))
    for f in range(2):
        for r in range(2):
            for z in range(zl):
                parts = []
                for kx in range(kxl):
                    base = (kx * 2 + f) * lanes + z * C
                    parts.append(out[r * ky : (r + 1) * ky, base : base + C])
                block = widen(jnp.concatenate(parts, axis=1), send_ref.shape[1])
                for g in range(ky // kyl):
                    start = (g * 2 + f) * kyl * 2 * zl + r * zl + z
                    send_ref[pl.ds(start, kyl, stride=2 * zl), :] = block[g * kyl : (g + 1) * kyl]


def spread(rows, C, kxl, eye, ones):
    n = rows.shape[0]
    high = rows.astype(jnp.bfloat16).astype(jnp.float32)
    both = jnp.concatenate([high, rows - high], axis=1)
    wide = jnp.broadcast_to(both[:, None, :], (n, C, both.shape[1]))
    wide = wide * eye[None]
    wide = wide.reshape(n * C, both.shape[1]).astype(jnp.bfloat16)
    return dot(wide, ones, precision=None)


def z_kernel(sizes, recv_ref, tab_ref, inv_ref, eye_ref, ones_ref, weights_ref, part_ref,
             send_ref, hat_ref):
    C, zl, kxl, kyl, kz, groups, part_rows, scale = sizes
    kc = kxl * C
    rows = 2 * zl
    chunk = kyl * rows
    wide = send_ref.shape[1]
    cols = []
    for k in range(kyl):
        for f in range(2):
            cols.append(
                jnp.concatenate(
                    [
                        recv_ref[pl.ds((s * 2 + f) * chunk + k * rows, rows), :]
                        for s in range(groups)
                    ],
                    axis=0,
                )
            )
    hat = dot(tab_ref[...], jnp.concatenate(cols, axis=1))
    eye, ones = eye_ref[...], ones_ref[...]
    for k in range(kyl):
        base = k * 2 * wide
        hat_ref[k, 0] = hat[:, base : base + kc]
        slope_hat = hat[:, base + wide : base + wide + kc] * scale
        hat_ref[k, 1] = slope_hat
        each = spread(slope_hat, C, kxl, eye, ones).reshape(2, kz, C, kc)
        w_re, w_im = weights_ref[0, :, k], weights_ref[1, :, k]
        re = w_re * each[0] + w_im * each[1]
        im = w_re * each[1] - w_im * each[0]
        dual = jnp.stack([re, im]).reshape(2, kz, C // SUB, SUB, kc)
        dual = jnp.sum(dual, axis=2).reshape(2 * kz * SUB, kc)
        back = widen(dot(inv_ref[...], dual), wide)
        for g in range(groups):
            send_ref[pl.ds(g * (chunk + part_rows) + k * rows, rows), :] = back[
                g * rows : (g + 1) * rows
            ]
    for g in range(groups):
        send_ref[pl.ds(g * (chunk + part_rows) + chunk, part_rows), :] = part_ref[...]


def grad_kernel(sizes, hat_ref, eye_ref, ones_ref, out_ref):
    C, kxl, kyl, kz = sizes
    kc = kxl * C
    step = pl.program_id(0)
    for k in range(kyl):
        in_re, in_im = hat_ref[k, 0, pl.ds(step, 1), :], hat_ref[k, 0, pl.ds(kz + step, 1), :]
        both = jnp.concatenate(
            [hat_ref[k, 1, pl.ds(step, 1), :], hat_ref[k, 1, pl.ds(kz + step, 1), :]], axis=0
        )
        wide = spread(both, C, kxl, eye_ref[...], ones_ref[...])
        re, im = wide[:C], wide[C:]
        grad_re = re * in_re + im * in_im
        grad_im = im * in_re - re * in_im
        for kx in range(kxl):
            out_ref[0, 0, k, kx] = grad_re[:, kx * C : (kx + 1) * C]
            out_ref[1, 0, k, kx] = grad_im[:, kx * C : (kx + 1) * C]


def pack_kernel(sizes, in_ref, out_ref):
    kxl, kyl = sizes
    for part in range(2):
        for k in range(kyl):
            out_ref[part, 0, k] = jnp.concatenate(
                [in_ref[part, 0, k, kx] for kx in range(kxl)], axis=1
            )


def y_back_kernel(sizes, recv_ref, tab_ref, send_ref):
    C, zl, kxl, ky, kyl, cells, yl, groups, dests, part_rows = sizes
    wide = recv_ref.shape[1]
    rows = 2 * zl
    kr = 2 * kxl
    chunk = kyl * rows + part_rows
    out_chunk = yl * kr + part_rows
    cols = []
    for z in range(zl):
        cols.append(
            jnp.concatenate(
                [
                    recv_ref[pl.ds(s * chunk + r * zl + z, kyl, stride=rows), :]
                    for r in range(2)
                    for s in range(groups)
                ],
                axis=0,
            )
        )
    out = dot(tab_ref[...], jnp.concatenate(cols, axis=1))
    total = recv_ref[pl.ds(kyl * rows, part_rows), :]
    for s in range(1, groups):
        total = total + recv_ref[pl.ds(s * chunk + kyl * rows, part_rows), :]
    for kx in range(kxl):
        for r in range(2):
            block = out[r * cells : (r + 1) * cells]
            piece = jnp.concatenate(
                [block[:, z * wide + kx * C : z * wide + (kx + 1) * C] for z in range(zl)], axis=1
            )
            for d in range(dests):
                send_ref[pl.ds(d * out_chunk + kx * 2 + r, yl, stride=kr), :] = piece[
                    d * yl : (d + 1) * yl
                ]
    for d in range(dests):
        send_ref[pl.ds(d * out_chunk + yl * kr, part_rows), :] = total


def x_back_kernel(sizes, recv_ref, tab_ref, local_ref, out_ref, mix_ref, coef_ref, work_ref):
    C, zl, yl, kxl, sources, part_rows = sizes
    kr = 2 * kxl
    chunk = yl * kr + part_rows
    for y in range(yl):
        column = jnp.concatenate(
            [recv_ref[pl.ds(s * chunk + y * kr, kr), :] for s in range(sources)], axis=0
        )
        value = dot(column.T, tab_ref[...])
        for z in range(zl):
            for half in range(value.shape[1] // LANES):
                work_ref[half, pl.ds(z * yl + y, C, stride=zl * yl), :] = value[
                    z * C : (z + 1) * C, half * LANES : (half + 1) * LANES
                ]
    for half in range(out_ref.shape[1] // LANES):
        cut = pl.ds(half * LANES, LANES)
        out_ref[:, cut] = work_ref[half] + local_ref[:, cut]
    total = recv_ref[pl.ds(yl * kr, part_rows), :]
    for s in range(1, sources):
        total = total + recv_ref[pl.ds(s * chunk + yl * kr, part_rows), :]
    total = total * (1.0 / 1024.0)
    high = C // kxl
    for b in range(kxl):
        mix_ref[pl.ds(b * high, high), :] = total[:high, b * C : (b + 1) * C]
    coef_ref[...] = total[high : high + 5, :C]


def local_kernel(sizes, in_ref, slope_ref, ybefore_ref, yafter_ref, zbefore_ref, zafter_ref,
                 kron_y_ref, kron_z_ref, coef_y_ref, coef_z_ref, sum_y_ref, sum_z_ref, same_y_ref,
                 same_z_ref, out_ref, part_ref):
    C, zl, yl, kxl = sizes
    length = in_ref.shape[1]

    def layer(ref, z):
        return jnp.concatenate(
            [ref[pl.ds((c * zl + z) * yl, yl), :] for c in range(C)], axis=0
        )

    def row_of(layers, y):
        return jnp.concatenate([each.reshape(C, yl, length)[:, y] for each in layers], axis=0)

    def up(values, edge):
        cube = values.reshape(C, yl, length)
        return jnp.concatenate([edge[:, None, :], cube[:, : yl - 1]], axis=1).reshape(
            C * yl, length
        )

    def down(values, edge):
        cube = values.reshape(C, yl, length)
        return jnp.concatenate([cube[:, 1:], edge[:, None, :]], axis=1).reshape(C * yl, length)

    coef = [coef_y_ref[:, j : j + 1] for j in range(5)]
    kron_y = kron_y_ref[...]
    slopes = [layer(slope_ref, z) for z in range(zl)]
    hidden = [dot(kron_y, zbefore_ref[...])]
    hidden += [dot(kron_y, slopes[z]) for z in range(zl)]
    hidden += [dot(kron_y, zafter_ref[...])]
    before = dot(kron_z_ref[...], ybefore_ref[...]).reshape(zl, C, length)
    after = dot(kron_z_ref[...], yafter_ref[...]).reshape(zl, C, length)
    inputs = [layer(in_ref, z) for z in range(zl)]
    nothing = jnp.zeros((C, length), jnp.float32)
    gram = None
    sums = [None] * 5
    for z in range(zl):
        shifted = [
            hidden[z + 1],
            up(hidden[z + 1], before[z]),
            down(hidden[z + 1], after[z]),
            hidden[z],
            hidden[z + 2],
        ]
        total = coef[0] * shifted[0]
        for j in range(1, 5):
            total = total + coef[j] * shifted[j]
        for c in range(C):
            out_ref[pl.ds((c * zl + z) * yl, yl), :] = total[c * yl : (c + 1) * yl]
        for j in range(5):
            term = inputs[z] * shifted[j]
            sums[j] = term if sums[j] is None else sums[j] + term
        stencil = (
            coef[0] * inputs[z]
            + coef[1] * down(inputs[z], nothing)
            + coef[2] * up(inputs[z], nothing)
        )
        if z + 1 < zl:
            stencil = stencil + coef[3] * inputs[z + 1]
        if z > 0:
            stencil = stencil + coef[4] * inputs[z - 1]
        term = dot(slopes[z], stencil, ((1,), (1,)))
        gram = term if gram is None else gram + term
    gram = gram + dot(zbefore_ref[...], coef[3] * inputs[0], ((1,), (1,)))
    gram = gram + dot(zafter_ref[...], coef[4] * inputs[zl - 1], ((1,), (1,)))
    edge = dot(ybefore_ref[...], coef_z_ref[:, 1:2] * row_of(inputs, 0), ((1,), (1,)))
    edge = edge + dot(yafter_ref[...], coef_z_ref[:, 2:3] * row_of(inputs, yl - 1), ((1,), (1,)))
    mix = dot(dot(sum_y_ref[...], gram * same_y_ref[...]), sum_y_ref[...], ((1,), (1,)))
    mix = mix + dot(dot(sum_z_ref[...], edge * same_z_ref[...]), sum_z_ref[...], ((1,), (1,)))
    columns = [jnp.sum(term, axis=1, keepdims=True) for term in sums]
    columns = jnp.concatenate(
        columns + [jnp.zeros((C * yl, SUB - 5), jnp.float32)], axis=1
    )
    eye = (
        lax.broadcasted_iota(jnp.int32, (SUB, SUB), 0)
        == lax.broadcasted_iota(jnp.int32, (SUB, SUB), 1)
    ).astype(jnp.float32)
    by_channel = dot(sum_y_ref[...], columns)
    coefs = dot(eye, by_channel, ((1,), (1,)))
    high = C // kxl
    packed = jnp.concatenate([mix[b * high : (b + 1) * high] for b in range(kxl)], axis=1)
    part_ref[pl.ds(0, high), :] = widen(packed, part_ref.shape[1])
    part_ref[pl.ds(high, SUB), :] = widen(coefs, part_ref.shape[1])


def per_device(input_field, pre_activation, cotangent, spectral_weights, mix_weights, coefficients):
    C, zl, yl, length = input_field.shape
    groups_y = lax.axis_size("gy")
    groups_z = lax.axis_size("gz")
    cells_y, cells_z = yl * groups_y, zl * groups_z
    kz, kyl, kxl = spectral_weights.shape[1:4]
    modes_y, modes_x = kyl * groups_z, kxl * groups_y
    scale = 1.0 / (length * cells_y * cells_z)
    rows = C * zl * yl
    kr = 2 * kxl
    kc = kxl * C
    lanes = zl * C
    wide = max(kc, LANES)
    part_rows = C // kxl + SUB

    tab_x = table_x(length, modes_x)
    tab_y = table_rows(cells_y, modes_y)
    z_rows = order_z(groups_z, zl)
    tab_z = table_rows(cells_z, kz)[:, z_rows]
    inv_z = np.repeat(table_rows(cells_z, kz).T[z_rows], SUB, axis=1)
    inv_y = np.ascontiguousarray(tab_y.T)
    inv_x = np.ascontiguousarray(tab_x.T)
    eye = np.tile(np.eye(C, dtype=np.float32), (1, 2 * kxl))
    ones = np.tile(np.kron(np.eye(kxl), np.ones((C, C))), (2, 1)).astype(jnp.bfloat16)

    flat = lambda values: values.reshape(rows, length)
    exchange = functools.partial(lax.all_to_all, split_axis=0, concat_axis=0, tiled=True)

    slope, send, ylast, yfirst, zlast, zfirst = call(
        functools.partial(x_kernel, (C, zl, yl, groups_y, kr)),
        (
            f32(rows, length),
            f32(groups_y * 2 * yl * kr, lanes),
            f32(C * zl, length),
            f32(C * zl, length),
            f32(C * yl, length),
            f32(C * yl, length),
        ),
        (flat(input_field), flat(pre_activation), flat(cotangent), jnp.asarray(wide_columns(tab_x))),
        24,
        flops=4 * rows * length * 2 * modes_x,
        bytes_accessed=6 * rows * length * 4,
        scratch=[
            pltpu.VMEM((2, rows, wide_columns(tab_x).shape[1]), jnp.float32),
            pltpu.VMEM((rows, LANES), jnp.float32),
        ],
    )
    lines = exchange(send, "gy")

    def from_below(values, axis):
        return lax.ppermute(values, axis, [(i, i + 1) for i in range(lax.axis_size(axis) - 1)])

    def from_above(values, axis):
        return lax.ppermute(values, axis, [(i + 1, i) for i in range(lax.axis_size(axis) - 1)])

    ybefore, yafter = from_below(ylast, "gy"), from_above(yfirst, "gy")
    zbefore, zafter = from_below(zlast, "gz"), from_above(zfirst, "gz")

    weights = call(
        functools.partial(pack_kernel, (kxl, kyl)),
        f32(2, kz, kyl, C, kc),
        (spectral_weights,),
        16,
        flops=2 * kz * kyl * C * kc,
        bytes_accessed=2 * kz * kyl * kxl * C * 128 * 4 * 2,
        grid=(kz,),
        in_specs=[pl.BlockSpec((2, 1, kyl, kxl, C, C), lambda i: (0, i, 0, 0, 0, 0))],
        out_specs=pl.BlockSpec((2, 1, kyl, C, kc), lambda i: (0, i, 0, 0, 0)),
    )

    send = call(
        functools.partial(y_kernel, (C, zl, kxl, modes_y, kyl, yl, groups_y)),
        f32(groups_z * 2 * kyl * 2 * zl, wide),
        (lines, jnp.asarray(tab_y)),
        16,
        flops=16 * modes_y * cells_y * kxl * lanes,
        bytes_accessed=4 * MIB,
    )
    owned = exchange(send, "gz")

    coef_rows = jnp.pad(coefficients.T, ((0, 0), (0, SUB - 5)))
    mixed = mix_weights.T
    local, part = call(
        functools.partial(local_kernel, (C, zl, yl, kxl)),
        (f32(rows, length), f32(part_rows, wide)),
        (
            flat(input_field),
            slope,
            ybefore,
            yafter,
            zbefore,
            zafter,
            jnp.kron(mixed, jnp.eye(yl, dtype=jnp.float32)),
            jnp.kron(jnp.eye(zl, dtype=jnp.float32), mixed),
            jnp.repeat(coef_rows, yl, axis=0),
            jnp.tile(coef_rows, (zl, 1)),
            jnp.asarray(np.repeat(np.eye(C, dtype=np.float32), yl, axis=1)),
            jnp.asarray(np.tile(np.eye(C, dtype=np.float32), (1, zl))),
            jnp.asarray(np.tile(np.eye(yl, dtype=np.float32), (C, C))),
            jnp.asarray(np.kron(np.eye(zl, dtype=np.float32), np.ones((C, C), np.float32))),
        ),
        32,
        flops=2 * 12 * (C * yl) ** 2 * length,
        bytes_accessed=6 * MIB,
    )

    chunk = kyl * 2 * zl + part_rows
    send, hats = call(
        functools.partial(z_kernel, (C, zl, kxl, kyl, kz, groups_z, part_rows, scale)),
        (f32(groups_z * chunk, wide), f32(kyl, 2, 2 * kz, kc)),
        (
            owned,
            jnp.asarray(tab_z),
            jnp.asarray(inv_z),
            jnp.asarray(eye),
            jnp.asarray(ones),
            weights,
            part,
        ),
        32,
        flops=16 * kz * kyl * C * kc,
        bytes_accessed=6 * MIB,
    )
    returned = exchange(send, "gz")

    grad_spectral = call(
        functools.partial(grad_kernel, (C, kxl, kyl, kz)),
        f32(2, kz, kyl, kxl, C, C),
        (hats, jnp.asarray(eye), jnp.asarray(ones)),
        16,
        flops=16 * kz * kyl * C * kc,
        bytes_accessed=2 * kz * kyl * kxl * C * 128 * 4,
        grid=(kz,),
        in_specs=[
            pl.BlockSpec((kyl, 2, 2 * kz, kc), lambda i: (0, 0, 0, 0)),
            pl.BlockSpec((C, 2 * kc), lambda i: (0, 0)),
            pl.BlockSpec((2 * kc, kc), lambda i: (0, 0)),
        ],
        out_specs=pl.BlockSpec((2, 1, kyl, kxl, C, C), lambda i: (0, i, 0, 0, 0, 0)),
    )

    send = call(
        functools.partial(
            y_back_kernel,
            (C, zl, kxl, modes_y, kyl, cells_y, yl, groups_z, groups_y, part_rows),
        ),
        f32(groups_y * (yl * kr + part_rows), lanes),
        (returned, jnp.asarray(inv_y)),
        16,
        flops=8 * modes_y * cells_y * kxl * lanes,
        bytes_accessed=2 * MIB,
    )
    arrived = exchange(send, "gy")

    grad_input, grad_mix, grad_coef = call(
        functools.partial(x_back_kernel, (C, zl, yl, kxl, groups_y, part_rows)),
        (f32(rows, length), f32(C, C), f32(5, C)),
        (arrived, jnp.asarray(inv_x), local),
        16,
        flops=2 * rows * length * 2 * modes_x,
        bytes_accessed=3 * MIB,
        scratch=[pltpu.VMEM((length // LANES, rows, LANES), jnp.float32)],
    )
    return (grad_input.reshape(input_field.shape), grad_spectral, grad_mix, grad_coef)


def solution(mesh):
    in_specs = (
        P(None, "gz", "gy", None),
        P(None, "gz", "gy", None),
        P(None, "gz", "gy", None),
        P(None, None, "gz", "gy", None, None),
        P(),
        P(),
    )
    out_specs = (P(None, "gz", "gy", None), P(None, None, "gz", "gy", None, None), P(), P())
    return jax.shard_map(
        per_device, mesh=mesh, in_specs=in_specs, out_specs=out_specs, check_vma=False
    )
```

profile of v0, /device:TPU:0, one launch (start us, length us, event | category | flops | bytes accessed | tf_op | source)
XLA Modules:
  0.0 108.2 jit_solution(17295621008120104009)
XLA Ops:
  0.6 1.2 %copy-done.3 = f32[32,4,8,256]{3,2,1,0:T(8,128)S(1)} copy-done((f32[32,4,8,256]{3,2,1,0:T(8,128)S(1)}, f32[32,4,8,256]{3,2,1,0:T(8,128)}, u32[]{:S(2)}) %copy-start.3) | copy-done | bytes 1048600
  1.9 1.2 %copy-done.5 = f32[32,4,8,256]{3,2,1,0:T(8,128)S(1)} copy-done((f32[32,4,8,256]{3,2,1,0:T(8,128)S(1)}, f32[32,4,8,256]{3,2,1,0:T(8,128)}, u32[]{:S(2)}) %copy-start.5) | copy-done | bytes 1048600
  3.1 1.2 %copy-done.6 = f32[32,4,8,256]{3,2,1,0:T(8,128)S(1)} copy-done((f32[32,4,8,256]{3,2,1,0:T(8,128)S(1)}, f32[32,4,8,256]{3,2,1,0:T(8,128)}, u32[]{:S(2)}) %copy-start.6) | copy-done | bytes 1048600
  4.3 0.9 copy-done.16
  5.2 2.9 %shard_map.201 = (f32[1024,256]{1,0:T(8,128)S(1)}, f32[1024,128]{1,0:T(8,128)}, f32[128,256]{1,0:T(8,128)}, f32[128,256]{1,0:T(8,128)}, f32[256,256]{1,0:T(8,128)}, /*index=5*/f32[256,256]{1,0:T(8,128)}) custom-call(f32[1024,256]{1,0:T(8,128)S(1)} %bitcast.19, f32[1024,256]{1,0:T(8,128)S(1)} %bitcast.23, f32[1024,256]{1,0:T(8,128)S(1)} %bitcast.24, ...), custom_call_target="tpu_custom_call" | custom-call | flops 67108864 | bytes 6291456 | tf_op jit(solution)/shard_map/pallas_call | solution.py:25
  8.2 7.3 %all-to-all-start = ((f32[8,128,128]{2,1,0:T(8,128)}), f32[8,128,128]{2,1,0:T(8,128)S(1)}, u32[]{:S(2)}, u32[]{:S(2)}) async-start(f32[8,128,128]{2,1,0:T(8,128)} %bitcast.3), calls=%async_computation | async-start | bytes 1048576 | tf_op jit(solution)/shard_map/all_to_all | solution.py:416
  15.4 3.9 %collective-permute-start = (f32[128,256]{1,0:T(8,128)}, f32[128,256]{1,0:T(8,128)S(1)}, u32[]{:S(2)}, u32[]{:S(2)}) collective-permute-start(f32[128,256]{1,0:T(8,128)} %get-tuple-element.19), channel_id=1, source_target_pairs={{0,1},{1,2},{2,3},{3,4},{4,5},{5,6},{6,7},{8,9},{9,10},{10,11},{11... | collective-permute-start | bytes 393224 | tf_op jit(solution)/shard_map/ppermute | solution.py:419
  19.4 1.3 %collective-permute-start.1 = (f32[128,256]{1,0:T(8,128)}, f32[128,256]{1,0:T(8,128)S(1)}, u32[]{:S(2)}, u32[]{:S(2)}) collective-permute-start(f32[128,256]{1,0:T(8,128)} %get-tuple-element.20), channel_id=1, source_target_pairs={{1,0},{2,1},{3,2},{4,3},{5,4},{6,5},{7,6},{9,8},{10,9},{11,10},{12... | collective-permute-start | bytes 393224 | tf_op jit(solution)/shard_map/ppermute | solution.py:422
  20.7 1.3 %collective-permute-start.2 = (f32[256,256]{1,0:T(8,128)}, f32[256,256]{1,0:T(8,128)S(1)}, u32[]{:S(2)}, u32[]{:S(2)}) collective-permute-start(f32[256,256]{1,0:T(8,128)} %get-tuple-element.21), channel_id=1, source_target_pairs={{0,8},{8,16},{16,24},{1,9},{9,17},{17,25},{2,10},{10,18},{18,26},{... | collective-permute-start | bytes 786440 | tf_op jit(solution)/shard_map/ppermute | solution.py:419
  22.0 1.3 %collective-permute-start.3 = (f32[256,256]{1,0:T(8,128)}, f32[256,256]{1,0:T(8,128)S(1)}, u32[]{:S(2)}, u32[]{:S(2)}) collective-permute-start(f32[256,256]{1,0:T(8,128)} %get-tuple-element.22), channel_id=1, source_target_pairs={{8,0},{16,8},{24,16},{9,1},{17,9},{25,17},{10,2},{18,10},{26,18},{... | collective-permute-start | bytes 786440 | tf_op jit(solution)/shard_map/ppermute | solution.py:422
  23.4 2.6 %broadcast_multiply_fusion = f32[32,8,32,8]{3,2,1,0:T(8,128)} fusion(f32[8,8]{1,0:T(8,128)S(1)} %fusion, f32[32,32]{1,0:T(8,128)S(1)} %copy.26), kind=kLoop, calls=%fused_computation | loop fusion | flops 65536 | bytes 266496 | tf_op jit(solution)/shard_map/jit(kron)/mul | solution.py:461
  26.3 4.7 %mul.51.kron_y_ref = f32[256,256]{1,0:T(8,128)} reshape(f32[32,8,32,8]{3,2,1,0:T(8,128)} %broadcast_multiply_fusion) | data formatting | bytes 524288 | tf_op jit(solution)/shard_map/jit(kron)/mul | solution.py:461
  31.0 0.6 pad.4.clone
  31.6 5.8 %copy-done = f32[2,16,8,4,32,32]{5,4,3,2,1,0:T(8,128)S(1)} copy-done((f32[2,16,8,4,32,32]{5,4,3,2,1,0:T(8,128)S(1)}, f32[2,16,8,4,32,32]{5,4,3,2,1,0:T(8,128)}, u32[]{:S(2)}) %copy-start) | copy-done | bytes 4194328
  37.4 5.6 %shard_map.203.weights_ref = f32[2,16,8,32,128]{4,3,2,1,0:T(8,128)S(1)} custom-call(f32[2,16,8,4,32,32]{5,4,3,2,1,0:T(8,128)S(1)} %copy-done), custom_call_target="tpu_custom_call" | custom-call | flops 1048576 | bytes 33554432 | tf_op jit(solution)/shard_map/pallas_call | solution.py:25
  43.1 2.0 %copy-done.1 = f32[2,16,8,32,128]{4,3,2,1,0:T(8,128)} copy-done((f32[2,16,8,32,128]{4,3,2,1,0:T(8,128)}, f32[2,16,8,32,128]{4,3,2,1,0:T(8,128)S(1)}, u32[]{:S(2)}) %copy-start.1) | copy-done | bytes 4194328
  45.1 0.8 copy-done.25
  45.9 1.2 %shard_map.202 = f32[512,128]{1,0:T(8,128)} custom-call(f32[1024,128]{1,0:T(8,128)S(1)} %bitcast.21, f32[64,128]{1,0:T(8,128)S(1)} %copy-done.25), custom_call_target="tpu_custom_call" | custom-call | flops 16777216 | bytes 4194304 | tf_op jit(solution)/shard_map/pallas_call | solution.py:25
  47.1 5.8 %all-to-all-start.1 = ((f32[4,128,128]{2,1,0:T(8,128)}), f32[4,128,128]{2,1,0:T(8,128)S(1)}, u32[]{:S(2)}, u32[]{:S(2)}) async-start(f32[4,128,128]{2,1,0:T(8,128)} %bitcast.5), calls=%async_computation.1 | async-start | bytes 524288 | tf_op jit(solution)/shard_map/all_to_all | solution.py:447
  52.8 0.7 broadcast_bitcast_fusion.coef_y_ref
  53.6 0.6 copy-done.17
  54.2 0.7 copy-done.19
  54.9 0.7 copy-done.10
  55.6 0.7 copy-done.12
  56.3 0.7 tile.4
  57.1 0.9 copy-done.7
  58.0 0.9 copy-done.9
  59.0 0.9 copy-done.11
  59.9 0.9 copy-done.13
  60.9 0.9 copy-done.18
  61.8 0.9 copy-done.20
  62.7 0.8 copy-done.23
  63.5 0.8 copy-done.26
  64.3 0.7 copy-done.28
  65.0 3.3 %shard_map.204 = (f32[1024,256]{1,0:T(8,128)S(1)}, f32[16,128]{1,0:T(8,128)S(1)}) custom-call(f32[1024,256]{1,0:T(8,128)S(1)} %bitcast.20, f32[1024,256]{1,0:T(8,128)S(1)} %get-tuple-element.18.slope_ref, f32[128,256]{1,0:T(8,128)S(1)} %copy-done.18, f32[128,256]{1,0:T(8,128)S(1)} %copy-done.20, f32[256,256]{1,0:T(8,128)S(1)} %copy-done.11, ...), custom_call_target="tpu_custom_call" | custom-call | flops 402653184 | bytes 6291456 | tf_op jit(solution)/shard_map/pallas_call | solution.py:25
  68.3 0.6 copy-done.29
  68.9 2.2 %copy-done.2 = f32[2,16,8,32,128]{4,3,2,1,0:T(8,128)S(1)} copy-done((f32[2,16,8,32,128]{4,3,2,1,0:T(8,128)S(1)}, f32[2,16,8,32,128]{4,3,2,1,0:T(8,128)}, u32[]{:S(2)}) %copy-start.2) | copy-done | bytes 4194328
  71.1 0.8 copy-done.14
  71.9 0.8 copy-done.24
  72.6 0.7 copy-done.30
  73.3 3.3 %shard_map.205 = (f32[320,128]{1,0:T(8,128)S(1)}, f32[8,2,32,128]{3,2,1,0:T(8,128)S(1)}) custom-call(f32[512,128]{1,0:T(8,128)S(1)} %bitcast.25, f32[32,32]{1,0:T(8,128)S(1)} %copy-done.27, f32[32,256]{1,0:T(8,128)S(1)} %copy-done.24, f32[32,256]{1,0:T(8,128)S(1)} %copy-done.14, bf16[256,128]{1,0:T(8,128)(2,1)S(1)} %copy-done.8, ...), custom_call_target="tpu_custom_call" | custom-call | flops 8388608 | bytes 6291456 | tf_op jit(solution)/shard_map/pallas_call | solution.py:25
  76.7 8.2 %all_to_all.44 = f32[4,80,128]{2,1,0:T(8,128)S(1)} all-to-all(f32[4,80,128]{2,1,0:T(8,128)S(1)} %bitcast.28), channel_id=1, replica_groups=mesh['gz'=4,'gy'=8] {'gz'}, dimensions={0} | all-to-all | bytes 327680 | tf_op jit(solution)/shard_map/all_to_all | solution.py:492
  84.9 0.8 copy-done.22
  85.7 1.2 %shard_map.206 = f32[640,128]{1,0:T(8,128)} custom-call(f32[320,128]{1,0:T(8,128)S(1)} %bitcast.26, f32[128,64]{1,0:T(8,128)S(1)} %copy-done.22), custom_call_target="tpu_custom_call" | custom-call | flops 8388608 | bytes 2097152 | tf_op jit(solution)/shard_map/pallas_call | solution.py:25
  86.9 6.6 %all-to-all-start.3 = ((f32[8,80,128]{2,1,0:T(8,128)}), f32[8,80,128]{2,1,0:T(8,128)S(1)}, u32[]{:S(2)}, u32[]{:S(2)}) async-start(f32[8,80,128]{2,1,0:T(8,128)} %bitcast.13), calls=%async_computation.3 | async-start | bytes 655360 | tf_op jit(solution)/shard_map/all_to_all | solution.py:521
  93.6 0.8 copy-done.15
  94.3 11.7 %shard_map.208 = f32[2,16,8,4,32,32]{5,4,3,2,1,0:T(8,128)} custom-call(f32[8,2,32,128]{3,2,1,0:T(8,128)S(1)} %get-tuple-element.27.hat_ref, f32[32,256]{1,0:T(8,128)S(1)} %copy-done.15, bf16[256,128]{1,0:T(8,128)(2,1)S(1)} %copy-done.8), custom_call_target="tpu_custom_call" | custom-call | flops 8388608 | bytes 16777216 | tf_op jit(solution)/shard_map/pallas_call | solution.py:25
  106.0 2.2 %shard_map.207 = (f32[1024,256]{1,0:T(8,128)}, f32[32,32]{1,0:T(8,128)}, f32[5,32]{1,0:T(8,128)}) custom-call(f32[640,128]{1,0:T(8,128)S(1)} %bitcast.22, f32[64,256]{1,0:T(8,128)S(1)} %copy-done.21, f32[1024,256]{1,0:T(8,128)S(1)} %get-tuple-element.25.local_ref), custom_call_target="tpu_custom_call" | custom-call | flops 33554432 | bytes 3145728 | tf_op jit(solution)/shard_map/pallas_call | solution.py:25
  (52 shorter events, 0.5 us)
Async XLA Ops:
  0.6 1.2 %copy-start.3 = (f32[32,4,8,256]{3,2,1,0:T(8,128)S(1)}, f32[32,4,8,256]{3,2,1,0:T(8,128)}, u32[]{:S(2)}) copy-start(f32[32,4,8,256]{3,2,1,0:T(8,128)} %param.18) | copy-start | bytes 3145732
  1.9 1.2 %copy-start.5 = (f32[32,4,8,256]{3,2,1,0:T(8,128)S(1)}, f32[32,4,8,256]{3,2,1,0:T(8,128)}, u32[]{:S(2)}) copy-start(f32[32,4,8,256]{3,2,1,0:T(8,128)} %param.19) | copy-start | bytes 3145732
  3.1 1.2 %copy-start.6 = (f32[32,4,8,256]{3,2,1,0:T(8,128)S(1)}, f32[32,4,8,256]{3,2,1,0:T(8,128)}, u32[]{:S(2)}) copy-start(f32[32,4,8,256]{3,2,1,0:T(8,128)} %param.20) | copy-start | bytes 3145732
  4.3 0.9 copy-start.16
  5.2 18.1 %copy-start.31 = (f32[32,32]{1,0:T(8,128)S(1)}, f32[32,32]{1,0:T(8,128)}, u32[]{:S(2)}) copy-start(f32[32,32]{1,0:T(8,128)} %param.22) | copy-start | bytes 12292
  5.2 20.9 %copy-start.32 = (f32[5,32]{1,0:T(8,128)S(1)}, f32[5,32]{1,0:T(8,128)}, u32[]{:S(2)}) copy-start(f32[5,32]{1,0:T(8,128)} %param.23) | copy-start | bytes 1924
  8.2 36.9 %all-to-all-start = ((f32[8,128,128]{2,1,0:T(8,128)}), f32[8,128,128]{2,1,0:T(8,128)S(1)}, u32[]{:S(2)}, u32[]{:S(2)}) async-start(f32[8,128,128]{2,1,0:T(8,128)} %bitcast.3), calls=%async_computation | async-start | bytes 1048576 | tf_op jit(solution)/shard_map/all_to_all | solution.py:416
  15.4 38.1 %collective-permute-start = (f32[128,256]{1,0:T(8,128)}, f32[128,256]{1,0:T(8,128)S(1)}, u32[]{:S(2)}, u32[]{:S(2)}) collective-permute-start(f32[128,256]{1,0:T(8,128)} %get-tuple-element.19), channel_id=1, source_target_pairs={{0,1},{1,2},{2,3},{3,4},{4,5},{5,6},{6,7},{8,9},{9,10},{10,11},{11... | collective-permute-start | bytes 393224 | tf_op jit(solution)/shard_map/ppermute | solution.py:419
  19.4 34.9 %collective-permute-start.1 = (f32[128,256]{1,0:T(8,128)}, f32[128,256]{1,0:T(8,128)S(1)}, u32[]{:S(2)}, u32[]{:S(2)}) collective-permute-start(f32[128,256]{1,0:T(8,128)} %get-tuple-element.20), channel_id=1, source_target_pairs={{1,0},{2,1},{3,2},{4,3},{5,4},{6,5},{7,6},{9,8},{10,9},{11,10},{12... | collective-permute-start | bytes 393224 | tf_op jit(solution)/shard_map/ppermute | solution.py:422
  20.7 34.2 %collective-permute-start.2 = (f32[256,256]{1,0:T(8,128)}, f32[256,256]{1,0:T(8,128)S(1)}, u32[]{:S(2)}, u32[]{:S(2)}) collective-permute-start(f32[256,256]{1,0:T(8,128)} %get-tuple-element.21), channel_id=1, source_target_pairs={{0,8},{8,16},{16,24},{1,9},{9,17},{17,25},{2,10},{10,18},{18,26},{... | collective-permute-start | bytes 786440 | tf_op jit(solution)/shard_map/ppermute | solution.py:419
  22.0 33.6 %collective-permute-start.3 = (f32[256,256]{1,0:T(8,128)}, f32[256,256]{1,0:T(8,128)S(1)}, u32[]{:S(2)}, u32[]{:S(2)}) collective-permute-start(f32[256,256]{1,0:T(8,128)} %get-tuple-element.22), channel_id=1, source_target_pairs={{8,0},{16,8},{24,16},{9,1},{17,9},{25,17},{10,2},{18,10},{26,18},{... | collective-permute-start | bytes 786440 | tf_op jit(solution)/shard_map/ppermute | solution.py:422
  31.6 5.8 %copy-start = (f32[2,16,8,4,32,32]{5,4,3,2,1,0:T(8,128)S(1)}, f32[2,16,8,4,32,32]{5,4,3,2,1,0:T(8,128)}, u32[]{:S(2)}) copy-start(f32[2,16,8,4,32,32]{5,4,3,2,1,0:T(8,128)} %in_ref.1) | copy-start | bytes 12582916
  37.4 19.6 %copy-start.4 = (f32[32,4,8,256]{3,2,1,0:T(8,128)S(1)}, f32[32,4,8,256]{3,2,1,0:T(8,128)}, u32[]{:S(2)}) copy-start(f32[32,4,8,256]{3,2,1,0:T(8,128)} %param.18) | copy-start | bytes 3145732
  37.4 31.5 %copy-start.27 = (f32[32,32]{1,0:T(8,128)S(1)}, f32[32,32]{1,0:T(8,128)}, u32[]{:S(2)}) copy-start(f32[32,32]{1,0:T(8,128)} %constant.33.clone.tab_ref) | copy-start | bytes 12292
  43.1 2.0 %copy-start.1 = (f32[2,16,8,32,128]{4,3,2,1,0:T(8,128)}, f32[2,16,8,32,128]{4,3,2,1,0:T(8,128)S(1)}, u32[]{:S(2)}) copy-start(f32[2,16,8,32,128]{4,3,2,1,0:T(8,128)S(1)} %shard_map.203.weights_ref) | copy-start | bytes 12582916
  45.1 23.8 %copy-start.8 = (bf16[256,128]{1,0:T(8,128)(2,1)S(1)}, bf16[256,128]{1,0:T(8,128)(2,1)}, u32[]{:S(2)}) copy-start(bf16[256,128]{1,0:T(8,128)(2,1)} %constant.36.clone.ones_ref) | copy-start | bytes 196612
  45.1 0.8 copy-start.25
  47.1 21.8 %all-to-all-start.1 = ((f32[4,128,128]{2,1,0:T(8,128)}), f32[4,128,128]{2,1,0:T(8,128)S(1)}, u32[]{:S(2)}, u32[]{:S(2)}) async-start(f32[4,128,128]{2,1,0:T(8,128)} %bitcast.5), calls=%async_computation.1 | async-start | bytes 524288 | tf_op jit(solution)/shard_map/all_to_all | solution.py:447
  53.6 0.7 copy-start.17
  54.2 0.7 copy-start.19
  54.9 0.7 copy-start.10
  55.6 0.7 copy-start.12
  57.0 1.0 copy-start.7
  58.0 0.9 copy-start.9
  58.9 0.9 copy-start.11
  59.9 0.9 copy-start.13
  60.8 0.9 copy-start.18
  61.8 0.9 copy-start.20
  62.7 0.8 copy-start.23
  63.5 0.8 copy-start.26
  64.3 0.7 copy-start.28
  68.3 0.6 copy-start.29
  68.9 2.2 %copy-start.2 = (f32[2,16,8,32,128]{4,3,2,1,0:T(8,128)S(1)}, f32[2,16,8,32,128]{4,3,2,1,0:T(8,128)}, u32[]{:S(2)}) copy-start(f32[2,16,8,32,128]{4,3,2,1,0:T(8,128)} %copy-done.1) | copy-start | bytes 12582916
  71.1 0.8 copy-start.14
  71.9 0.8 copy-start.24
  72.6 0.7 copy-start.30
  84.9 0.8 copy-start.22
  86.9 19.0 %all-to-all-start.3 = ((f32[8,80,128]{2,1,0:T(8,128)}), f32[8,80,128]{2,1,0:T(8,128)S(1)}, u32[]{:S(2)}, u32[]{:S(2)}) async-start(f32[8,80,128]{2,1,0:T(8,128)} %bitcast.13), calls=%async_computation.3 | async-start | bytes 655360 | tf_op jit(solution)/shard_map/all_to_all | solution.py:521
  93.6 0.8 copy-start.15
  94.3 11.7 %copy-start.21 = (f32[64,256]{1,0:T(8,128)S(1)}, f32[64,256]{1,0:T(8,128)}, u32[]{:S(2)}) copy-start(f32[64,256]{1,0:T(8,128)} %constant.38.clone.tab_ref) | copy-start | bytes 196612
where the time goes:
time: 110 us; the launch traced here: 108 us
  local copies, waits for them, and re-layouts  37.5 us (34%)
  Pallas kernels  31.5 us (29%)
  starting transfers between devices  27.4 us (25%)
  blocking collectives  8.19 us (7%)
  other arithmetic  2.73 us (2%)
    pallas_call x8, Pallas kernels, call(): pl.pallas_call(body, out_shape=outs, scratch_shapes=list(scratch), compil...  31.5 us
    unnamed x67, local copies, waits for them, and re-layouts  30.5 us
    all_to_all x1, blocking collectives, per_device(): returned = exchange(send, 'gz')  8.19 us
    all_to_all x1, starting transfers between devices, per_device(): lines = exchange(send, 'gy')  7.25 us
    all_to_all x1, starting transfers between devices, per_device(): arrived = exchange(send, 'gy')  6.63 us
    all_to_all x1, starting transfers between devices, per_device(): owned = exchange(send, 'gz')  5.75 us
    ppermute x2, starting transfers between devices, from_below(): lax.ppermute(values, axis, [(i, i + 1) for i in range(lax.axis_size(axis)...  5.23 us
    mul x1, local copies, waits for them, and re-layouts, per_device(): jnp.kron(mixed, jnp.eye(yl, dtype=jnp.float32))  4.68 us
  transfers between devices with their start and end apart: 7, of which 0 were waited for; matrix products, arithmetic and copies ran while one was open for 9% of the time, Pallas kernels for 20%

commit v1 on v0

v1 whole, which is shorter than its diff:
```python
import functools
import math

import jax
import jax.numpy as jnp
import numpy as np
from jax import lax
from jax.experimental import pallas as pl
from jax.experimental.pallas import tpu as pltpu
from jax.sharding import PartitionSpec as P

PRECISION = lax.Precision.HIGH
MIB = 1 << 20
SUB = 8
LANES = 128


def dot(left, right, dims=((1,), (0,)), precision=PRECISION):
    return lax.dot_general(
        left, right, (dims, ((), ())), precision=precision, preferred_element_type=jnp.float32
    )


def call(body, outs, operands, limit_mib, flops, bytes_accessed, scratch=(), **grid):
    return pl.pallas_call(
        body,
        out_shape=outs,
        scratch_shapes=list(scratch),
        compiler_params=pltpu.CompilerParams(vmem_limit_bytes=limit_mib * MIB),
        cost_estimate=pl.CostEstimate(
            flops=flops, bytes_accessed=bytes_accessed, transcendentals=0
        ),
        **grid,
    )(*operands)


def f32(*shape):
    return jax.ShapeDtypeStruct(shape, jnp.float32)


def vmem(*shape):
    return pltpu.VMEM(shape, jnp.float32)


def far_out(*shape):
    return pltpu.HBM(shape, jnp.float32)


def hbm(values):
    return pltpu.with_memory_space_constraint(values, pltpu.HBM)


def held(values):
    return pltpu.with_memory_space_constraint(values, pltpu.VMEM)


def iota(shape, axis):
    return lax.broadcasted_iota(jnp.int32, shape, axis)


SERIES = [(-1.0) ** n * (2.0 * math.pi) ** (2 * n) / math.factorial(2 * n) for n in range(10)]


def cos_turns(turns):
    part = turns - jnp.floor(turns + 0.5)
    size = jnp.abs(part)
    flip = size > 0.25
    part = jnp.where(flip, 0.5 - size, size)
    square = part * part
    total = jnp.full_like(square, SERIES[-1])
    for factor in SERIES[-2::-1]:
        total = total * square + factor
    return jnp.where(flip, -total, total)


def mode_of(position, modes):
    return jnp.where(position < modes // 2, position, position - modes)


def turns_of(cell, mode, cells, quarter):
    return (cell * mode).astype(jnp.float32) * (1.0 / cells) - 0.25 * quarter.astype(jnp.float32)


def split(index, size):
    high = index // size
    return high, index - high * size


def table_x(cells, modes, mode_axis, columns=None):
    shape = [cells, cells]
    shape[mode_axis] = columns or 2 * modes
    mode, part = split(iota(tuple(shape), mode_axis), 2)
    value = cos_turns(turns_of(iota(tuple(shape), 1 - mode_axis), mode_of(mode, modes), cells, part))
    value = jnp.where(part == 1, -value, value)
    return jnp.where(mode < modes, value, 0.0)


def pair_table(mode, mode_part, cell, cell_part, modes, cells):
    value = cos_turns(turns_of(cell, mode_of(mode, modes), cells, mode_part ^ cell_part))
    return jnp.where((mode_part == 1) & (cell_part == 0), -value, value)


def table_y(cells, modes, mode_axis):
    shape = [2 * cells, 2 * cells]
    shape[mode_axis] = 2 * modes
    mode_part, mode = split(iota(tuple(shape), mode_axis), modes)
    cell_part, cell = split(iota(tuple(shape), 1 - mode_axis), cells)
    return pair_table(mode, mode_part, cell, cell_part, modes, cells)


def table_z(cells, modes, mode_axis, groups, times=1):
    shape = [2 * cells, 2 * cells]
    shape[mode_axis] = 2 * modes * times
    mode_part, mode = split(iota(tuple(shape), mode_axis) // times, modes)
    depth = cells // groups
    group, rest = split(iota(tuple(shape), 1 - mode_axis), 2 * depth)
    cell_part, cell = split(rest, depth)
    return pair_table(mode, mode_part, cell + group * depth, cell_part, modes, cells)


def gelu_slope(values):
    normal_cdf = 0.5 * (1.0 + lax.erf(values * 0.7071067811865476))
    return normal_cdf + values * jnp.exp(-0.5 * values * values) * 0.3989422804014327


def fetch(sources, targets, sems):
    copies = [
        pltpu.make_async_copy(source, target, sems.at[i])
        for i, (source, target) in enumerate(zip(sources, targets))
    ]
    for copy in copies:
        copy.start()
    return copies


def x_kernel(sizes, in_hbm, pre_hbm, cot_hbm, slope_ref, send_ref, ylast_ref, yfirst_ref,
             zlast_ref, zfirst_ref, in_ref, pre_ref, cot_ref, work_ref, half_ref, sems):
    C, zl, yl, dests, kr = sizes
    copies = fetch((in_hbm, pre_hbm, cot_hbm), (in_ref, pre_ref, cot_ref), sems)
    table = table_x(in_ref.shape[1], dests * kr // 2, 1, work_ref.shape[2])

    def transform(f, field):
        work_ref[f] = dot(field, table)
        for y in range(yl):
            rows = [work_ref[f, pl.ds(z * yl + y, C, stride=zl * yl), :] for z in range(zl)]
            turned = jnp.concatenate(rows, axis=0).T
            for d in range(dests):
                send_ref[pl.ds(((d * 2 + f) * yl + y) * kr, kr), :] = turned[d * kr : (d + 1) * kr]

    copies[0].wait()
    transform(0, in_ref[...])
    copies[1].wait()
    copies[2].wait()
    slope = cot_ref[...] * gelu_slope(pre_ref[...])
    slope_ref[...] = slope
    transform(1, slope)
    for half in range(slope_ref.shape[1] // LANES):
        cut = pl.ds(half * LANES, LANES)
        half_ref[...] = slope[:, half * LANES : (half + 1) * LANES]
        for z in range(zl):
            to = pl.ds(z * C, C)
            ylast_ref[to, cut] = half_ref[pl.ds(z * yl + yl - 1, C, stride=zl * yl), :]
            yfirst_ref[to, cut] = half_ref[pl.ds(z * yl, C, stride=zl * yl), :]
    for c in range(C):
        zlast_ref[pl.ds(c * yl, yl), :] = slope_ref[pl.ds((c * zl + zl - 1) * yl, yl), :]
        zfirst_ref[pl.ds(c * yl, yl), :] = slope_ref[pl.ds(c * zl * yl, yl), :]


def widen(values, lanes):
    spare = lanes - values.shape[1]
    if spare == 0:
        return values
    return jnp.concatenate([values, jnp.zeros((values.shape[0], spare), jnp.float32)], axis=1)


def y_kernel(sizes, recv_ref, *refs):
    send_ref = refs[-1]
    C, zl, kxl, ky, kyl, yl, sources = sizes
    kr = 2 * kxl
    lanes = zl * C
    pieces = []
    for kx in range(kxl):
        for f in range(2):
            pieces.append(
                jnp.concatenate(
                    [
                        recv_ref[pl.ds((s * 2 + f) * yl * kr + kx * 2 + r, yl, stride=kr), :]
                        for r in range(2)
                        for s in range(sources)
                    ],
                    axis=0,
                )
            )
    out = dot(table_y(yl * sources, ky, 0), jnp.concatenate(pieces, axis=1))
    for f in range(2):
        for r in range(2):
            for z in range(zl):
                parts = []
                for kx in range(kxl):
                    base = (kx * 2 + f) * lanes + z * C
                    parts.append(out[r * ky : (r + 1) * ky, base : base + C])
                block = widen(jnp.concatenate(parts, axis=1), send_ref.shape[1])
                for g in range(ky // kyl):
                    start = (g * 2 + f) * kyl * 2 * zl + r * zl + z
                    send_ref[pl.ds(start, kyl, stride=2 * zl), :] = block[g * kyl : (g + 1) * kyl]


def spread(rows, C):
    n, kc = rows.shape
    high = rows.astype(jnp.bfloat16).astype(jnp.float32)
    both = jnp.concatenate([high, rows - high], axis=1)
    own = jnp.remainder(iota((C, 2 * kc), 1), C) == iota((C, 2 * kc), 0)
    wide = jnp.where(own[None], jnp.broadcast_to(both[:, None, :], (n, C, 2 * kc)), 0.0)
    wide = wide.reshape(n * C, 2 * kc).astype(jnp.bfloat16)
    same = jnp.remainder(iota((2 * kc, kc), 0), kc) // C == iota((2 * kc, kc), 1) // C
    return dot(wide, same.astype(jnp.bfloat16), precision=None)


def z_kernel(sizes, recv_ref, weights_hbm, part_hbm, send_ref, hat_ref, weights_ref, part_ref,
             sems):
    C, zl, kxl, kyl, kz, groups, part_rows, scale = sizes
    copies = fetch(
        [weights_hbm.at[:, k] for k in range(kyl)] + [part_hbm],
        [weights_ref.at[:, k] for k in range(kyl)] + [part_ref],
        sems,
    )
    forward = table_z(zl * groups, kz, 1, groups).T
    back_table = table_z(zl * groups, kz, 1, groups, SUB)
    kc = kxl * C
    rows = 2 * zl
    chunk = kyl * rows
    wide = send_ref.shape[1]
    cols = []
    for k in range(kyl):
        for f in range(2):
            cols.append(
                jnp.concatenate(
                    [
                        recv_ref[pl.ds((s * 2 + f) * chunk + k * rows, rows), :]
                        for s in range(groups)
                    ],
                    axis=0,
                )
            )
    hat = dot(forward, jnp.concatenate(cols, axis=1))
    for k in range(kyl):
        slope_hat = None
        for f in range(2):
            base = (k * 2 + f) * wide
            value = hat[:, base : base + wide]
            if f == 1:
                value = value * scale
                slope_hat = value[:, :kc]
            for r in range(2):
                hat_ref[pl.ds((f * 2 + r) * kyl + k, kz, stride=4 * kyl), :] = value[
                    r * kz : (r + 1) * kz
                ]
        each = spread(slope_hat, C).reshape(2, kz, C, kc)
        copies[k].wait()
        w_re, w_im = weights_ref[0, k], weights_ref[1, k]
        re = w_re * each[0] + w_im * each[1]
        im = w_re * each[1] - w_im * each[0]
        dual = jnp.stack([re, im]).reshape(2, kz, C // SUB, SUB, kc)
        dual = jnp.sum(dual, axis=2).reshape(2 * kz * SUB, kc)
        back = widen(dot(back_table, dual), wide)
        for g in range(groups):
            send_ref[pl.ds(g * (chunk + part_rows) + k * rows, rows), :] = back[
                g * rows : (g + 1) * rows
            ]
    copies[kyl].wait()
    for g in range(groups):
        send_ref[pl.ds(g * (chunk + part_rows) + chunk, part_rows), :] = part_ref[...]


def grad_kernel(sizes, first, hat_ref, *refs):
    C, kxl, kyl, kz, steps = sizes
    out_hbm, out_ref, sems = refs[-3:]
    kc = kxl * C

    def copy(step):
        return pltpu.make_async_copy(
            out_ref.at[step], out_hbm.at[:, first + step], sems.at[step]
        )

    for step in range(steps):
        base = (first + step) * 4 * kyl
        in_re = hat_ref[pl.ds(base, kyl), :][:, :kc]
        in_im = hat_ref[pl.ds(base + kyl, kyl), :][:, :kc]
        wide = spread(hat_ref[pl.ds(base + 2 * kyl, 2 * kyl), :][:, :kc], C)
        wide = wide.reshape(2, kyl, C, kc)
        re, im = wide[0], wide[1]
        grad_re = re * in_re[:, None, :] + im * in_im[:, None, :]
        grad_im = im * in_re[:, None, :] - re * in_im[:, None, :]
        for kx in range(kxl):
            out_ref[step, 0, :, kx] = grad_re[:, :, kx * C : (kx + 1) * C]
            out_ref[step, 1, :, kx] = grad_im[:, :, kx * C : (kx + 1) * C]
        copy(step).start()
    for step in range(steps):
        copy(step).wait()


def y_back_kernel(sizes, recv_ref, *refs):
    send_ref = refs[-1]
    C, zl, kxl, ky, kyl, cells, yl, groups, dests, part_rows = sizes
    wide = recv_ref.shape[1]
    rows = 2 * zl
    kr = 2 * kxl
    chunk = kyl * rows + part_rows
    out_chunk = yl * kr + part_rows
    cols = []
    for z in range(zl):
        cols.append(
            jnp.concatenate(
                [
                    recv_ref[pl.ds(s * chunk + r * zl + z, kyl, stride=rows), :]
                    for r in range(2)
                    for s in range(groups)
                ],
                axis=0,
            )
        )
    out = dot(table_y(cells, ky, 1), jnp.concatenate(cols, axis=1))
    total = recv_ref[pl.ds(kyl * rows, part_rows), :]
    for s in range(1, groups):
        total = total + recv_ref[pl.ds(s * chunk + kyl * rows, part_rows), :]
    for kx in range(kxl):
        for r in range(2):
            block = out[r * cells : (r + 1) * cells]
            piece = jnp.concatenate(
                [block[:, z * wide + kx * C : z * wide + (kx + 1) * C] for z in range(zl)], axis=1
            )
            for d in range(dests):
                send_ref[pl.ds(d * out_chunk + kx * 2 + r, yl, stride=kr), :] = piece[
                    d * yl : (d + 1) * yl
                ]
    for d in range(dests):
        send_ref[pl.ds(d * out_chunk + yl * kr, part_rows), :] = total


def x_back_kernel(sizes, recv_ref, local_ref, fix_ref, out_ref, mix_ref, coef_ref, work_ref):
    C, zl, yl, kxl, sources, part_rows = sizes
    table = table_x(out_ref.shape[1], sources * kxl, 0)
    kr = 2 * kxl
    chunk = yl * kr + part_rows
    edge = 2 * C * yl
    for y in range(yl):
        column = jnp.concatenate(
            [recv_ref[pl.ds(s * chunk + y * kr, kr), :] for s in range(sources)], axis=0
        )
        value = dot(column.T, table)
        if y == 0:
            value = value + fix_ref[pl.ds(edge, zl * C), :]
        if y == yl - 1:
            value = value + fix_ref[pl.ds(edge + zl * C, zl * C), :]
        for z in range(zl):
            for half in range(value.shape[1] // LANES):
                work_ref[half, pl.ds(z * yl + y, C, stride=zl * yl), :] = value[
                    z * C : (z + 1) * C, half * LANES : (half + 1) * LANES
                ]
    for half in range(out_ref.shape[1] // LANES):
        cut = pl.ds(half * LANES, LANES)
        for c in range(C):
            for z in range(zl):
                row = pl.ds((c * zl + z) * yl, yl)
                value = work_ref[half, row, :] + local_ref[row, cut]
                if z == 0:
                    value = value + fix_ref[pl.ds(c * yl, yl), cut]
                if z == zl - 1:
                    value = value + fix_ref[pl.ds((C + c) * yl, yl), cut]
                out_ref[row, cut] = value
    total = recv_ref[pl.ds(yl * kr, part_rows), :]
    for s in range(1, sources):
        total = total + recv_ref[pl.ds(s * chunk + yl * kr, part_rows), :]
    total = total * (1.0 / 1024.0)
    high = C // kxl
    for b in range(kxl):
        mix_ref[pl.ds(b * high, high), :] = total[:high, b * C : (b + 1) * C]
    coef_ref[...] = total[high : high + 5, :C]


EXACT = lax.Precision.HIGHEST


def one_hot(rows, columns, times, major):
    if rows > columns:
        channel = iota((rows, columns), 0)
        channel = channel // times if major else jnp.remainder(channel, columns)
        return (channel == iota((rows, columns), 1)).astype(jnp.float32)
    channel = iota((rows, columns), 1)
    channel = channel // times if major else jnp.remainder(channel, rows)
    return (channel == iota((rows, columns), 0)).astype(jnp.float32)


def mixer(mix, C, times, major):
    n = C * times
    tall, flat = one_hot(n, C, times, major), one_hot(C, n, times, major)
    full = dot(dot(tall, mix, ((1,), (1,)), EXACT), flat, precision=EXACT)
    if major:
        place = [jnp.remainder(iota((n, n), axis), times) for axis in range(2)]
    else:
        place = [iota((n, n), axis) // C for axis in range(2)]
    return jnp.where(place[0] == place[1], full, 0.0)


def layer(ref, z, C, zl, yl):
    return jnp.concatenate([ref[pl.ds((c * zl + z) * yl, yl), :] for c in range(C)], axis=0)


def inner_kernel(sizes, in_hbm, slope_ref, mix_hbm, coefs_hbm, weights_hbm, out_ref, gram_ref,
                 sums_ref, kron_ref, packed_ref, in_ref, mix_ref, coefs_ref, raw_ref, sems):
    C, zl, yl, kxl, kyl, kz = sizes
    length = in_ref.shape[1]
    copies = fetch((mix_hbm, coefs_hbm, in_hbm), (mix_ref, coefs_ref, in_ref), sems)

    def raw_copy(z):
        return pltpu.make_async_copy(weights_hbm.at[:, z], raw_ref.at[z], sems.at[3 + z])

    for z in range(kz):
        raw_copy(z).start()

    def up(values):
        cube = values.reshape(C, yl, length)
        return jnp.concatenate(
            [jnp.zeros((C, 1, length), jnp.float32), cube[:, : yl - 1]], axis=1
        ).reshape(C * yl, length)

    def down(values):
        cube = values.reshape(C, yl, length)
        return jnp.concatenate(
            [cube[:, 1:], jnp.zeros((C, 1, length), jnp.float32)], axis=1
        ).reshape(C * yl, length)

    tall = one_hot(C * yl, C, yl, True)
    copies[0].wait()
    copies[1].wait()
    coef_rows = dot(tall, coefs_ref[...], ((1,), (1,)), EXACT)
    coef = [coef_rows[:, j : j + 1] for j in range(5)]
    kron = mixer(mix_ref[...], C, yl, True)
    kron_ref[...] = kron
    slopes = [layer(slope_ref, z, C, zl, yl) for z in range(zl)]
    hidden = [dot(kron, slopes[z]) for z in range(zl)]
    copies[2].wait()
    inputs = [layer(in_ref, z, C, zl, yl) for z in range(zl)]
    gram = None
    sums = [None] * 5
    for z in range(zl):
        shifted = {0: hidden[z], 1: up(hidden[z]), 2: down(hidden[z])}
        if z > 0:
            shifted[3] = hidden[z - 1]
        if z + 1 < zl:
            shifted[4] = hidden[z + 1]
        total = None
        for j, value in shifted.items():
            term = coef[j] * value
            total = term if total is None else total + term
            term = inputs[z] * value
            sums[j] = term if sums[j] is None else sums[j] + term
        for c in range(C):
            out_ref[pl.ds((c * zl + z) * yl, yl), :] = total[c * yl : (c + 1) * yl]
        stencil = coef[0] * inputs[z] + coef[1] * down(inputs[z]) + coef[2] * up(inputs[z])
        if z + 1 < zl:
            stencil = stencil + coef[3] * inputs[z + 1]
        if z > 0:
            stencil = stencil + coef[4] * inputs[z - 1]
        term = dot(slopes[z], stencil, ((1,), (1,)))
        gram = term if gram is None else gram + term
    gram_ref[...] = gram
    columns = []
    for term in sums:
        if term is None:
            columns.append(jnp.zeros((C * yl, 1), jnp.float32))
        else:
            columns.append(jnp.sum(term, axis=1, keepdims=True))
    columns.append(jnp.zeros((C * yl, SUB - 5), jnp.float32))
    sums_ref[...] = jnp.concatenate(columns, axis=1)
    for z in range(kz):
        raw_copy(z).wait()
        for part in range(2):
            for k in range(kyl):
                packed_ref[part, k, z] = jnp.concatenate(
                    [raw_ref[z, part, k, kx] for kx in range(kxl)], axis=1
                )


def edge_kernel(sizes, ybefore_ref, yafter_ref, zbefore_ref, zafter_ref, *refs):
    C, zl, yl, kxl = sizes
    hbms, (fix_ref, part_ref), refs, sems = refs[:6], refs[6:8], refs[8:-1], refs[-1]
    for copy in fetch(hbms, refs, sems):
        copy.wait()
    in_ref, mix_ref, coefs_ref, kron_ref, gram_ref, sums_ref = refs
    length = in_ref.shape[1]
    first, last = layer(in_ref, 0, C, zl, yl), layer(in_ref, zl - 1, C, zl, yl)
    layers = [layer(in_ref, z, C, zl, yl) for z in range(zl)]

    def row_of(y):
        return jnp.concatenate([each.reshape(C, yl, length)[:, y] for each in layers], axis=0)

    low, high_row = row_of(0), row_of(yl - 1)
    flat_y, tall_y = one_hot(C, C * yl, yl, True), one_hot(C * yl, C, yl, True)
    flat_z, tall_z = one_hot(C, C * zl, zl, False), one_hot(C * zl, C, zl, False)
    coef_y = dot(tall_y, coefs_ref[...], ((1,), (1,)), EXACT)
    coef_z = dot(tall_z, coefs_ref[...], ((1,), (1,)), EXACT)
    kron_z = mixer(mix_ref[...], C, zl, False)
    zbefore, zafter = zbefore_ref[...], zafter_ref[...]
    ybefore, yafter = ybefore_ref[...], yafter_ref[...]
    hidden_zb, hidden_za = dot(kron_ref[...], zbefore), dot(kron_ref[...], zafter)
    hidden_yb, hidden_ya = dot(kron_z, ybefore), dot(kron_z, yafter)
    n, m = C * yl, C * zl
    fix_ref[pl.ds(0, n), :] = coef_y[:, 3:4] * hidden_zb
    fix_ref[pl.ds(n, n), :] = coef_y[:, 4:5] * hidden_za
    fix_ref[pl.ds(2 * n, m), :] = coef_z[:, 1:2] * hidden_yb
    fix_ref[pl.ds(2 * n + m, m), :] = coef_z[:, 2:3] * hidden_ya
    gram = gram_ref[...]
    gram = gram + dot(zbefore, coef_y[:, 3:4] * first, ((1,), (1,)))
    gram = gram + dot(zafter, coef_y[:, 4:5] * last, ((1,), (1,)))
    edge = dot(ybefore, coef_z[:, 1:2] * low, ((1,), (1,)))
    edge = edge + dot(yafter, coef_z[:, 2:3] * high_row, ((1,), (1,)))
    same_y = jnp.remainder(iota((n, n), 0), yl) == jnp.remainder(iota((n, n), 1), yl)
    same_z = iota((m, m), 0) // C == iota((m, m), 1) // C
    mix = dot(dot(flat_y, jnp.where(same_y, gram, 0.0)), flat_y, ((1,), (1,)))
    mix = mix + dot(dot(flat_z, jnp.where(same_z, edge, 0.0)), flat_z, ((1,), (1,)))

    def column(values, place):
        total = jnp.sum(values, axis=1, keepdims=True)
        return jnp.where(iota((values.shape[0], SUB), 1) == place, total, 0.0)

    by_y = sums_ref[...] + column(first * hidden_zb, 3) + column(last * hidden_za, 4)
    by_z = column(low * hidden_yb, 1) + column(high_row * hidden_ya, 2)
    by_channel = dot(flat_y, by_y) + dot(flat_z, by_z)
    eye = (iota((SUB, SUB), 0) == iota((SUB, SUB), 1)).astype(jnp.float32)
    coefs = dot(eye, by_channel, ((1,), (1,)))
    high = C // kxl
    packed = jnp.concatenate([mix[b * high : (b + 1) * high] for b in range(kxl)], axis=1)
    part_ref[pl.ds(0, high), :] = widen(packed, part_ref.shape[1])
    part_ref[pl.ds(high, SUB), :] = widen(coefs, part_ref.shape[1])


def per_device(input_field, pre_activation, cotangent, spectral_weights, mix_weights, coefficients):
    C, zl, yl, length = input_field.shape
    groups_y = lax.axis_size("gy")
    groups_z = lax.axis_size("gz")
    cells_y, cells_z = yl * groups_y, zl * groups_z
    kz, kyl, kxl = spectral_weights.shape[1:4]
    modes_y, modes_x = kyl * groups_z, kxl * groups_y
    scale = 1.0 / (length * cells_y * cells_z)
    rows = C * zl * yl
    kr = 2 * kxl
    kc = kxl * C
    lanes = zl * C
    wide = max(kc, LANES)
    part_rows = C // kxl + SUB

    flat = lambda values: values.reshape(rows, length)
    exchange = functools.partial(lax.all_to_all, split_axis=0, concat_axis=0, tiled=True)
    far = pl.BlockSpec(memory_space=pl.ANY)
    near = pl.BlockSpec(memory_space=pltpu.VMEM)

    slope, send, ylast, yfirst, zlast, zfirst = call(
        functools.partial(x_kernel, (C, zl, yl, groups_y, kr)),
        (
            vmem(rows, length),
            f32(groups_y * 2 * yl * kr, lanes),
            far_out(C * zl, length),
            far_out(C * zl, length),
            far_out(C * yl, length),
            far_out(C * yl, length),
        ),
        (
            hbm(flat(input_field)),
            hbm(flat(pre_activation)),
            hbm(flat(cotangent)),
        ),
        24,
        flops=4 * rows * length * 2 * modes_x,
        bytes_accessed=6 * rows * length * 4,
        in_specs=[far] * 3,
        scratch=[
            pltpu.VMEM((rows, length), jnp.float32),
            pltpu.VMEM((rows, length), jnp.float32),
            pltpu.VMEM((rows, length), jnp.float32),
            pltpu.VMEM((2, rows, -(-2 * modes_x // LANES) * LANES), jnp.float32),
            pltpu.VMEM((rows, LANES), jnp.float32),
            pltpu.SemaphoreType.DMA((3,)),
        ],
    )
    lines = exchange(send, "gy")

    def from_below(values, axis):
        return lax.ppermute(values, axis, [(i, i + 1) for i in range(lax.axis_size(axis) - 1)])

    def from_above(values, axis):
        return lax.ppermute(values, axis, [(i + 1, i) for i in range(lax.axis_size(axis) - 1)])

    ybefore, yafter = from_below(ylast, "gy"), from_above(yfirst, "gy")
    zbefore, zafter = from_below(zlast, "gz"), from_above(zfirst, "gz")

    local, gram, sums, kron, weights = call(
        functools.partial(inner_kernel, (C, zl, yl, kxl, kyl, kz)),
        (
            vmem(rows, length),
            far_out(C * yl, C * yl),
            far_out(C * yl, SUB),
            far_out(C * yl, C * yl),
            far_out(2, kyl, kz, C, kc),
        ),
        (
            hbm(flat(input_field)),
            held(slope),
            hbm(mix_weights),
            hbm(coefficients),
            hbm(spectral_weights),
        ),
        44,
        flops=2 * 12 * (C * yl) ** 2 * length,
        bytes_accessed=2 * kz * kyl * kxl * C * 128 * 4 * 2,
        in_specs=[far, near, far, far, far],
        scratch=[
            pltpu.VMEM((rows, length), jnp.float32),
            pltpu.VMEM((C, C), jnp.float32),
            pltpu.VMEM(coefficients.shape, jnp.float32),
            pltpu.VMEM((kz, 2, kyl, kxl, C, C), jnp.float32),
            pltpu.SemaphoreType.DMA((3 + kz,)),
        ],
    )

    send = call(
        functools.partial(y_kernel, (C, zl, kxl, modes_y, kyl, yl, groups_y)),
        f32(groups_z * 2 * kyl * 2 * zl, wide),
        (lines, held(ybefore), held(yafter), held(zbefore), held(zafter), hbm(gram)),
        16,
        flops=16 * modes_y * cells_y * kxl * lanes,
        bytes_accessed=4 * MIB,
        in_specs=[near] + [far] * 5,
    )
    owned = exchange(send, "gz")

    fix, part = call(
        functools.partial(edge_kernel, (C, zl, yl, kxl)),
        (vmem(2 * C * yl + 2 * C * zl, length), far_out(part_rows, wide)),
        (
            held(ybefore),
            held(yafter),
            held(zbefore),
            held(zafter),
            hbm(flat(input_field)),
            hbm(mix_weights),
            hbm(coefficients),
            hbm(kron),
            hbm(gram),
            hbm(sums),
        ),
        24,
        flops=2 * 6 * (C * yl) ** 2 * length,
        bytes_accessed=3 * MIB,
        in_specs=[near] * 4 + [far] * 6,
        scratch=[
            pltpu.VMEM((rows, length), jnp.float32),
            pltpu.VMEM((C, C), jnp.float32),
            pltpu.VMEM(coefficients.shape, jnp.float32),
            pltpu.VMEM(kron.shape, jnp.float32),
            pltpu.VMEM(gram.shape, jnp.float32),
            pltpu.VMEM(sums.shape, jnp.float32),
            pltpu.SemaphoreType.DMA((6,)),
        ],
    )

    chunk = kyl * 2 * zl + part_rows
    send, hats = call(
        functools.partial(z_kernel, (C, zl, kxl, kyl, kz, groups_z, part_rows, scale)),
        (f32(groups_z * chunk, wide), vmem(kz * 4 * kyl, wide)),
        (owned, hbm(weights), hbm(part)),
        24,
        flops=16 * kz * kyl * C * kc,
        bytes_accessed=6 * MIB,
        in_specs=[near, far, far],
        scratch=[
            pltpu.VMEM((2, kyl, kz, C, kc), jnp.float32),
            pltpu.VMEM((part_rows, wide), jnp.float32),
            pltpu.SemaphoreType.DMA((kyl + 1,)),
        ],
    )
    returned = exchange(send, "gz")

    def gradient(first, steps, *before):
        return call(
            functools.partial(grad_kernel, (C, kxl, kyl, kz, steps), first),
            pltpu.HBM((2, kz, kyl, kxl, C, C), jnp.float32),
            (held(hats), *[hbm(each) for each in before]),
            16,
            flops=16 * steps * kyl * C * kc,
            bytes_accessed=2 * steps * kyl * kxl * C * 128 * 4,
            in_specs=[near] + [far] * len(before),
            out_specs=far,
            scratch=[
                pltpu.VMEM((steps, 2, kyl, kxl, C, C), jnp.float32),
                pltpu.SemaphoreType.DMA((steps,)),
            ],
            input_output_aliases={1: 0} if before else {},
        )

    grad_half = gradient(0, kz // 2)

    send = call(
        functools.partial(
            y_back_kernel,
            (C, zl, kxl, modes_y, kyl, cells_y, yl, groups_z, groups_y, part_rows),
        ),
        f32(groups_y * (yl * kr + part_rows), lanes),
        (returned, hbm(grad_half)),
        16,
        flops=8 * modes_y * cells_y * kxl * lanes,
        bytes_accessed=2 * MIB,
        in_specs=[near, far],
    )
    arrived = exchange(send, "gy")
    grad_spectral = gradient(kz // 2, kz - kz // 2, grad_half)

    grad_input, grad_mix, grad_coef = call(
        functools.partial(x_back_kernel, (C, zl, yl, kxl, groups_y, part_rows)),
        (f32(rows, length), f32(C, C), f32(5, C)),
        (arrived, held(local), held(fix)),
        16,
        flops=2 * rows * length * 2 * modes_x,
        bytes_accessed=3 * MIB,
        scratch=[pltpu.VMEM((length // LANES, rows, LANES), jnp.float32)],
    )
    return (grad_input.reshape(input_field.shape), grad_spectral, grad_mix, grad_coef)


def solution(mesh):
    in_specs = (
        P(None, "gz", "gy", None),
        P(None, "gz", "gy", None),
        P(None, "gz", "gy", None),
        P(None, None, "gz", "gy", None, None),
        P(),
        P(),
    )
    out_specs = (P(None, "gz", "gy", None), P(None, None, "gz", "gy", None, None), P(), P())
    return jax.shard_map(
        per_device, mesh=mesh, in_specs=in_specs, out_specs=out_specs, check_vma=False
    )
```

time: 110 us -> 78.9 us (0.72); the launches traced: 108 us -> 78.4 us
  local copies, waits for them, and re-layouts: 37.5 us -> 0 us
  waiting for transfers between devices: 0.02 us -> 9.09 us
  blocking collectives: 8.19 us -> 0 us
  Pallas kernels: 31.5 us -> 37.7 us
  starting transfers between devices: 27.4 us -> 30.8 us
  other arithmetic: 2.73 us -> 0 us
    unnamed x67 -> x0, local copies, waits for them, and re-layouts: 30.5 us -> none
    all_to_all x1 -> x0, blocking collectives: 8.19 us -> none  [per_device(): returned = exchange(send, 'gz')]
    pallas_call x8 -> x9, Pallas kernels: 31.5 us -> 37.7 us  [call(): pl.pallas_call(body, out_shape=outs, scratch_shapes=list(scratch), compil...]
    all_to_all x1, waiting for transfers between devices: 0.01 us -> 6.02 us  [per_device(): arrived = exchange(send, 'gy')]
    mul x2 -> x0, local copies, waits for them, and re-layouts: 4.85 us -> none  [the longest x1 4.68 us: per_device(): jnp.kron(mixed, jnp.eye(yl, dtype=jnp.float32))]
    all_to_all x0 -> x1, starting transfers between devices: none -> 3.36 us  [per_device(): returned = exchange(send, 'gz')]
    mul x2 -> x0, other arithmetic: 2.72 us -> none  [the longest x1 2.61 us: per_device(): jnp.kron(mixed, jnp.eye(yl, dtype=jnp.float32))]
    all_to_all x1, waiting for transfers between devices: 0.01 us -> 2.09 us  [per_device(): owned = exchange(send, 'gz')]
  transfers between devices with their start and end apart: 7 -> 8, of which waited for: 0 -> 3; matrix products, arithmetic and copies ran while one was open for 9% -> 0% of each run, Pallas kernels for 20% -> 28%
where the time goes in v1:
time: 78.9 us; the launch traced here: 78.4 us
  Pallas kernels  37.7 us (48%)
  starting transfers between devices  30.8 us (39%)
  waiting for transfers between devices  9.09 us (12%)
    pallas_call x9, Pallas kernels, call(): pl.pallas_call(body, out_shape=outs, scratch_shapes=list(scratch), compil...  37.7 us
    all_to_all x1, starting transfers between devices, per_device(): lines = exchange(send, 'gy')  7.26 us
    all_to_all x1, starting transfers between devices, per_device(): arrived = exchange(send, 'gy')  6.62 us
    all_to_all x1, waiting for transfers between devices, per_device(): arrived = exchange(send, 'gy')  6.02 us
    all_to_all x1, starting transfers between devices, per_device(): owned = exchange(send, 'gz')  5.75 us
    ppermute x2, starting transfers between devices, from_below(): lax.ppermute(values, axis, [(i, i + 1) for i in range(lax.axis_size(axis)...  5.23 us
    all_to_all x1, starting transfers between devices, per_device(): returned = exchange(send, 'gz')  3.36 us
    ppermute x2, starting transfers between devices, from_above(): lax.ppermute(values, axis, [(i + 1, i) for i in range(lax.axis_size(axis)...  2.58 us
  transfers between devices with their start and end apart: 8, of which 3 were waited for; matrix products, arithmetic and copies ran while one was open for 0% of the time, Pallas kernels for 28%

profile of v1, /device:TPU:0, one launch (start us, length us, event | category | flops | bytes accessed | tf_op | source)
XLA Modules:
  0.0 78.4 jit_solution(9009603687974246165)
XLA Ops:
  0.6 5.1 %shard_map.93 = (f32[1024,256]{1,0:T(8,128)S(1)}, f32[1024,128]{1,0:T(8,128)}, f32[128,256]{1,0:T(8,128)}, f32[128,256]{1,0:T(8,128)}, f32[256,256]{1,0:T(8,128)}, /*index=5*/f32[256,256]{1,0:T(8,128)}) custom-call(f32[1024,256]{1,0:T(8,128)} %bitcast.16, f32[1024,256]{1,0:T(8,128)} %bitcast.19, f32[1024,256]{1,0:T(8,128)} %bitcast.20), custom_call_target="tpu_custom_call" | custom-call | flops 67108864 | bytes 6291456 | tf_op jit(solution)/shard_map/pallas_call | solution.py:25
  5.7 7.3 %all-to-all-start = ((f32[8,128,128]{2,1,0:T(8,128)}), f32[8,128,128]{2,1,0:T(8,128)S(1)}, u32[]{:S(2)}, u32[]{:S(2)}) async-start(f32[8,128,128]{2,1,0:T(8,128)} %bitcast.3), calls=%async_computation | async-start | bytes 1048576 | tf_op jit(solution)/shard_map/all_to_all | solution.py:586
  13.0 1.5 %collective-permute-start.2 = (f32[256,256]{1,0:T(8,128)}, f32[256,256]{1,0:T(8,128)S(1)}, u32[]{:S(2)}, u32[]{:S(2)}) collective-permute-start(f32[256,256]{1,0:T(8,128)} %get-tuple-element.25), channel_id=1, source_target_pairs={{0,8},{8,16},{16,24},{1,9},{9,17},{17,25},{2,10},{10,18},{18,26},{... | collective-permute-start | bytes 786440 | tf_op jit(solution)/shard_map/ppermute | solution.py:589
  14.4 1.3 %collective-permute-start.3 = (f32[256,256]{1,0:T(8,128)}, f32[256,256]{1,0:T(8,128)S(1)}, u32[]{:S(2)}, u32[]{:S(2)}) collective-permute-start(f32[256,256]{1,0:T(8,128)} %get-tuple-element.26), channel_id=1, source_target_pairs={{8,0},{16,8},{24,16},{9,1},{17,9},{25,17},{10,2},{18,10},{26,18},{... | collective-permute-start | bytes 786440 | tf_op jit(solution)/shard_map/ppermute | solution.py:592
  15.7 3.8 %collective-permute-start = (f32[128,256]{1,0:T(8,128)}, f32[128,256]{1,0:T(8,128)S(1)}, u32[]{:S(2)}, u32[]{:S(2)}) collective-permute-start(f32[128,256]{1,0:T(8,128)} %get-tuple-element.23), channel_id=1, source_target_pairs={{0,1},{1,2},{2,3},{3,4},{4,5},{5,6},{6,7},{8,9},{9,10},{10,11},{11... | collective-permute-start | bytes 393224 | tf_op jit(solution)/shard_map/ppermute | solution.py:589
  19.5 1.3 %collective-permute-start.1 = (f32[128,256]{1,0:T(8,128)}, f32[128,256]{1,0:T(8,128)S(1)}, u32[]{:S(2)}, u32[]{:S(2)}) collective-permute-start(f32[128,256]{1,0:T(8,128)} %get-tuple-element.24), channel_id=1, source_target_pairs={{1,0},{2,1},{3,2},{4,3},{5,4},{6,5},{7,6},{9,8},{10,9},{11,10},{12... | collective-permute-start | bytes 393224 | tf_op jit(solution)/shard_map/ppermute | solution.py:592
  20.8 10.4 %shard_map.94 = (f32[1024,256]{1,0:T(8,128)S(1)}, f32[256,256]{1,0:T(8,128)}, f32[256,8]{1,0:T(8,128)}, f32[256,256]{1,0:T(8,128)}, f32[2,8,16,32,128]{4,3,2,1,0:T(8,128)}) custom-call(f32[1024,256]{1,0:T(8,128)} %bitcast.17, f32[1024,256]{1,0:T(8,128)S(1)} %get-tuple-element.27.slope_ref, f32[32,32]{1,0:T(8,128)} %refs_1_.1, f32[5,32]{1,0:T(8,128)} %refs_2_.1, ...), custom_call_target="tpu_custom_call" | custom-call | flops 402653184 | bytes 33554432 | tf_op jit(solution)/shard_map/pallas_call | solution.py:25
  31.2 0.0 collective-permute-done.refs_0_.ybefore_ref
  31.2 0.0 collective-permute-done.1.refs_1_.yafter_ref
  31.2 0.0 collective-permute-done.2.refs_2_.zbefore_ref
  31.2 0.0 collective-permute-done.3.refs_3_.zafter_ref
  31.2 0.0 all-to-all-done
  31.2 1.2 %shard_map.95 = f32[512,128]{1,0:T(8,128)} custom-call(f32[1024,128]{1,0:T(8,128)S(1)} %bitcast.12, f32[128,256]{1,0:T(8,128)S(1)} %collective-permute-done.refs_0_.ybefore_ref, f32[128,256]{1,0:T(8,128)S(1)} %collective-permute-done.1.refs_1_.yafter_ref, f32[256,256]{1,0:T(8,128)S(1)} %collective-permute-done.2.refs_2_.zbefore_ref, ...), custom_call_target="tpu_custom_call" | custom-call | flops 16777216 | bytes 4194304 | tf_op jit(solution)/shard_map/pallas_call | solution.py:25
  32.5 5.8 %all-to-all-start.1 = ((f32[4,128,128]{2,1,0:T(8,128)}), f32[4,128,128]{2,1,0:T(8,128)S(1)}, u32[]{:S(2)}, u32[]{:S(2)}) async-start(f32[4,128,128]{2,1,0:T(8,128)} %bitcast.5), calls=%async_computation.1 | async-start | bytes 524288 | tf_op jit(solution)/shard_map/all_to_all | solution.py:635
  38.2 3.9 %shard_map.96 = (f32[768,256]{1,0:T(8,128)S(1)}, f32[16,128]{1,0:T(8,128)}) custom-call(f32[128,256]{1,0:T(8,128)S(1)} %collective-permute-done.refs_0_.ybefore_ref, f32[128,256]{1,0:T(8,128)S(1)} %collective-permute-done.1.refs_1_.yafter_ref, f32[256,256]{1,0:T(8,128)S(1)} %collective-permute-done.2.refs_2_.zbefore_ref, ...), custom_call_target="tpu_custom_call" | custom-call | flops 201326592 | bytes 3145728 | tf_op jit(solution)/shard_map/pallas_call | solution.py:25
  42.2 2.1 %all-to-all-done.1 = f32[4,128,128]{2,1,0:T(8,128)S(1)} async-done(((f32[4,128,128]{2,1,0:T(8,128)}), f32[4,128,128]{2,1,0:T(8,128)S(1)}, u32[]{:S(2)}, u32[]{:S(2)}) %all-to-all-start.1) | async-done | bytes 262176 | tf_op jit(solution)/shard_map/all_to_all | solution.py:635
  44.3 5.5 %shard_map.97 = (f32[320,128]{1,0:T(8,128)}, f32[512,128]{1,0:T(8,128)S(1)}) custom-call(f32[512,128]{1,0:T(8,128)S(1)} %bitcast.14, f32[2,8,16,32,128]{4,3,2,1,0:T(8,128)} %get-tuple-element.29.weights_hbm, f32[16,128]{1,0:T(8,128)} %get-tuple-element.32.part_hbm), custom_call_target="tpu_custom_call" | custom-call | flops 8388608 | bytes 6291456 | tf_op jit(solution)/shard_map/pallas_call | solution.py:25
  49.8 3.4 %all-to-all-start.2 = ((f32[4,80,128]{2,1,0:T(8,128)}), f32[4,80,128]{2,1,0:T(8,128)S(1)}, u32[]{:S(2)}, u32[]{:S(2)}) async-start(f32[4,80,128]{2,1,0:T(8,128)} %bitcast.7), calls=%async_computation.2 | async-start | bytes 327680 | tf_op jit(solution)/shard_map/all_to_all | solution.py:682
  53.2 4.0 %shard_map.98.refs_0_ = f32[2,16,8,4,32,32]{5,4,3,2,1,0:T(8,128)} custom-call(f32[512,128]{1,0:T(8,128)S(1)} %get-tuple-element.34.hat_ref), custom_call_target="tpu_custom_call" | custom-call | flops 4194304 | bytes 8388608 | tf_op jit(solution)/shard_map/pallas_call | solution.py:25
  57.1 1.0 %all-to-all-done.2 = f32[4,80,128]{2,1,0:T(8,128)S(1)} async-done(((f32[4,80,128]{2,1,0:T(8,128)}), f32[4,80,128]{2,1,0:T(8,128)S(1)}, u32[]{:S(2)}, u32[]{:S(2)}) %all-to-all-start.2) | async-done | bytes 163872 | tf_op jit(solution)/shard_map/all_to_all | solution.py:682
  58.1 1.3 %shard_map.99 = f32[640,128]{1,0:T(8,128)} custom-call(f32[320,128]{1,0:T(8,128)S(1)} %bitcast.15, f32[2,16,8,4,32,32]{5,4,3,2,1,0:T(8,128)} %shard_map.98.refs_0_), custom_call_target="tpu_custom_call" | custom-call | flops 8388608 | bytes 2097152 | tf_op jit(solution)/shard_map/pallas_call | solution.py:25
  59.4 6.6 %all-to-all-start.3 = ((f32[8,80,128]{2,1,0:T(8,128)}), f32[8,80,128]{2,1,0:T(8,128)S(1)}, u32[]{:S(2)}, u32[]{:S(2)}) async-start(f32[8,80,128]{2,1,0:T(8,128)} %bitcast.9), calls=%async_computation.3 | async-start | bytes 655360 | tf_op jit(solution)/shard_map/all_to_all | solution.py:715
  66.0 4.0 %shard_map.101 = f32[2,16,8,4,32,32]{5,4,3,2,1,0:T(8,128)} custom-call(f32[512,128]{1,0:T(8,128)S(1)} %get-tuple-element.34.hat_ref, f32[2,16,8,4,32,32]{5,4,3,2,1,0:T(8,128)} %shard_map.98.refs_0_), custom_call_target="tpu_custom_call", output_to_operand_aliasing={{}: (1, {})} | custom-call | flops 4194304 | bytes 8388608 | tf_op jit(solution)/shard_map/pallas_call | solution.py:25
  70.0 6.0 %all-to-all-done.3 = f32[8,80,128]{2,1,0:T(8,128)S(1)} async-done(((f32[8,80,128]{2,1,0:T(8,128)}), f32[8,80,128]{2,1,0:T(8,128)S(1)}, u32[]{:S(2)}, u32[]{:S(2)}) %all-to-all-start.3) | async-done | bytes 327712 | tf_op jit(solution)/shard_map/all_to_all | solution.py:715
  76.0 2.4 %shard_map.100 = (f32[1024,256]{1,0:T(8,128)}, f32[32,32]{1,0:T(8,128)}, f32[5,32]{1,0:T(8,128)}) custom-call(f32[640,128]{1,0:T(8,128)S(1)} %bitcast.13, f32[1024,256]{1,0:T(8,128)S(1)} %get-tuple-element.35.local_ref, f32[768,256]{1,0:T(8,128)S(1)} %get-tuple-element.36.fix_ref), custom_call_target="tpu_custom_call" | custom-call | flops 33554432 | bytes 3145728 | tf_op jit(solution)/shard_map/pallas_call | solution.py:25
Async XLA Ops:
  5.7 25.5 %all-to-all-start = ((f32[8,128,128]{2,1,0:T(8,128)}), f32[8,128,128]{2,1,0:T(8,128)S(1)}, u32[]{:S(2)}, u32[]{:S(2)}) async-start(f32[8,128,128]{2,1,0:T(8,128)} %bitcast.3), calls=%async_computation | async-start | bytes 1048576 | tf_op jit(solution)/shard_map/all_to_all | solution.py:586
  13.0 18.2 %collective-permute-start.2 = (f32[256,256]{1,0:T(8,128)}, f32[256,256]{1,0:T(8,128)S(1)}, u32[]{:S(2)}, u32[]{:S(2)}) collective-permute-start(f32[256,256]{1,0:T(8,128)} %get-tuple-element.25), channel_id=1, source_target_pairs={{0,8},{8,16},{16,24},{1,9},{9,17},{17,25},{2,10},{10,18},{18,26},{... | collective-permute-start | bytes 786440 | tf_op jit(solution)/shard_map/ppermute | solution.py:589
  14.4 16.8 %collective-permute-start.3 = (f32[256,256]{1,0:T(8,128)}, f32[256,256]{1,0:T(8,128)S(1)}, u32[]{:S(2)}, u32[]{:S(2)}) collective-permute-start(f32[256,256]{1,0:T(8,128)} %get-tuple-element.26), channel_id=1, source_target_pairs={{8,0},{16,8},{24,16},{9,1},{17,9},{25,17},{10,2},{18,10},{26,18},{... | collective-permute-start | bytes 786440 | tf_op jit(solution)/shard_map/ppermute | solution.py:592
  15.7 15.5 %collective-permute-start = (f32[128,256]{1,0:T(8,128)}, f32[128,256]{1,0:T(8,128)S(1)}, u32[]{:S(2)}, u32[]{:S(2)}) collective-permute-start(f32[128,256]{1,0:T(8,128)} %get-tuple-element.23), channel_id=1, source_target_pairs={{0,1},{1,2},{2,3},{3,4},{4,5},{5,6},{6,7},{8,9},{9,10},{10,11},{11... | collective-permute-start | bytes 393224 | tf_op jit(solution)/shard_map/ppermute | solution.py:589
  19.5 11.7 %collective-permute-start.1 = (f32[128,256]{1,0:T(8,128)}, f32[128,256]{1,0:T(8,128)S(1)}, u32[]{:S(2)}, u32[]{:S(2)}) collective-permute-start(f32[128,256]{1,0:T(8,128)} %get-tuple-element.24), channel_id=1, source_target_pairs={{1,0},{2,1},{3,2},{4,3},{5,4},{6,5},{7,6},{9,8},{10,9},{11,10},{12... | collective-permute-start | bytes 393224 | tf_op jit(solution)/shard_map/ppermute | solution.py:592
  32.5 11.8 %all-to-all-start.1 = ((f32[4,128,128]{2,1,0:T(8,128)}), f32[4,128,128]{2,1,0:T(8,128)S(1)}, u32[]{:S(2)}, u32[]{:S(2)}) async-start(f32[4,128,128]{2,1,0:T(8,128)} %bitcast.5), calls=%async_computation.1 | async-start | bytes 524288 | tf_op jit(solution)/shard_map/all_to_all | solution.py:635
  49.8 8.3 %all-to-all-start.2 = ((f32[4,80,128]{2,1,0:T(8,128)}), f32[4,80,128]{2,1,0:T(8,128)S(1)}, u32[]{:S(2)}, u32[]{:S(2)}) async-start(f32[4,80,128]{2,1,0:T(8,128)} %bitcast.7), calls=%async_computation.2 | async-start | bytes 327680 | tf_op jit(solution)/shard_map/all_to_all | solution.py:682
  59.4 16.6 %all-to-all-start.3 = ((f32[8,80,128]{2,1,0:T(8,128)}), f32[8,80,128]{2,1,0:T(8,128)S(1)}, u32[]{:S(2)}, u32[]{:S(2)}) async-start(f32[8,80,128]{2,1,0:T(8,128)} %bitcast.9), calls=%async_computation.3 | async-start | bytes 655360 | tf_op jit(solution)/shard_map/all_to_all | solution.py:715

commit v2 on v1

--- a/solution.py
+++ b/solution.py
@@ -133,17 +133,27 @@
     return copies
 
 
+def halves(values):
+    high = values.astype(jnp.bfloat16)
+    return high, (values - high.astype(jnp.float32)).astype(jnp.bfloat16)
+
+
 def x_kernel(sizes, in_hbm, pre_hbm, cot_hbm, slope_ref, send_ref, ylast_ref, yfirst_ref,
              zlast_ref, zfirst_ref, in_ref, pre_ref, cot_ref, work_ref, half_ref, sems):
     C, zl, yl, dests, kr = sizes
     copies = fetch((in_hbm, pre_hbm, cot_hbm), (in_ref, pre_ref, cot_ref), sems)
-    table = table_x(in_ref.shape[1], dests * kr // 2, 1, work_ref.shape[2])
+    table = table_x(in_ref.shape[1], dests * kr // 2, 1, dests * kr)
+    high, low = halves(table)
+    both = jnp.concatenate([high, low], axis=1)
+    alone = jnp.concatenate([high, jnp.zeros_like(low)], axis=1)
 
     def transform(f, field):
-        work_ref[f] = dot(field, table)
+        upper, lower = halves(field)
+        work_ref[f] = dot(upper, both, precision=None) + dot(lower, alone, precision=None)
         for y in range(yl):
             rows = [work_ref[f, pl.ds(z * yl + y, C, stride=zl * yl), :] for z in range(zl)]
             turned = jnp.concatenate(rows, axis=0).T
+            turned = turned[: dests * kr] + turned[dests * kr :]
             for d in range(dests):
                 send_ref[pl.ds(((d * 2 + f) * yl + y) * kr, kr), :] = turned[d * kr : (d + 1) * kr]
 
@@ -378,7 +388,7 @@
     coef_ref[...] = total[high : high + 5, :C]
 
 
-EXACT = lax.Precision.HIGHEST
+EXACT = PRECISION
 
 
 def one_hot(rows, columns, times, major):
@@ -407,16 +417,20 @@
 
 
 def inner_kernel(sizes, in_hbm, slope_ref, mix_hbm, coefs_hbm, weights_hbm, out_ref, gram_ref,
-                 sums_ref, kron_ref, packed_ref, in_ref, mix_ref, coefs_ref, raw_ref, sems):
+                 sums_ref, packed_ref, in_ref, mix_ref, coefs_ref, raw_ref, sems):
     C, zl, yl, kxl, kyl, kz = sizes
     length = in_ref.shape[1]
     copies = fetch((mix_hbm, coefs_hbm, in_hbm), (mix_ref, coefs_ref, in_ref), sems)
 
-    def raw_copy(z):
-        return pltpu.make_async_copy(weights_hbm.at[:, z], raw_ref.at[z], sems.at[3 + z])
-
-    for z in range(kz):
-        raw_copy(z).start()
+    groups = math.gcd(4, kz)
+    size = kz // groups
+
+    def raw_copy(g):
+        cut = pl.ds(g * size, size)
+        return pltpu.make_async_copy(weights_hbm.at[:, cut], raw_ref.at[:, cut], sems.at[3 + g])
+
+    for g in range(groups):
+        raw_copy(g).start()
 
     def up(values):
         cube = values.reshape(C, yl, length)
@@ -436,7 +450,6 @@
     coef_rows = dot(tall, coefs_ref[...], ((1,), (1,)), EXACT)
     coef = [coef_rows[:, j : j + 1] for j in range(5)]
     kron = mixer(mix_ref[...], C, yl, True)
-    kron_ref[...] = kron
     slopes = [layer(slope_ref, z, C, zl, yl) for z in range(zl)]
     hidden = [dot(kron, slopes[z]) for z in range(zl)]
     copies[2].wait()
@@ -474,20 +487,34 @@
     columns.append(jnp.zeros((C * yl, SUB - 5), jnp.float32))
     sums_ref[...] = jnp.concatenate(columns, axis=1)
     for z in range(kz):
-        raw_copy(z).wait()
+        if z % size == 0:
+            raw_copy(z // size).wait()
         for part in range(2):
             for k in range(kyl):
                 packed_ref[part, k, z] = jnp.concatenate(
-                    [raw_ref[z, part, k, kx] for kx in range(kxl)], axis=1
+                    [raw_ref[part, z, k, kx] for kx in range(kxl)], axis=1
                 )
 
 
 def edge_kernel(sizes, ybefore_ref, yafter_ref, zbefore_ref, zafter_ref, *refs):
     C, zl, yl, kxl = sizes
-    hbms, (fix_ref, part_ref), refs, sems = refs[:6], refs[6:8], refs[8:-1], refs[-1]
-    for copy in fetch(hbms, refs, sems):
+    *hbms, fix_ref, part_ref, mix_ref, coefs_ref, in_ref, gram_ref, sums_ref, sems = refs
+    copies = fetch(hbms, (mix_ref, coefs_ref, in_ref, gram_ref, sums_ref), sems)
+
+    def inside(ref, axis, place):
+        return ref[...] * (lax.axis_index(axis) != place).astype(jnp.float32)
+
+    last_y, last_z = lax.axis_size("gy") - 1, lax.axis_size("gz") - 1
+    zbefore, zafter = inside(zbefore_ref, "gz", 0), inside(zafter_ref, "gz", last_z)
+    ybefore, yafter = inside(ybefore_ref, "gy", 0), inside(yafter_ref, "gy", last_y)
+    copies[0].wait()
+    copies[1].wait()
+    kron_y = mixer(mix_ref[...], C, yl, True)
+    kron_z = mixer(mix_ref[...], C, zl, False)
+    hidden_zb, hidden_za = dot(kron_y, zbefore), dot(kron_y, zafter)
+    hidden_yb, hidden_ya = dot(kron_z, ybefore), dot(kron_z, yafter)
+    for copy in copies[2:]:
         copy.wait()
-    in_ref, mix_ref, coefs_ref, kron_ref, gram_ref, sums_ref = refs
     length = in_ref.shape[1]
     first, last = layer(in_ref, 0, C, zl, yl), layer(in_ref, zl - 1, C, zl, yl)
     layers = [layer(in_ref, z, C, zl, yl) for z in range(zl)]
@@ -500,11 +527,6 @@
     flat_z, tall_z = one_hot(C, C * zl, zl, False), one_hot(C * zl, C, zl, False)
     coef_y = dot(tall_y, coefs_ref[...], ((1,), (1,)), EXACT)
     coef_z = dot(tall_z, coefs_ref[...], ((1,), (1,)), EXACT)
-    kron_z = mixer(mix_ref[...], C, zl, False)
-    zbefore, zafter = zbefore_ref[...], zafter_ref[...]
-    ybefore, yafter = ybefore_ref[...], yafter_ref[...]
-    hidden_zb, hidden_za = dot(kron_ref[...], zbefore), dot(kron_ref[...], zafter)
-    hidden_yb, hidden_ya = dot(kron_z, ybefore), dot(kron_z, yafter)
     n, m = C * yl, C * zl
     fix_ref[pl.ds(0, n), :] = coef_y[:, 3:4] * hidden_zb
     fix_ref[pl.ds(n, n), :] = coef_y[:, 4:5] * hidden_za
@@ -578,7 +600,7 @@
             pltpu.VMEM((rows, length), jnp.float32),
             pltpu.VMEM((rows, length), jnp.float32),
             pltpu.VMEM((rows, length), jnp.float32),
-            pltpu.VMEM((2, rows, -(-2 * modes_x // LANES) * LANES), jnp.float32),
+            pltpu.VMEM((2, rows, 4 * modes_x), jnp.float32),
             pltpu.VMEM((rows, LANES), jnp.float32),
             pltpu.SemaphoreType.DMA((3,)),
         ],
@@ -586,21 +608,22 @@
     lines = exchange(send, "gy")
 
     def from_below(values, axis):
-        return lax.ppermute(values, axis, [(i, i + 1) for i in range(lax.axis_size(axis) - 1)])
+        size = lax.axis_size(axis)
+        return lax.ppermute(values, axis, [(i, (i + 1) % size) for i in range(size)])
 
     def from_above(values, axis):
-        return lax.ppermute(values, axis, [(i + 1, i) for i in range(lax.axis_size(axis) - 1)])
+        size = lax.axis_size(axis)
+        return lax.ppermute(values, axis, [((i + 1) % size, i) for i in range(size)])
 
     ybefore, yafter = from_below(ylast, "gy"), from_above(yfirst, "gy")
     zbefore, zafter = from_below(zlast, "gz"), from_above(zfirst, "gz")
 
-    local, gram, sums, kron, weights = call(
+    local, gram, sums, weights = call(
         functools.partial(inner_kernel, (C, zl, yl, kxl, kyl, kz)),
         (
             vmem(rows, length),
             far_out(C * yl, C * yl),
             far_out(C * yl, SUB),
-            far_out(C * yl, C * yl),
             far_out(2, kyl, kz, C, kc),
         ),
         (
@@ -618,15 +641,15 @@
             pltpu.VMEM((rows, length), jnp.float32),
             pltpu.VMEM((C, C), jnp.float32),
             pltpu.VMEM(coefficients.shape, jnp.float32),
-            pltpu.VMEM((kz, 2, kyl, kxl, C, C), jnp.float32),
-            pltpu.SemaphoreType.DMA((3 + kz,)),
+            pltpu.VMEM((2, kz, kyl, kxl, C, C), jnp.float32),
+            pltpu.SemaphoreType.DMA((3 + math.gcd(4, kz),)),
         ],
     )
 
     send = call(
         functools.partial(y_kernel, (C, zl, kxl, modes_y, kyl, yl, groups_y)),
         f32(groups_z * 2 * kyl * 2 * zl, wide),
-        (lines, held(ybefore), held(yafter), held(zbefore), held(zafter), hbm(gram)),
+        (lines, held(ybefore), held(yafter), held(zbefore), held(zafter), hbm(weights)),
         16,
         flops=16 * modes_y * cells_y * kxl * lanes,
         bytes_accessed=4 * MIB,
@@ -642,25 +665,23 @@
             held(yafter),
             held(zbefore),
             held(zafter),
-            hbm(flat(input_field)),
             hbm(mix_weights),
             hbm(coefficients),
-            hbm(kron),
+            hbm(flat(input_field)),
             hbm(gram),
             hbm(sums),
         ),
         24,
         flops=2 * 6 * (C * yl) ** 2 * length,
         bytes_accessed=3 * MIB,
-        in_specs=[near] * 4 + [far] * 6,
+        in_specs=[near] * 4 + [far] * 5,
         scratch=[
-            pltpu.VMEM((rows, length), jnp.float32),
             pltpu.VMEM((C, C), jnp.float32),
             pltpu.VMEM(coefficients.shape, jnp.float32),
-            pltpu.VMEM(kron.shape, jnp.float32),
+            pltpu.VMEM((rows, length), jnp.float32),
             pltpu.VMEM(gram.shape, jnp.float32),
             pltpu.VMEM(sums.shape, jnp.float32),
-            pltpu.SemaphoreType.DMA((6,)),
+            pltpu.SemaphoreType.DMA((5,)),
         ],
     )
 

time: 78.9 us -> 71.1 us (0.901)
  starting transfers between devices: 30.8 us -> 24.3 us
  Pallas kernels: 37.7 us -> 35.9 us
    all_to_all x1, starting transfers between devices: 6.62 us -> 3.65 us  [per_device(): arrived = exchange(send, 'gy')]
    all_to_all x1, starting transfers between devices: 5.75 us -> 3.59 us  [per_device(): owned = exchange(send, 'gz')]
    pallas_call x9, Pallas kernels: 37.7 us -> 35.9 us  [call(): pl.pallas_call(body, out_shape=outs, scratch_shapes=list(scratch), compil...]
    ppermute x4, starting transfers between devices: 7.81 us -> 6.46 us  [the longest x2 4.44 us: from_above(): lax.ppermute(values, axis, [((i + 1) % size, i) for i in range(size)])]
  transfers between devices with their start and end apart: 8 -> 8, of which waited for: 3 -> 4; matrix products, arithmetic and copies ran while one was open for 0% -> 0% of each run, Pallas kernels for 28% -> 30%
where the time goes in v2:
time: 71.1 us; the launch traced here: 70.6 us
  Pallas kernels  35.9 us (50%)
  starting transfers between devices  24.3 us (34%)
  waiting for transfers between devices  9.63 us (14%)
  between operations  0.72 us (1%)
    pallas_call x9, Pallas kernels, call(): pl.pallas_call(body, out_shape=outs, scratch_shapes=list(scratch), compil...  35.9 us
    all_to_all x1, starting transfers between devices, per_device(): lines = exchange(send, 'gy')  7.26 us
    all_to_all x1, waiting for transfers between devices, per_device(): arrived = exchange(send, 'gy')  6.01 us
    ppermute x2, starting transfers between devices, from_above(): lax.ppermute(values, axis, [((i + 1) % size, i) for i in range(size)])  4.44 us
    all_to_all x1, starting transfers between devices, per_device(): arrived = exchange(send, 'gy')  3.65 us
    all_to_all x1, starting transfers between devices, per_device(): owned = exchange(send, 'gz')  3.59 us
    all_to_all x1, starting transfers between devices, per_device(): returned = exchange(send, 'gz')  3.36 us
    ppermute x2, starting transfers between devices, from_below(): lax.ppermute(values, axis, [(i, (i + 1) % size) for i in range(size)])  2.02 us
  transfers between devices with their start and end apart: 8, of which 4 were waited for; matrix products, arithmetic and copies ran while one was open for 0% of the time, Pallas kernels for 30%

profile of v2, /device:TPU:0, one launch (start us, length us, event | category | flops | bytes accessed | tf_op | source)
XLA Modules:
  0.0 70.6 jit_solution(13558312480524157592)
XLA Ops:
  0.6 4.5 %shard_map.93 = (f32[1024,256]{1,0:T(8,128)S(1)}, f32[1024,128]{1,0:T(8,128)}, f32[128,256]{1,0:T(8,128)}, f32[128,256]{1,0:T(8,128)}, f32[256,256]{1,0:T(8,128)}, /*index=5*/f32[256,256]{1,0:T(8,128)}) custom-call(f32[1024,256]{1,0:T(8,128)} %bitcast.16, f32[1024,256]{1,0:T(8,128)} %bitcast.19, f32[1024,256]{1,0:T(8,128)} %bitcast.20), custom_call_target="tpu_custom_call" | custom-call | flops 67108864 | bytes 6291456 | tf_op jit(solution)/shard_map/pallas_call | solution.py:25
  5.2 7.3 %all-to-all-start = ((f32[8,128,128]{2,1,0:T(8,128)}), f32[8,128,128]{2,1,0:T(8,128)S(1)}, u32[]{:S(2)}, u32[]{:S(2)}) async-start(f32[8,128,128]{2,1,0:T(8,128)} %bitcast.3), calls=%async_computation | async-start | bytes 1048576 | tf_op jit(solution)/shard_map/all_to_all | solution.py:608
  12.4 0.0 collective-permute-start.2
  12.4 1.7 %collective-permute-start.3 = (f32[256,256]{1,0:T(8,128)}, f32[256,256]{1,0:T(8,128)S(1)}, u32[]{:S(2)}, u32[]{:S(2)}) collective-permute-start(f32[256,256]{1,0:T(8,128)} %get-tuple-element.25), channel_id=1, source_target_pairs={{8,0},{16,8},{24,16},{0,24},{9,1},{17,9},{25,17},{1,25},{10,2},{18... | collective-permute-start | bytes 786440 | tf_op jit(solution)/shard_map/ppermute | solution.py:616
  14.2 2.0 %collective-permute-start = (f32[128,256]{1,0:T(8,128)}, f32[128,256]{1,0:T(8,128)S(1)}, u32[]{:S(2)}, u32[]{:S(2)}) collective-permute-start(f32[128,256]{1,0:T(8,128)} %get-tuple-element.22), channel_id=1, source_target_pairs={{0,1},{1,2},{2,3},{3,4},{4,5},{5,6},{6,7},{7,0},{8,9},{9,10},{10,1... | collective-permute-start | bytes 393224 | tf_op jit(solution)/shard_map/ppermute | solution.py:612
  16.2 2.7 %collective-permute-start.1 = (f32[128,256]{1,0:T(8,128)}, f32[128,256]{1,0:T(8,128)S(1)}, u32[]{:S(2)}, u32[]{:S(2)}) collective-permute-start(f32[128,256]{1,0:T(8,128)} %get-tuple-element.23), channel_id=1, source_target_pairs={{1,0},{2,1},{3,2},{4,3},{5,4},{6,5},{7,6},{0,7},{9,8},{10,9},{11,1... | collective-permute-start | bytes 393224 | tf_op jit(solution)/shard_map/ppermute | solution.py:616
  18.9 9.2 %shard_map.94 = (f32[1024,256]{1,0:T(8,128)S(1)}, f32[256,256]{1,0:T(8,128)}, f32[256,8]{1,0:T(8,128)}, f32[2,8,16,32,128]{4,3,2,1,0:T(8,128)}) custom-call(f32[1024,256]{1,0:T(8,128)} %bitcast.17, f32[1024,256]{1,0:T(8,128)S(1)} %get-tuple-element.26.slope_ref, f32[32,32]{1,0:T(8,128)} %refs_0_.1, f32[5,32]{1,0:T(8,128)} %refs_1_.1, ...), custom_call_target="tpu_custom_call" | custom-call | flops 402653184 | bytes 33554432 | tf_op jit(solution)/shard_map/pallas_call | solution.py:25
  28.1 0.7 collective-permute-done.refs_0_.ybefore_ref
  28.8 0.0 collective-permute-done.1.refs_1_.yafter_ref
  28.8 0.0 collective-permute-done.2.refs_2_.zbefore_ref
  28.8 0.0 collective-permute-done.3.refs_3_.zafter_ref
  28.8 0.0 all-to-all-done
  28.8 1.2 %shard_map.95 = f32[512,128]{1,0:T(8,128)} custom-call(f32[1024,128]{1,0:T(8,128)S(1)} %bitcast.12, f32[128,256]{1,0:T(8,128)S(1)} %collective-permute-done.refs_0_.ybefore_ref, f32[128,256]{1,0:T(8,128)S(1)} %collective-permute-done.1.refs_1_.yafter_ref, f32[256,256]{1,0:T(8,128)S(1)} %collective-permute-done.2.refs_2_.zbefore_ref, ...), custom_call_target="tpu_custom_call" | custom-call | flops 16777216 | bytes 4194304 | tf_op jit(solution)/shard_map/pallas_call | solution.py:25
  30.1 3.6 %all-to-all-start.1 = ((f32[4,128,128]{2,1,0:T(8,128)}), f32[4,128,128]{2,1,0:T(8,128)S(1)}, u32[]{:S(2)}, u32[]{:S(2)}) async-start(f32[4,128,128]{2,1,0:T(8,128)} %bitcast.5), calls=%async_computation.1 | async-start | bytes 524288 | tf_op jit(solution)/shard_map/all_to_all | solution.py:658
  33.7 3.8 %shard_map.96 = (f32[768,256]{1,0:T(8,128)S(1)}, f32[16,128]{1,0:T(8,128)}) custom-call(f32[128,256]{1,0:T(8,128)S(1)} %collective-permute-done.refs_0_.ybefore_ref, f32[128,256]{1,0:T(8,128)S(1)} %collective-permute-done.1.refs_1_.yafter_ref, f32[256,256]{1,0:T(8,128)S(1)} %collective-permute-done.2.refs_2_.zbefore_ref, ...), custom_call_target="tpu_custom_call" | custom-call | flops 201326592 | bytes 3145728 | tf_op jit(solution)/shard_map/pallas_call | solution.py:25
  37.5 2.0 %all-to-all-done.1 = f32[4,128,128]{2,1,0:T(8,128)S(1)} async-done(((f32[4,128,128]{2,1,0:T(8,128)}), f32[4,128,128]{2,1,0:T(8,128)S(1)}, u32[]{:S(2)}, u32[]{:S(2)}) %all-to-all-start.1) | async-done | bytes 262176 | tf_op jit(solution)/shard_map/all_to_all | solution.py:658
  39.5 5.5 %shard_map.97 = (f32[320,128]{1,0:T(8,128)}, f32[512,128]{1,0:T(8,128)S(1)}) custom-call(f32[512,128]{1,0:T(8,128)S(1)} %bitcast.14, f32[2,8,16,32,128]{4,3,2,1,0:T(8,128)} %get-tuple-element.27.refs_4_.weights_hbm, f32[16,128]{1,0:T(8,128)} %get-tuple-element.30.part_hbm), custom_call_target="tpu_custom_call" | custom-call | flops 8388608 | bytes 6291456 | tf_op jit(solution)/shard_map/pallas_call | solution.py:25
  45.0 3.4 %all-to-all-start.2 = ((f32[4,80,128]{2,1,0:T(8,128)}), f32[4,80,128]{2,1,0:T(8,128)S(1)}, u32[]{:S(2)}, u32[]{:S(2)}) async-start(f32[4,80,128]{2,1,0:T(8,128)} %bitcast.7), calls=%async_computation.2 | async-start | bytes 327680 | tf_op jit(solution)/shard_map/all_to_all | solution.py:703
  48.4 4.0 %shard_map.98.refs_0_ = f32[2,16,8,4,32,32]{5,4,3,2,1,0:T(8,128)} custom-call(f32[512,128]{1,0:T(8,128)S(1)} %get-tuple-element.32.hat_ref), custom_call_target="tpu_custom_call" | custom-call | flops 4194304 | bytes 8388608 | tf_op jit(solution)/shard_map/pallas_call | solution.py:25
  52.3 1.0 %all-to-all-done.2 = f32[4,80,128]{2,1,0:T(8,128)S(1)} async-done(((f32[4,80,128]{2,1,0:T(8,128)}), f32[4,80,128]{2,1,0:T(8,128)S(1)}, u32[]{:S(2)}, u32[]{:S(2)}) %all-to-all-start.2) | async-done | bytes 163872 | tf_op jit(solution)/shard_map/all_to_all | solution.py:703
  53.3 1.3 %shard_map.99 = f32[640,128]{1,0:T(8,128)} custom-call(f32[320,128]{1,0:T(8,128)S(1)} %bitcast.15, f32[2,16,8,4,32,32]{5,4,3,2,1,0:T(8,128)} %shard_map.98.refs_0_), custom_call_target="tpu_custom_call" | custom-call | flops 8388608 | bytes 2097152 | tf_op jit(solution)/shard_map/pallas_call | solution.py:25
  54.6 3.7 %all-to-all-start.3 = ((f32[8,80,128]{2,1,0:T(8,128)}), f32[8,80,128]{2,1,0:T(8,128)S(1)}, u32[]{:S(2)}, u32[]{:S(2)}) async-start(f32[8,80,128]{2,1,0:T(8,128)} %bitcast.9), calls=%async_computation.3 | async-start | bytes 655360 | tf_op jit(solution)/shard_map/all_to_all | solution.py:736
  58.3 4.0 %shard_map.101 = f32[2,16,8,4,32,32]{5,4,3,2,1,0:T(8,128)} custom-call(f32[512,128]{1,0:T(8,128)S(1)} %get-tuple-element.32.hat_ref, f32[2,16,8,4,32,32]{5,4,3,2,1,0:T(8,128)} %shard_map.98.refs_0_), custom_call_target="tpu_custom_call", output_to_operand_aliasing={{}: (1, {})} | custom-call | flops 4194304 | bytes 8388608 | tf_op jit(solution)/shard_map/pallas_call | solution.py:25
  62.2 6.0 %all-to-all-done.3 = f32[8,80,128]{2,1,0:T(8,128)S(1)} async-done(((f32[8,80,128]{2,1,0:T(8,128)}), f32[8,80,128]{2,1,0:T(8,128)S(1)}, u32[]{:S(2)}, u32[]{:S(2)}) %all-to-all-start.3) | async-done | bytes 327712 | tf_op jit(solution)/shard_map/all_to_all | solution.py:736
  68.3 2.4 %shard_map.100 = (f32[1024,256]{1,0:T(8,128)}, f32[32,32]{1,0:T(8,128)}, f32[5,32]{1,0:T(8,128)}) custom-call(f32[640,128]{1,0:T(8,128)S(1)} %bitcast.13, f32[1024,256]{1,0:T(8,128)S(1)} %get-tuple-element.33.local_ref, f32[768,256]{1,0:T(8,128)S(1)} %get-tuple-element.34.fix_ref), custom_call_target="tpu_custom_call" | custom-call | flops 33554432 | bytes 3145728 | tf_op jit(solution)/shard_map/pallas_call | solution.py:25
Async XLA Ops:
  5.2 23.7 %all-to-all-start = ((f32[8,128,128]{2,1,0:T(8,128)}), f32[8,128,128]{2,1,0:T(8,128)S(1)}, u32[]{:S(2)}, u32[]{:S(2)}) async-start(f32[8,128,128]{2,1,0:T(8,128)} %bitcast.3), calls=%async_computation | async-start | bytes 1048576 | tf_op jit(solution)/shard_map/all_to_all | solution.py:608
  12.4 16.4 %collective-permute-start.2 = (f32[256,256]{1,0:T(8,128)}, f32[256,256]{1,0:T(8,128)S(1)}, u32[]{:S(2)}, u32[]{:S(2)}) collective-permute-start(f32[256,256]{1,0:T(8,128)} %get-tuple-element.24), channel_id=1, source_target_pairs={{0,8},{8,16},{16,24},{24,0},{1,9},{9,17},{17,25},{25,1},{2,10},{10... | collective-permute-start | bytes 786440 | tf_op jit(solution)/shard_map/ppermute | solution.py:612
  12.4 16.4 %collective-permute-start.3 = (f32[256,256]{1,0:T(8,128)}, f32[256,256]{1,0:T(8,128)S(1)}, u32[]{:S(2)}, u32[]{:S(2)}) collective-permute-start(f32[256,256]{1,0:T(8,128)} %get-tuple-element.25), channel_id=1, source_target_pairs={{8,0},{16,8},{24,16},{0,24},{9,1},{17,9},{25,17},{1,25},{10,2},{18... | collective-permute-start | bytes 786440 | tf_op jit(solution)/shard_map/ppermute | solution.py:616
  14.2 14.6 %collective-permute-start = (f32[128,256]{1,0:T(8,128)}, f32[128,256]{1,0:T(8,128)S(1)}, u32[]{:S(2)}, u32[]{:S(2)}) collective-permute-start(f32[128,256]{1,0:T(8,128)} %get-tuple-element.22), channel_id=1, source_target_pairs={{0,1},{1,2},{2,3},{3,4},{4,5},{5,6},{6,7},{7,0},{8,9},{9,10},{10,1... | collective-permute-start | bytes 393224 | tf_op jit(solution)/shard_map/ppermute | solution.py:612
  16.2 12.6 %collective-permute-start.1 = (f32[128,256]{1,0:T(8,128)}, f32[128,256]{1,0:T(8,128)S(1)}, u32[]{:S(2)}, u32[]{:S(2)}) collective-permute-start(f32[128,256]{1,0:T(8,128)} %get-tuple-element.23), channel_id=1, source_target_pairs={{1,0},{2,1},{3,2},{4,3},{5,4},{6,5},{7,6},{0,7},{9,8},{10,9},{11,1... | collective-permute-start | bytes 393224 | tf_op jit(solution)/shard_map/ppermute | solution.py:616
  30.1 9.4 %all-to-all-start.1 = ((f32[4,128,128]{2,1,0:T(8,128)}), f32[4,128,128]{2,1,0:T(8,128)S(1)}, u32[]{:S(2)}, u32[]{:S(2)}) async-start(f32[4,128,128]{2,1,0:T(8,128)} %bitcast.5), calls=%async_computation.1 | async-start | bytes 524288 | tf_op jit(solution)/shard_map/all_to_all | solution.py:658
  45.0 8.3 %all-to-all-start.2 = ((f32[4,80,128]{2,1,0:T(8,128)}), f32[4,80,128]{2,1,0:T(8,128)S(1)}, u32[]{:S(2)}, u32[]{:S(2)}) async-start(f32[4,80,128]{2,1,0:T(8,128)} %bitcast.7), calls=%async_computation.2 | async-start | bytes 327680 | tf_op jit(solution)/shard_map/all_to_all | solution.py:703
  54.6 13.6 %all-to-all-start.3 = ((f32[8,80,128]{2,1,0:T(8,128)}), f32[8,80,128]{2,1,0:T(8,128)S(1)}, u32[]{:S(2)}, u32[]{:S(2)}) async-start(f32[8,80,128]{2,1,0:T(8,128)} %bitcast.9), calls=%async_computation.3 | async-start | bytes 655360 | tf_op jit(solution)/shard_map/all_to_all | solution.py:736

commit v3 on v2

--- a/solution.py
+++ b/solution.py
@@ -227,11 +227,11 @@
 
 
 def z_kernel(sizes, recv_ref, weights_hbm, part_hbm, send_ref, hat_ref, weights_ref, part_ref,
-             sems):
+             each_ref, sems):
     C, zl, kxl, kyl, kz, groups, part_rows, scale = sizes
     copies = fetch(
-        [weights_hbm.at[:, k] for k in range(kyl)] + [part_hbm],
-        [weights_ref.at[:, k] for k in range(kyl)] + [part_ref],
+        (part_hbm, weights_hbm.at[0], weights_hbm.at[1]),
+        (part_ref, weights_ref.at[0], weights_ref.at[1]),
         sems,
     )
     forward = table_z(zl * groups, kz, 1, groups).T
@@ -265,21 +265,23 @@
                 hat_ref[pl.ds((f * 2 + r) * kyl + k, kz, stride=4 * kyl), :] = value[
                     r * kz : (r + 1) * kz
                 ]
-        each = spread(slope_hat, C).reshape(2, kz, C, kc)
-        copies[k].wait()
+        each_ref[k] = spread(slope_hat, C).reshape(2, kz, C, kc)
+    for copy in copies:
+        copy.wait()
+    duals = []
+    for k in range(kyl):
         w_re, w_im = weights_ref[0, k], weights_ref[1, k]
-        re = w_re * each[0] + w_im * each[1]
-        im = w_re * each[1] - w_im * each[0]
+        re = w_re * each_ref[k, 0] + w_im * each_ref[k, 1]
+        im = w_re * each_ref[k, 1] - w_im * each_ref[k, 0]
         dual = jnp.stack([re, im]).reshape(2, kz, C // SUB, SUB, kc)
-        dual = jnp.sum(dual, axis=2).reshape(2 * kz * SUB, kc)
-        back = widen(dot(back_table, dual), wide)
-        for g in range(groups):
-            send_ref[pl.ds(g * (chunk + part_rows) + k * rows, rows), :] = back[
-                g * rows : (g + 1) * rows
-            ]
-    copies[kyl].wait()
+        duals.append(jnp.sum(dual, axis=2).reshape(2 * kz * SUB, kc))
+    back = dot(back_table, jnp.concatenate(duals, axis=1))
     for g in range(groups):
-        send_ref[pl.ds(g * (chunk + part_rows) + chunk, part_rows), :] = part_ref[...]
+        start = g * (chunk + part_rows)
+        for k in range(kyl):
+            piece = back[g * rows : (g + 1) * rows, k * kc : (k + 1) * kc]
+            send_ref[pl.ds(start + k * rows, rows), :] = widen(piece, wide)
+        send_ref[pl.ds(start + chunk, part_rows), :] = part_ref[...]
 
 
 def grad_kernel(sizes, first, hat_ref, *refs):
@@ -697,7 +699,8 @@
         scratch=[
             pltpu.VMEM((2, kyl, kz, C, kc), jnp.float32),
             pltpu.VMEM((part_rows, wide), jnp.float32),
-            pltpu.SemaphoreType.DMA((kyl + 1,)),
+            pltpu.VMEM((kyl, 2, kz, C, kc), jnp.float32),
+            pltpu.SemaphoreType.DMA((3,)),
         ],
     )
     returned = exchange(send, "gz")
@@ -719,7 +722,8 @@
             input_output_aliases={1: 0} if before else {},
         )
 
-    grad_half = gradient(0, kz // 2)
+    few = max(1, kz * 5 // 16)
+    grad_half = gradient(0, few)
 
     send = call(
         functools.partial(
@@ -734,7 +738,7 @@
         in_specs=[near, far],
     )
     arrived = exchange(send, "gy")
-    grad_spectral = gradient(kz // 2, kz - kz // 2, grad_half)
+    grad_spectral = gradient(few, kz - few, grad_half)
 
     grad_input, grad_mix, grad_coef = call(
         functools.partial(x_back_kernel, (C, zl, yl, kxl, groups_y, part_rows)),

time: 71.1 us -> 69.9 us (0.983)
  Pallas kernels: 35.9 us -> 34.6 us
    pallas_call x9, Pallas kernels: 35.9 us -> 34.6 us  [call(): pl.pallas_call(body, out_shape=outs, scratch_shapes=list(scratch), compil...]
    all_to_all x1, waiting for transfers between devices: 0.97 us -> 2.09 us  [per_device(): returned = exchange(send, 'gz')]
    all_to_all x1, waiting for transfers between devices: 6.01 us -> 5.02 us  [per_device(): arrived = exchange(send, 'gy')]
where the time goes in v3:
time: 69.9 us; the launch traced here: 69.4 us
  Pallas kernels  34.6 us (49%)
  starting transfers between devices  24.3 us (35%)
  waiting for transfers between devices  9.77 us (14%)
  between operations  0.72 us (1%)
    pallas_call x9, Pallas kernels, call(): pl.pallas_call(body, out_shape=outs, scratch_shapes=list(scratch), compil...  34.6 us
    all_to_all x1, starting transfers between devices, per_device(): lines = exchange(send, 'gy')  7.26 us
    all_to_all x1, waiting for transfers between devices, per_device(): arrived = exchange(send, 'gy')  5.02 us
    ppermute x2, starting transfers between devices, from_above(): lax.ppermute(values, axis, [((i + 1) % size, i) for i in range(size)])  4.44 us
    all_to_all x1, starting transfers between devices, per_device(): arrived = exchange(send, 'gy')  3.65 us
    all_to_all x1, starting transfers between devices, per_device(): owned = exchange(send, 'gz')  3.59 us
    all_to_all x1, starting transfers between devices, per_device(): returned = exchange(send, 'gz')  3.36 us
    all_to_all x1, waiting for transfers between devices, per_device(): returned = exchange(send, 'gz')  2.09 us
  transfers between devices with their start and end apart: 8, of which 4 were waited for; matrix products, arithmetic and copies ran while one was open for 0% of the time, Pallas kernels for 30%

profile of v3, /device:TPU:0, one launch (start us, length us, event | category | flops | bytes accessed | tf_op | source)
XLA Modules:
  0.0 69.4 jit_solution(12233981752797462804)
XLA Ops:
  0.6 4.5 %shard_map.93 = (f32[1024,256]{1,0:T(8,128)S(1)}, f32[1024,128]{1,0:T(8,128)}, f32[128,256]{1,0:T(8,128)}, f32[128,256]{1,0:T(8,128)}, f32[256,256]{1,0:T(8,128)}, /*index=5*/f32[256,256]{1,0:T(8,128)}) custom-call(f32[1024,256]{1,0:T(8,128)} %bitcast.16, f32[1024,256]{1,0:T(8,128)} %bitcast.19, f32[1024,256]{1,0:T(8,128)} %bitcast.20), custom_call_target="tpu_custom_call" | custom-call | flops 67108864 | bytes 6291456 | tf_op jit(solution)/shard_map/pallas_call | solution.py:25
  5.2 7.3 %all-to-all-start = ((f32[8,128,128]{2,1,0:T(8,128)}), f32[8,128,128]{2,1,0:T(8,128)S(1)}, u32[]{:S(2)}, u32[]{:S(2)}) async-start(f32[8,128,128]{2,1,0:T(8,128)} %bitcast.3), calls=%async_computation | async-start | bytes 1048576 | tf_op jit(solution)/shard_map/all_to_all | solution.py:610
  12.4 0.0 collective-permute-start.2
  12.4 1.7 %collective-permute-start.3 = (f32[256,256]{1,0:T(8,128)}, f32[256,256]{1,0:T(8,128)S(1)}, u32[]{:S(2)}, u32[]{:S(2)}) collective-permute-start(f32[256,256]{1,0:T(8,128)} %get-tuple-element.25), channel_id=1, source_target_pairs={{8,0},{16,8},{24,16},{0,24},{9,1},{17,9},{25,17},{1,25},{10,2},{18... | collective-permute-start | bytes 786440 | tf_op jit(solution)/shard_map/ppermute | solution.py:618
  14.2 2.0 %collective-permute-start = (f32[128,256]{1,0:T(8,128)}, f32[128,256]{1,0:T(8,128)S(1)}, u32[]{:S(2)}, u32[]{:S(2)}) collective-permute-start(f32[128,256]{1,0:T(8,128)} %get-tuple-element.22), channel_id=1, source_target_pairs={{0,1},{1,2},{2,3},{3,4},{4,5},{5,6},{6,7},{7,0},{8,9},{9,10},{10,1... | collective-permute-start | bytes 393224 | tf_op jit(solution)/shard_map/ppermute | solution.py:614
  16.2 2.7 %collective-permute-start.1 = (f32[128,256]{1,0:T(8,128)}, f32[128,256]{1,0:T(8,128)S(1)}, u32[]{:S(2)}, u32[]{:S(2)}) collective-permute-start(f32[128,256]{1,0:T(8,128)} %get-tuple-element.23), channel_id=1, source_target_pairs={{1,0},{2,1},{3,2},{4,3},{5,4},{6,5},{7,6},{0,7},{9,8},{10,9},{11,1... | collective-permute-start | bytes 393224 | tf_op jit(solution)/shard_map/ppermute | solution.py:618
  18.9 9.2 %shard_map.94 = (f32[1024,256]{1,0:T(8,128)S(1)}, f32[256,256]{1,0:T(8,128)}, f32[256,8]{1,0:T(8,128)}, f32[2,8,16,32,128]{4,3,2,1,0:T(8,128)}) custom-call(f32[1024,256]{1,0:T(8,128)} %bitcast.17, f32[1024,256]{1,0:T(8,128)S(1)} %get-tuple-element.26.slope_ref, f32[32,32]{1,0:T(8,128)} %refs_0_.1, f32[5,32]{1,0:T(8,128)} %refs_1_.1, ...), custom_call_target="tpu_custom_call" | custom-call | flops 402653184 | bytes 33554432 | tf_op jit(solution)/shard_map/pallas_call | solution.py:25
  28.1 0.7 collective-permute-done.refs_0_.ybefore_ref
  28.8 0.0 collective-permute-done.1.refs_1_.yafter_ref
  28.8 0.0 collective-permute-done.2.refs_2_.zbefore_ref
  28.8 0.0 collective-permute-done.3.refs_3_.zafter_ref
  28.8 0.0 all-to-all-done
  28.8 1.2 %shard_map.95 = f32[512,128]{1,0:T(8,128)} custom-call(f32[1024,128]{1,0:T(8,128)S(1)} %bitcast.12, f32[128,256]{1,0:T(8,128)S(1)} %collective-permute-done.refs_0_.ybefore_ref, f32[128,256]{1,0:T(8,128)S(1)} %collective-permute-done.1.refs_1_.yafter_ref, f32[256,256]{1,0:T(8,128)S(1)} %collective-permute-done.2.refs_2_.zbefore_ref, ...), custom_call_target="tpu_custom_call" | custom-call | flops 16777216 | bytes 4194304 | tf_op jit(solution)/shard_map/pallas_call | solution.py:25
  30.1 3.6 %all-to-all-start.1 = ((f32[4,128,128]{2,1,0:T(8,128)}), f32[4,128,128]{2,1,0:T(8,128)S(1)}, u32[]{:S(2)}, u32[]{:S(2)}) async-start(f32[4,128,128]{2,1,0:T(8,128)} %bitcast.5), calls=%async_computation.1 | async-start | bytes 524288 | tf_op jit(solution)/shard_map/all_to_all | solution.py:660
  33.7 3.8 %shard_map.96 = (f32[768,256]{1,0:T(8,128)S(1)}, f32[16,128]{1,0:T(8,128)}) custom-call(f32[128,256]{1,0:T(8,128)S(1)} %collective-permute-done.refs_0_.ybefore_ref, f32[128,256]{1,0:T(8,128)S(1)} %collective-permute-done.1.refs_1_.yafter_ref, f32[256,256]{1,0:T(8,128)S(1)} %collective-permute-done.2.refs_2_.zbefore_ref, ...), custom_call_target="tpu_custom_call" | custom-call | flops 201326592 | bytes 3145728 | tf_op jit(solution)/shard_map/pallas_call | solution.py:25
  37.5 2.0 %all-to-all-done.1 = f32[4,128,128]{2,1,0:T(8,128)S(1)} async-done(((f32[4,128,128]{2,1,0:T(8,128)}), f32[4,128,128]{2,1,0:T(8,128)S(1)}, u32[]{:S(2)}, u32[]{:S(2)}) %all-to-all-start.1) | async-done | bytes 262176 | tf_op jit(solution)/shard_map/all_to_all | solution.py:660
  39.5 4.5 %shard_map.97 = (f32[320,128]{1,0:T(8,128)}, f32[512,128]{1,0:T(8,128)S(1)}) custom-call(f32[512,128]{1,0:T(8,128)S(1)} %bitcast.14, f32[2,8,16,32,128]{4,3,2,1,0:T(8,128)} %get-tuple-element.27.refs_4_.weights_hbm, f32[16,128]{1,0:T(8,128)} %get-tuple-element.30.part_hbm), custom_call_target="tpu_custom_call" | custom-call | flops 8388608 | bytes 6291456 | tf_op jit(solution)/shard_map/pallas_call | solution.py:25
  43.9 3.4 %all-to-all-start.2 = ((f32[4,80,128]{2,1,0:T(8,128)}), f32[4,80,128]{2,1,0:T(8,128)S(1)}, u32[]{:S(2)}, u32[]{:S(2)}) async-start(f32[4,80,128]{2,1,0:T(8,128)} %bitcast.7), calls=%async_computation.2 | async-start | bytes 327680 | tf_op jit(solution)/shard_map/all_to_all | solution.py:706
  47.3 2.8 %shard_map.98.refs_0_ = f32[2,16,8,4,32,32]{5,4,3,2,1,0:T(8,128)} custom-call(f32[512,128]{1,0:T(8,128)S(1)} %get-tuple-element.32.hat_ref), custom_call_target="tpu_custom_call" | custom-call | flops 2621440 | bytes 5242880 | tf_op jit(solution)/shard_map/pallas_call | solution.py:25
  50.2 2.1 %all-to-all-done.2 = f32[4,80,128]{2,1,0:T(8,128)S(1)} async-done(((f32[4,80,128]{2,1,0:T(8,128)}), f32[4,80,128]{2,1,0:T(8,128)S(1)}, u32[]{:S(2)}, u32[]{:S(2)}) %all-to-all-start.2) | async-done | bytes 163872 | tf_op jit(solution)/shard_map/all_to_all | solution.py:706
  52.3 1.3 %shard_map.99 = f32[640,128]{1,0:T(8,128)} custom-call(f32[320,128]{1,0:T(8,128)S(1)} %bitcast.15, f32[2,16,8,4,32,32]{5,4,3,2,1,0:T(8,128)} %shard_map.98.refs_0_), custom_call_target="tpu_custom_call" | custom-call | flops 8388608 | bytes 2097152 | tf_op jit(solution)/shard_map/pallas_call | solution.py:25
  53.6 3.7 %all-to-all-start.3 = ((f32[8,80,128]{2,1,0:T(8,128)}), f32[8,80,128]{2,1,0:T(8,128)S(1)}, u32[]{:S(2)}, u32[]{:S(2)}) async-start(f32[8,80,128]{2,1,0:T(8,128)} %bitcast.9), calls=%async_computation.3 | async-start | bytes 655360 | tf_op jit(solution)/shard_map/all_to_all | solution.py:740
  57.2 4.8 %shard_map.101 = f32[2,16,8,4,32,32]{5,4,3,2,1,0:T(8,128)} custom-call(f32[512,128]{1,0:T(8,128)S(1)} %get-tuple-element.32.hat_ref, f32[2,16,8,4,32,32]{5,4,3,2,1,0:T(8,128)} %shard_map.98.refs_0_), custom_call_target="tpu_custom_call", output_to_operand_aliasing={{}: (1, {})} | custom-call | flops 5767168 | bytes 11534336 | tf_op jit(solution)/shard_map/pallas_call | solution.py:25
  62.0 5.0 %all-to-all-done.3 = f32[8,80,128]{2,1,0:T(8,128)S(1)} async-done(((f32[8,80,128]{2,1,0:T(8,128)}), f32[8,80,128]{2,1,0:T(8,128)S(1)}, u32[]{:S(2)}, u32[]{:S(2)}) %all-to-all-start.3) | async-done | bytes 327712 | tf_op jit(solution)/shard_map/all_to_all | solution.py:740
  67.0 2.4 %shard_map.100 = (f32[1024,256]{1,0:T(8,128)}, f32[32,32]{1,0:T(8,128)}, f32[5,32]{1,0:T(8,128)}) custom-call(f32[640,128]{1,0:T(8,128)S(1)} %bitcast.13, f32[1024,256]{1,0:T(8,128)S(1)} %get-tuple-element.33.local_ref, f32[768,256]{1,0:T(8,128)S(1)} %get-tuple-element.34.fix_ref), custom_call_target="tpu_custom_call" | custom-call | flops 33554432 | bytes 3145728 | tf_op jit(solution)/shard_map/pallas_call | solution.py:25
Async XLA Ops:
  5.2 23.7 %all-to-all-start = ((f32[8,128,128]{2,1,0:T(8,128)}), f32[8,128,128]{2,1,0:T(8,128)S(1)}, u32[]{:S(2)}, u32[]{:S(2)}) async-start(f32[8,128,128]{2,1,0:T(8,128)} %bitcast.3), calls=%async_computation | async-start | bytes 1048576 | tf_op jit(solution)/shard_map/all_to_all | solution.py:610
  12.4 16.4 %collective-permute-start.2 = (f32[256,256]{1,0:T(8,128)}, f32[256,256]{1,0:T(8,128)S(1)}, u32[]{:S(2)}, u32[]{:S(2)}) collective-permute-start(f32[256,256]{1,0:T(8,128)} %get-tuple-element.24), channel_id=1, source_target_pairs={{0,8},{8,16},{16,24},{24,0},{1,9},{9,17},{17,25},{25,1},{2,10},{10... | collective-permute-start | bytes 786440 | tf_op jit(solution)/shard_map/ppermute | solution.py:614
  12.4 16.4 %collective-permute-start.3 = (f32[256,256]{1,0:T(8,128)}, f32[256,256]{1,0:T(8,128)S(1)}, u32[]{:S(2)}, u32[]{:S(2)}) collective-permute-start(f32[256,256]{1,0:T(8,128)} %get-tuple-element.25), channel_id=1, source_target_pairs={{8,0},{16,8},{24,16},{0,24},{9,1},{17,9},{25,17},{1,25},{10,2},{18... | collective-permute-start | bytes 786440 | tf_op jit(solution)/shard_map/ppermute | solution.py:618
  14.2 14.6 %collective-permute-start = (f32[128,256]{1,0:T(8,128)}, f32[128,256]{1,0:T(8,128)S(1)}, u32[]{:S(2)}, u32[]{:S(2)}) collective-permute-start(f32[128,256]{1,0:T(8,128)} %get-tuple-element.22), channel_id=1, source_target_pairs={{0,1},{1,2},{2,3},{3,4},{4,5},{5,6},{6,7},{7,0},{8,9},{9,10},{10,1... | collective-permute-start | bytes 393224 | tf_op jit(solution)/shard_map/ppermute | solution.py:614
  16.2 12.6 %collective-permute-start.1 = (f32[128,256]{1,0:T(8,128)}, f32[128,256]{1,0:T(8,128)S(1)}, u32[]{:S(2)}, u32[]{:S(2)}) collective-permute-start(f32[128,256]{1,0:T(8,128)} %get-tuple-element.23), channel_id=1, source_target_pairs={{1,0},{2,1},{3,2},{4,3},{5,4},{6,5},{7,6},{0,7},{9,8},{10,9},{11,1... | collective-permute-start | bytes 393224 | tf_op jit(solution)/shard_map/ppermute | solution.py:618
  30.1 9.4 %all-to-all-start.1 = ((f32[4,128,128]{2,1,0:T(8,128)}), f32[4,128,128]{2,1,0:T(8,128)S(1)}, u32[]{:S(2)}, u32[]{:S(2)}) async-start(f32[4,128,128]{2,1,0:T(8,128)} %bitcast.5), calls=%async_computation.1 | async-start | bytes 524288 | tf_op jit(solution)/shard_map/all_to_all | solution.py:660
  43.9 8.3 %all-to-all-start.2 = ((f32[4,80,128]{2,1,0:T(8,128)}), f32[4,80,128]{2,1,0:T(8,128)S(1)}, u32[]{:S(2)}, u32[]{:S(2)}) async-start(f32[4,80,128]{2,1,0:T(8,128)} %bitcast.7), calls=%async_computation.2 | async-start | bytes 327680 | tf_op jit(solution)/shard_map/all_to_all | solution.py:706
  53.6 13.5 %all-to-all-start.3 = ((f32[8,80,128]{2,1,0:T(8,128)}), f32[8,80,128]{2,1,0:T(8,128)S(1)}, u32[]{:S(2)}, u32[]{:S(2)}) async-start(f32[8,80,128]{2,1,0:T(8,128)} %bitcast.9), calls=%async_computation.3 | async-start | bytes 655360 | tf_op jit(solution)/shard_map/all_to_all | solution.py:740

commit v4 on v3

--- a/solution.py
+++ b/solution.py
@@ -419,7 +419,7 @@
 
 
 def inner_kernel(sizes, in_hbm, slope_ref, mix_hbm, coefs_hbm, weights_hbm, out_ref, gram_ref,
-                 sums_ref, packed_ref, in_ref, mix_ref, coefs_ref, raw_ref, sems):
+                 sums_ref, kron_ref, packed_ref, in_ref, mix_ref, coefs_ref, raw_ref, sems):
     C, zl, yl, kxl, kyl, kz = sizes
     length = in_ref.shape[1]
     copies = fetch((mix_hbm, coefs_hbm, in_hbm), (mix_ref, coefs_ref, in_ref), sems)
@@ -452,6 +452,7 @@
     coef_rows = dot(tall, coefs_ref[...], ((1,), (1,)), EXACT)
     coef = [coef_rows[:, j : j + 1] for j in range(5)]
     kron = mixer(mix_ref[...], C, yl, True)
+    kron_ref[...] = kron
     slopes = [layer(slope_ref, z, C, zl, yl) for z in range(zl)]
     hidden = [dot(kron, slopes[z]) for z in range(zl)]
     copies[2].wait()
@@ -500,8 +501,9 @@
 
 def edge_kernel(sizes, ybefore_ref, yafter_ref, zbefore_ref, zafter_ref, *refs):
     C, zl, yl, kxl = sizes
-    *hbms, fix_ref, part_ref, mix_ref, coefs_ref, in_ref, gram_ref, sums_ref, sems = refs
-    copies = fetch(hbms, (mix_ref, coefs_ref, in_ref, gram_ref, sums_ref), sems)
+    hbms, (fix_ref, part_ref), refs, sems = refs[:6], refs[6:8], refs[8:-1], refs[-1]
+    copies = fetch(hbms, refs, sems)
+    mix_ref, coefs_ref, kron_ref, in_ref, gram_ref, sums_ref = refs
 
     def inside(ref, axis, place):
         return ref[...] * (lax.axis_index(axis) != place).astype(jnp.float32)
@@ -509,14 +511,12 @@
     last_y, last_z = lax.axis_size("gy") - 1, lax.axis_size("gz") - 1
     zbefore, zafter = inside(zbefore_ref, "gz", 0), inside(zafter_ref, "gz", last_z)
     ybefore, yafter = inside(ybefore_ref, "gy", 0), inside(yafter_ref, "gy", last_y)
-    copies[0].wait()
-    copies[1].wait()
-    kron_y = mixer(mix_ref[...], C, yl, True)
+    for copy in copies:
+        copy.wait()
+    kron_y = kron_ref[...]
     kron_z = mixer(mix_ref[...], C, zl, False)
     hidden_zb, hidden_za = dot(kron_y, zbefore), dot(kron_y, zafter)
     hidden_yb, hidden_ya = dot(kron_z, ybefore), dot(kron_z, yafter)
-    for copy in copies[2:]:
-        copy.wait()
     length = in_ref.shape[1]
     first, last = layer(in_ref, 0, C, zl, yl), layer(in_ref, zl - 1, C, zl, yl)
     layers = [layer(in_ref, z, C, zl, yl) for z in range(zl)]
@@ -620,12 +620,13 @@
     ybefore, yafter = from_below(ylast, "gy"), from_above(yfirst, "gy")
     zbefore, zafter = from_below(zlast, "gz"), from_above(zfirst, "gz")
 
-    local, gram, sums, weights = call(
+    local, gram, sums, kron, weights = call(
         functools.partial(inner_kernel, (C, zl, yl, kxl, kyl, kz)),
         (
             vmem(rows, length),
             far_out(C * yl, C * yl),
             far_out(C * yl, SUB),
+            far_out(C * yl, C * yl),
             far_out(2, kyl, kz, C, kc),
         ),
         (
@@ -669,6 +670,7 @@
             held(zafter),
             hbm(mix_weights),
             hbm(coefficients),
+            hbm(kron),
             hbm(flat(input_field)),
             hbm(gram),
             hbm(sums),
@@ -676,14 +678,15 @@
         24,
         flops=2 * 6 * (C * yl) ** 2 * length,
         bytes_accessed=3 * MIB,
-        in_specs=[near] * 4 + [far] * 5,
+        in_specs=[near] * 4 + [far] * 6,
         scratch=[
             pltpu.VMEM((C, C), jnp.float32),
             pltpu.VMEM(coefficients.shape, jnp.float32),
+            pltpu.VMEM(kron.shape, jnp.float32),
             pltpu.VMEM((rows, length), jnp.float32),
             pltpu.VMEM(gram.shape, jnp.float32),
             pltpu.VMEM(sums.shape, jnp.float32),
-            pltpu.SemaphoreType.DMA((5,)),
+            pltpu.SemaphoreType.DMA((6,)),
         ],
     )
 

time: 69.9 us -> 69.9 us (level)
  no operation moved by 1% of the time
where the time goes in v4:
time: 69.9 us; the launch traced here: 69.4 us
  Pallas kernels  34.8 us (50%)
  starting transfers between devices  24.3 us (35%)
  waiting for transfers between devices  9.52 us (14%)
  between operations  0.72 us (1%)
    pallas_call x9, Pallas kernels, call(): pl.pallas_call(body, out_shape=outs, scratch_shapes=list(scratch), compil...  34.8 us
    all_to_all x1, starting transfers between devices, per_device(): lines = exchange(send, 'gy')  7.26 us
    all_to_all x1, waiting for transfers between devices, per_device(): arrived = exchange(send, 'gy')  5.02 us
    ppermute x2, starting transfers between devices, from_above(): lax.ppermute(values, axis, [((i + 1) % size, i) for i in range(size)])  4.44 us
    all_to_all x1, starting transfers between devices, per_device(): arrived = exchange(send, 'gy')  3.65 us
    all_to_all x1, starting transfers between devices, per_device(): owned = exchange(send, 'gz')  3.59 us
    all_to_all x1, starting transfers between devices, per_device(): returned = exchange(send, 'gz')  3.36 us
    all_to_all x1, waiting for transfers between devices, per_device(): returned = exchange(send, 'gz')  2.09 us
  transfers between devices with their start and end apart: 8, of which 4 were waited for; matrix products, arithmetic and copies ran while one was open for 0% of the time, Pallas kernels for 30%

profile of v4, /device:TPU:0, one launch (start us, length us, event | category | flops | bytes accessed | tf_op | source)
XLA Modules:
  0.0 69.4 jit_solution(6368889080640453553)
XLA Ops:
  0.6 4.5 %shard_map.93 = (f32[1024,256]{1,0:T(8,128)S(1)}, f32[1024,128]{1,0:T(8,128)}, f32[128,256]{1,0:T(8,128)}, f32[128,256]{1,0:T(8,128)}, f32[256,256]{1,0:T(8,128)}, /*index=5*/f32[256,256]{1,0:T(8,128)}) custom-call(f32[1024,256]{1,0:T(8,128)} %bitcast.16, f32[1024,256]{1,0:T(8,128)} %bitcast.19, f32[1024,256]{1,0:T(8,128)} %bitcast.20), custom_call_target="tpu_custom_call" | custom-call | flops 67108864 | bytes 6291456 | tf_op jit(solution)/shard_map/pallas_call | solution.py:25
  5.2 7.3 %all-to-all-start = ((f32[8,128,128]{2,1,0:T(8,128)}), f32[8,128,128]{2,1,0:T(8,128)S(1)}, u32[]{:S(2)}, u32[]{:S(2)}) async-start(f32[8,128,128]{2,1,0:T(8,128)} %bitcast.3), calls=%async_computation | async-start | bytes 1048576 | tf_op jit(solution)/shard_map/all_to_all | solution.py:610
  12.4 0.0 collective-permute-start.2
  12.4 1.7 %collective-permute-start.3 = (f32[256,256]{1,0:T(8,128)}, f32[256,256]{1,0:T(8,128)S(1)}, u32[]{:S(2)}, u32[]{:S(2)}) collective-permute-start(f32[256,256]{1,0:T(8,128)} %get-tuple-element.26), channel_id=1, source_target_pairs={{8,0},{16,8},{24,16},{0,24},{9,1},{17,9},{25,17},{1,25},{10,2},{18... | collective-permute-start | bytes 786440 | tf_op jit(solution)/shard_map/ppermute | solution.py:618
  14.2 2.0 %collective-permute-start = (f32[128,256]{1,0:T(8,128)}, f32[128,256]{1,0:T(8,128)S(1)}, u32[]{:S(2)}, u32[]{:S(2)}) collective-permute-start(f32[128,256]{1,0:T(8,128)} %get-tuple-element.23), channel_id=1, source_target_pairs={{0,1},{1,2},{2,3},{3,4},{4,5},{5,6},{6,7},{7,0},{8,9},{9,10},{10,1... | collective-permute-start | bytes 393224 | tf_op jit(solution)/shard_map/ppermute | solution.py:614
  16.2 2.7 %collective-permute-start.1 = (f32[128,256]{1,0:T(8,128)}, f32[128,256]{1,0:T(8,128)S(1)}, u32[]{:S(2)}, u32[]{:S(2)}) collective-permute-start(f32[128,256]{1,0:T(8,128)} %get-tuple-element.24), channel_id=1, source_target_pairs={{1,0},{2,1},{3,2},{4,3},{5,4},{6,5},{7,6},{0,7},{9,8},{10,9},{11,1... | collective-permute-start | bytes 393224 | tf_op jit(solution)/shard_map/ppermute | solution.py:618
  18.9 9.2 %shard_map.94 = (f32[1024,256]{1,0:T(8,128)S(1)}, f32[256,256]{1,0:T(8,128)}, f32[256,8]{1,0:T(8,128)}, f32[256,256]{1,0:T(8,128)}, f32[2,8,16,32,128]{4,3,2,1,0:T(8,128)}) custom-call(f32[1024,256]{1,0:T(8,128)} %bitcast.17, f32[1024,256]{1,0:T(8,128)S(1)} %get-tuple-element.27.slope_ref, f32[32,32]{1,0:T(8,128)} %refs_0_.1, f32[5,32]{1,0:T(8,128)} %refs_1_.1, ...), custom_call_target="tpu_custom_call" | custom-call | flops 402653184 | bytes 33554432 | tf_op jit(solution)/shard_map/pallas_call | solution.py:25
  28.1 0.7 collective-permute-done.refs_0_.ybefore_ref
  28.8 0.0 collective-permute-done.1.refs_1_.yafter_ref
  28.8 0.0 collective-permute-done.2.refs_2_.zbefore_ref
  28.8 0.0 collective-permute-done.3.refs_3_.zafter_ref
  28.8 0.0 all-to-all-done
  28.8 1.2 %shard_map.95 = f32[512,128]{1,0:T(8,128)} custom-call(f32[1024,128]{1,0:T(8,128)S(1)} %bitcast.12, f32[128,256]{1,0:T(8,128)S(1)} %collective-permute-done.refs_0_.ybefore_ref, f32[128,256]{1,0:T(8,128)S(1)} %collective-permute-done.1.refs_1_.yafter_ref, f32[256,256]{1,0:T(8,128)S(1)} %collective-permute-done.2.refs_2_.zbefore_ref, ...), custom_call_target="tpu_custom_call" | custom-call | flops 16777216 | bytes 4194304 | tf_op jit(solution)/shard_map/pallas_call | solution.py:25
  30.1 3.6 %all-to-all-start.1 = ((f32[4,128,128]{2,1,0:T(8,128)}), f32[4,128,128]{2,1,0:T(8,128)S(1)}, u32[]{:S(2)}, u32[]{:S(2)}) async-start(f32[4,128,128]{2,1,0:T(8,128)} %bitcast.5), calls=%async_computation.1 | async-start | bytes 524288 | tf_op jit(solution)/shard_map/all_to_all | solution.py:661
  33.7 4.1 %shard_map.96 = (f32[768,256]{1,0:T(8,128)S(1)}, f32[16,128]{1,0:T(8,128)}) custom-call(f32[128,256]{1,0:T(8,128)S(1)} %collective-permute-done.refs_0_.ybefore_ref, f32[128,256]{1,0:T(8,128)S(1)} %collective-permute-done.1.refs_1_.yafter_ref, f32[256,256]{1,0:T(8,128)S(1)} %collective-permute-done.2.refs_2_.zbefore_ref, ...), custom_call_target="tpu_custom_call" | custom-call | flops 201326592 | bytes 3145728 | tf_op jit(solution)/shard_map/pallas_call | solution.py:25
  37.8 1.7 %all-to-all-done.1 = f32[4,128,128]{2,1,0:T(8,128)S(1)} async-done(((f32[4,128,128]{2,1,0:T(8,128)}), f32[4,128,128]{2,1,0:T(8,128)S(1)}, u32[]{:S(2)}, u32[]{:S(2)}) %all-to-all-start.1) | async-done | bytes 262176 | tf_op jit(solution)/shard_map/all_to_all | solution.py:661
  39.5 4.5 %shard_map.97 = (f32[320,128]{1,0:T(8,128)}, f32[512,128]{1,0:T(8,128)S(1)}) custom-call(f32[512,128]{1,0:T(8,128)S(1)} %bitcast.14, f32[2,8,16,32,128]{4,3,2,1,0:T(8,128)} %get-tuple-element.28.refs_4_.weights_hbm, f32[16,128]{1,0:T(8,128)} %get-tuple-element.32.part_hbm), custom_call_target="tpu_custom_call" | custom-call | flops 8388608 | bytes 6291456 | tf_op jit(solution)/shard_map/pallas_call | solution.py:25
  43.9 3.4 %all-to-all-start.2 = ((f32[4,80,128]{2,1,0:T(8,128)}), f32[4,80,128]{2,1,0:T(8,128)S(1)}, u32[]{:S(2)}, u32[]{:S(2)}) async-start(f32[4,80,128]{2,1,0:T(8,128)} %bitcast.7), calls=%async_computation.2 | async-start | bytes 327680 | tf_op jit(solution)/shard_map/all_to_all | solution.py:709
  47.3 2.8 %shard_map.98.refs_0_ = f32[2,16,8,4,32,32]{5,4,3,2,1,0:T(8,128)} custom-call(f32[512,128]{1,0:T(8,128)S(1)} %get-tuple-element.34.hat_ref), custom_call_target="tpu_custom_call" | custom-call | flops 2621440 | bytes 5242880 | tf_op jit(solution)/shard_map/pallas_call | solution.py:25
  50.2 2.1 %all-to-all-done.2 = f32[4,80,128]{2,1,0:T(8,128)S(1)} async-done(((f32[4,80,128]{2,1,0:T(8,128)}), f32[4,80,128]{2,1,0:T(8,128)S(1)}, u32[]{:S(2)}, u32[]{:S(2)}) %all-to-all-start.2) | async-done | bytes 163872 | tf_op jit(solution)/shard_map/all_to_all | solution.py:709
  52.3 1.3 %shard_map.99 = f32[640,128]{1,0:T(8,128)} custom-call(f32[320,128]{1,0:T(8,128)S(1)} %bitcast.15, f32[2,16,8,4,32,32]{5,4,3,2,1,0:T(8,128)} %shard_map.98.refs_0_), custom_call_target="tpu_custom_call" | custom-call | flops 8388608 | bytes 2097152 | tf_op jit(solution)/shard_map/pallas_call | solution.py:25
  53.6 3.7 %all-to-all-start.3 = ((f32[8,80,128]{2,1,0:T(8,128)}), f32[8,80,128]{2,1,0:T(8,128)S(1)}, u32[]{:S(2)}, u32[]{:S(2)}) async-start(f32[8,80,128]{2,1,0:T(8,128)} %bitcast.9), calls=%async_computation.3 | async-start | bytes 655360 | tf_op jit(solution)/shard_map/all_to_all | solution.py:743
  57.2 4.8 %shard_map.101 = f32[2,16,8,4,32,32]{5,4,3,2,1,0:T(8,128)} custom-call(f32[512,128]{1,0:T(8,128)S(1)} %get-tuple-element.34.hat_ref, f32[2,16,8,4,32,32]{5,4,3,2,1,0:T(8,128)} %shard_map.98.refs_0_), custom_call_target="tpu_custom_call", output_to_operand_aliasing={{}: (1, {})} | custom-call | flops 5767168 | bytes 11534336 | tf_op jit(solution)/shard_map/pallas_call | solution.py:25
  62.0 5.0 %all-to-all-done.3 = f32[8,80,128]{2,1,0:T(8,128)S(1)} async-done(((f32[8,80,128]{2,1,0:T(8,128)}), f32[8,80,128]{2,1,0:T(8,128)S(1)}, u32[]{:S(2)}, u32[]{:S(2)}) %all-to-all-start.3) | async-done | bytes 327712 | tf_op jit(solution)/shard_map/all_to_all | solution.py:743
  67.0 2.4 %shard_map.100 = (f32[1024,256]{1,0:T(8,128)}, f32[32,32]{1,0:T(8,128)}, f32[5,32]{1,0:T(8,128)}) custom-call(f32[640,128]{1,0:T(8,128)S(1)} %bitcast.13, f32[1024,256]{1,0:T(8,128)S(1)} %get-tuple-element.35.local_ref, f32[768,256]{1,0:T(8,128)S(1)} %get-tuple-element.36.fix_ref), custom_call_target="tpu_custom_call" | custom-call | flops 33554432 | bytes 3145728 | tf_op jit(solution)/shard_map/pallas_call | solution.py:25
Async XLA Ops:
  5.2 23.7 %all-to-all-start = ((f32[8,128,128]{2,1,0:T(8,128)}), f32[8,128,128]{2,1,0:T(8,128)S(1)}, u32[]{:S(2)}, u32[]{:S(2)}) async-start(f32[8,128,128]{2,1,0:T(8,128)} %bitcast.3), calls=%async_computation | async-start | bytes 1048576 | tf_op jit(solution)/shard_map/all_to_all | solution.py:610
  12.4 16.4 %collective-permute-start.2 = (f32[256,256]{1,0:T(8,128)}, f32[256,256]{1,0:T(8,128)S(1)}, u32[]{:S(2)}, u32[]{:S(2)}) collective-permute-start(f32[256,256]{1,0:T(8,128)} %get-tuple-element.25), channel_id=1, source_target_pairs={{0,8},{8,16},{16,24},{24,0},{1,9},{9,17},{17,25},{25,1},{2,10},{10... | collective-permute-start | bytes 786440 | tf_op jit(solution)/shard_map/ppermute | solution.py:614
  12.4 16.4 %collective-permute-start.3 = (f32[256,256]{1,0:T(8,128)}, f32[256,256]{1,0:T(8,128)S(1)}, u32[]{:S(2)}, u32[]{:S(2)}) collective-permute-start(f32[256,256]{1,0:T(8,128)} %get-tuple-element.26), channel_id=1, source_target_pairs={{8,0},{16,8},{24,16},{0,24},{9,1},{17,9},{25,17},{1,25},{10,2},{18... | collective-permute-start | bytes 786440 | tf_op jit(solution)/shard_map/ppermute | solution.py:618
  14.2 14.6 %collective-permute-start = (f32[128,256]{1,0:T(8,128)}, f32[128,256]{1,0:T(8,128)S(1)}, u32[]{:S(2)}, u32[]{:S(2)}) collective-permute-start(f32[128,256]{1,0:T(8,128)} %get-tuple-element.23), channel_id=1, source_target_pairs={{0,1},{1,2},{2,3},{3,4},{4,5},{5,6},{6,7},{7,0},{8,9},{9,10},{10,1... | collective-permute-start | bytes 393224 | tf_op jit(solution)/shard_map/ppermute | solution.py:614
  16.2 12.6 %collective-permute-start.1 = (f32[128,256]{1,0:T(8,128)}, f32[128,256]{1,0:T(8,128)S(1)}, u32[]{:S(2)}, u32[]{:S(2)}) collective-permute-start(f32[128,256]{1,0:T(8,128)} %get-tuple-element.24), channel_id=1, source_target_pairs={{1,0},{2,1},{3,2},{4,3},{5,4},{6,5},{7,6},{0,7},{9,8},{10,9},{11,1... | collective-permute-start | bytes 393224 | tf_op jit(solution)/shard_map/ppermute | solution.py:618
  30.1 9.4 %all-to-all-start.1 = ((f32[4,128,128]{2,1,0:T(8,128)}), f32[4,128,128]{2,1,0:T(8,128)S(1)}, u32[]{:S(2)}, u32[]{:S(2)}) async-start(f32[4,128,128]{2,1,0:T(8,128)} %bitcast.5), calls=%async_computation.1 | async-start | bytes 524288 | tf_op jit(solution)/shard_map/all_to_all | solution.py:661
  43.9 8.3 %all-to-all-start.2 = ((f32[4,80,128]{2,1,0:T(8,128)}), f32[4,80,128]{2,1,0:T(8,128)S(1)}, u32[]{:S(2)}, u32[]{:S(2)}) async-start(f32[4,80,128]{2,1,0:T(8,128)} %bitcast.7), calls=%async_computation.2 | async-start | bytes 327680 | tf_op jit(solution)/shard_map/all_to_all | solution.py:709
  53.6 13.5 %all-to-all-start.3 = ((f32[8,80,128]{2,1,0:T(8,128)}), f32[8,80,128]{2,1,0:T(8,128)S(1)}, u32[]{:S(2)}, u32[]{:S(2)}) async-start(f32[8,80,128]{2,1,0:T(8,128)} %bitcast.9), calls=%async_computation.3 | async-start | bytes 655360 | tf_op jit(solution)/shard_map/all_to_all | solution.py:743

commit v5 on v4

--- a/solution.py
+++ b/solution.py
@@ -725,7 +725,7 @@
             input_output_aliases={1: 0} if before else {},
         )
 
-    few = max(1, kz * 5 // 16)
+    few = max(1, kz * 3 // 16)
     grad_half = gradient(0, few)
 
     send = call(

time: 69.9 us -> 69.9 us (level)
    all_to_all x1, waiting for transfers between devices: 2.09 us -> 2.8 us  [per_device(): returned = exchange(send, 'gz')]
where the time goes in v5:
time: 69.9 us; the launch traced here: 69.4 us
  Pallas kernels  34.8 us (50%)
  starting transfers between devices  24.3 us (35%)
  waiting for transfers between devices  9.57 us (14%)
  between operations  0.72 us (1%)
    pallas_call x9, Pallas kernels, call(): pl.pallas_call(body, out_shape=outs, scratch_shapes=list(scratch), compil...  34.8 us
    all_to_all x1, starting transfers between devices, per_device(): lines = exchange(send, 'gy')  7.26 us
    ppermute x2, starting transfers between devices, from_above(): lax.ppermute(values, axis, [((i + 1) % size, i) for i in range(size)])  4.44 us
    all_to_all x1, waiting for transfers between devices, per_device(): arrived = exchange(send, 'gy')  4.37 us
    all_to_all x1, starting transfers between devices, per_device(): arrived = exchange(send, 'gy')  3.65 us
    all_to_all x1, starting transfers between devices, per_device(): owned = exchange(send, 'gz')  3.59 us
    all_to_all x1, starting transfers between devices, per_device(): returned = exchange(send, 'gz')  3.36 us
    all_to_all x1, waiting for transfers between devices, per_device(): returned = exchange(send, 'gz')  2.8 us
  transfers between devices with their start and end apart: 8, of which 4 were waited for; matrix products, arithmetic and copies ran while one was open for 0% of the time, Pallas kernels for 30%

profile of v5, /device:TPU:0, one launch (start us, length us, event | category | flops | bytes accessed | tf_op | source)
XLA Modules:
  0.0 69.4 jit_solution(6526212877597787578)
XLA Ops:
  0.6 4.5 %shard_map.93 = (f32[1024,256]{1,0:T(8,128)S(1)}, f32[1024,128]{1,0:T(8,128)}, f32[128,256]{1,0:T(8,128)}, f32[128,256]{1,0:T(8,128)}, f32[256,256]{1,0:T(8,128)}, /*index=5*/f32[256,256]{1,0:T(8,128)}) custom-call(f32[1024,256]{1,0:T(8,128)} %bitcast.16, f32[1024,256]{1,0:T(8,128)} %bitcast.19, f32[1024,256]{1,0:T(8,128)} %bitcast.20), custom_call_target="tpu_custom_call" | custom-call | flops 67108864 | bytes 6291456 | tf_op jit(solution)/shard_map/pallas_call | solution.py:25
  5.2 7.3 %all-to-all-start = ((f32[8,128,128]{2,1,0:T(8,128)}), f32[8,128,128]{2,1,0:T(8,128)S(1)}, u32[]{:S(2)}, u32[]{:S(2)}) async-start(f32[8,128,128]{2,1,0:T(8,128)} %bitcast.3), calls=%async_computation | async-start | bytes 1048576 | tf_op jit(solution)/shard_map/all_to_all | solution.py:610
  12.4 0.0 collective-permute-start.2
  12.4 1.7 %collective-permute-start.3 = (f32[256,256]{1,0:T(8,128)}, f32[256,256]{1,0:T(8,128)S(1)}, u32[]{:S(2)}, u32[]{:S(2)}) collective-permute-start(f32[256,256]{1,0:T(8,128)} %get-tuple-element.26), channel_id=1, source_target_pairs={{8,0},{16,8},{24,16},{0,24},{9,1},{17,9},{25,17},{1,25},{10,2},{18... | collective-permute-start | bytes 786440 | tf_op jit(solution)/shard_map/ppermute | solution.py:618
  14.2 2.0 %collective-permute-start = (f32[128,256]{1,0:T(8,128)}, f32[128,256]{1,0:T(8,128)S(1)}, u32[]{:S(2)}, u32[]{:S(2)}) collective-permute-start(f32[128,256]{1,0:T(8,128)} %get-tuple-element.23), channel_id=1, source_target_pairs={{0,1},{1,2},{2,3},{3,4},{4,5},{5,6},{6,7},{7,0},{8,9},{9,10},{10,1... | collective-permute-start | bytes 393224 | tf_op jit(solution)/shard_map/ppermute | solution.py:614
  16.2 2.7 %collective-permute-start.1 = (f32[128,256]{1,0:T(8,128)}, f32[128,256]{1,0:T(8,128)S(1)}, u32[]{:S(2)}, u32[]{:S(2)}) collective-permute-start(f32[128,256]{1,0:T(8,128)} %get-tuple-element.24), channel_id=1, source_target_pairs={{1,0},{2,1},{3,2},{4,3},{5,4},{6,5},{7,6},{0,7},{9,8},{10,9},{11,1... | collective-permute-start | bytes 393224 | tf_op jit(solution)/shard_map/ppermute | solution.py:618
  18.9 9.2 %shard_map.94 = (f32[1024,256]{1,0:T(8,128)S(1)}, f32[256,256]{1,0:T(8,128)}, f32[256,8]{1,0:T(8,128)}, f32[256,256]{1,0:T(8,128)}, f32[2,8,16,32,128]{4,3,2,1,0:T(8,128)}) custom-call(f32[1024,256]{1,0:T(8,128)} %bitcast.17, f32[1024,256]{1,0:T(8,128)S(1)} %get-tuple-element.27.slope_ref, f32[32,32]{1,0:T(8,128)} %refs_0_.1, f32[5,32]{1,0:T(8,128)} %refs_1_.1, ...), custom_call_target="tpu_custom_call" | custom-call | flops 402653184 | bytes 33554432 | tf_op jit(solution)/shard_map/pallas_call | solution.py:25
  28.1 0.7 collective-permute-done.refs_0_.ybefore_ref
  28.8 0.0 collective-permute-done.1.refs_1_.yafter_ref
  28.8 0.0 collective-permute-done.2.refs_2_.zbefore_ref
  28.8 0.0 collective-permute-done.3.refs_3_.zafter_ref
  28.8 0.0 all-to-all-done
  28.8 1.2 %shard_map.95 = f32[512,128]{1,0:T(8,128)} custom-call(f32[1024,128]{1,0:T(8,128)S(1)} %bitcast.12, f32[128,256]{1,0:T(8,128)S(1)} %collective-permute-done.refs_0_.ybefore_ref, f32[128,256]{1,0:T(8,128)S(1)} %collective-permute-done.1.refs_1_.yafter_ref, f32[256,256]{1,0:T(8,128)S(1)} %collective-permute-done.2.refs_2_.zbefore_ref, ...), custom_call_target="tpu_custom_call" | custom-call | flops 16777216 | bytes 4194304 | tf_op jit(solution)/shard_map/pallas_call | solution.py:25
  30.1 3.6 %all-to-all-start.1 = ((f32[4,128,128]{2,1,0:T(8,128)}), f32[4,128,128]{2,1,0:T(8,128)S(1)}, u32[]{:S(2)}, u32[]{:S(2)}) async-start(f32[4,128,128]{2,1,0:T(8,128)} %bitcast.5), calls=%async_computation.1 | async-start | bytes 524288 | tf_op jit(solution)/shard_map/all_to_all | solution.py:661
  33.7 4.1 %shard_map.96 = (f32[768,256]{1,0:T(8,128)S(1)}, f32[16,128]{1,0:T(8,128)}) custom-call(f32[128,256]{1,0:T(8,128)S(1)} %collective-permute-done.refs_0_.ybefore_ref, f32[128,256]{1,0:T(8,128)S(1)} %collective-permute-done.1.refs_1_.yafter_ref, f32[256,256]{1,0:T(8,128)S(1)} %collective-permute-done.2.refs_2_.zbefore_ref, ...), custom_call_target="tpu_custom_call" | custom-call | flops 201326592 | bytes 3145728 | tf_op jit(solution)/shard_map/pallas_call | solution.py:25
  37.8 1.7 %all-to-all-done.1 = f32[4,128,128]{2,1,0:T(8,128)S(1)} async-done(((f32[4,128,128]{2,1,0:T(8,128)}), f32[4,128,128]{2,1,0:T(8,128)S(1)}, u32[]{:S(2)}, u32[]{:S(2)}) %all-to-all-start.1) | async-done | bytes 262176 | tf_op jit(solution)/shard_map/all_to_all | solution.py:661
  39.5 4.5 %shard_map.97 = (f32[320,128]{1,0:T(8,128)}, f32[512,128]{1,0:T(8,128)S(1)}) custom-call(f32[512,128]{1,0:T(8,128)S(1)} %bitcast.14, f32[2,8,16,32,128]{4,3,2,1,0:T(8,128)} %get-tuple-element.28.refs_4_.weights_hbm, f32[16,128]{1,0:T(8,128)} %get-tuple-element.32.part_hbm), custom_call_target="tpu_custom_call" | custom-call | flops 8388608 | bytes 6291456 | tf_op jit(solution)/shard_map/pallas_call | solution.py:25
  43.9 3.4 %all-to-all-start.2 = ((f32[4,80,128]{2,1,0:T(8,128)}), f32[4,80,128]{2,1,0:T(8,128)S(1)}, u32[]{:S(2)}, u32[]{:S(2)}) async-start(f32[4,80,128]{2,1,0:T(8,128)} %bitcast.7), calls=%async_computation.2 | async-start | bytes 327680 | tf_op jit(solution)/shard_map/all_to_all | solution.py:709
  47.3 2.1 %shard_map.98.refs_0_ = f32[2,16,8,4,32,32]{5,4,3,2,1,0:T(8,128)} custom-call(f32[512,128]{1,0:T(8,128)S(1)} %get-tuple-element.34.hat_ref), custom_call_target="tpu_custom_call" | custom-call | flops 1572864 | bytes 3145728 | tf_op jit(solution)/shard_map/pallas_call | solution.py:25
  49.5 2.8 %all-to-all-done.2 = f32[4,80,128]{2,1,0:T(8,128)S(1)} async-done(((f32[4,80,128]{2,1,0:T(8,128)}), f32[4,80,128]{2,1,0:T(8,128)S(1)}, u32[]{:S(2)}, u32[]{:S(2)}) %all-to-all-start.2) | async-done | bytes 163872 | tf_op jit(solution)/shard_map/all_to_all | solution.py:709
  52.3 1.3 %shard_map.99 = f32[640,128]{1,0:T(8,128)} custom-call(f32[320,128]{1,0:T(8,128)S(1)} %bitcast.15, f32[2,16,8,4,32,32]{5,4,3,2,1,0:T(8,128)} %shard_map.98.refs_0_), custom_call_target="tpu_custom_call" | custom-call | flops 8388608 | bytes 2097152 | tf_op jit(solution)/shard_map/pallas_call | solution.py:25
  53.6 3.7 %all-to-all-start.3 = ((f32[8,80,128]{2,1,0:T(8,128)}), f32[8,80,128]{2,1,0:T(8,128)S(1)}, u32[]{:S(2)}, u32[]{:S(2)}) async-start(f32[8,80,128]{2,1,0:T(8,128)} %bitcast.9), calls=%async_computation.3 | async-start | bytes 655360 | tf_op jit(solution)/shard_map/all_to_all | solution.py:743
  57.2 5.4 %shard_map.101 = f32[2,16,8,4,32,32]{5,4,3,2,1,0:T(8,128)} custom-call(f32[512,128]{1,0:T(8,128)S(1)} %get-tuple-element.34.hat_ref, f32[2,16,8,4,32,32]{5,4,3,2,1,0:T(8,128)} %shard_map.98.refs_0_), custom_call_target="tpu_custom_call", output_to_operand_aliasing={{}: (1, {})} | custom-call | flops 6815744 | bytes 13631488 | tf_op jit(solution)/shard_map/pallas_call | solution.py:25
  62.7 4.4 %all-to-all-done.3 = f32[8,80,128]{2,1,0:T(8,128)S(1)} async-done(((f32[8,80,128]{2,1,0:T(8,128)}), f32[8,80,128]{2,1,0:T(8,128)S(1)}, u32[]{:S(2)}, u32[]{:S(2)}) %all-to-all-start.3) | async-done | bytes 327712 | tf_op jit(solution)/shard_map/all_to_all | solution.py:743
  67.0 2.4 %shard_map.100 = (f32[1024,256]{1,0:T(8,128)}, f32[32,32]{1,0:T(8,128)}, f32[5,32]{1,0:T(8,128)}) custom-call(f32[640,128]{1,0:T(8,128)S(1)} %bitcast.13, f32[1024,256]{1,0:T(8,128)S(1)} %get-tuple-element.35.local_ref, f32[768,256]{1,0:T(8,128)S(1)} %get-tuple-element.36.fix_ref), custom_call_target="tpu_custom_call" | custom-call | flops 33554432 | bytes 3145728 | tf_op jit(solution)/shard_map/pallas_call | solution.py:25
Async XLA Ops:
  5.2 23.7 %all-to-all-start = ((f32[8,128,128]{2,1,0:T(8,128)}), f32[8,128,128]{2,1,0:T(8,128)S(1)}, u32[]{:S(2)}, u32[]{:S(2)}) async-start(f32[8,128,128]{2,1,0:T(8,128)} %bitcast.3), calls=%async_computation | async-start | bytes 1048576 | tf_op jit(solution)/shard_map/all_to_all | solution.py:610
  12.4 16.4 %collective-permute-start.2 = (f32[256,256]{1,0:T(8,128)}, f32[256,256]{1,0:T(8,128)S(1)}, u32[]{:S(2)}, u32[]{:S(2)}) collective-permute-start(f32[256,256]{1,0:T(8,128)} %get-tuple-element.25), channel_id=1, source_target_pairs={{0,8},{8,16},{16,24},{24,0},{1,9},{9,17},{17,25},{25,1},{2,10},{10... | collective-permute-start | bytes 786440 | tf_op jit(solution)/shard_map/ppermute | solution.py:614
  12.4 16.4 %collective-permute-start.3 = (f32[256,256]{1,0:T(8,128)}, f32[256,256]{1,0:T(8,128)S(1)}, u32[]{:S(2)}, u32[]{:S(2)}) collective-permute-start(f32[256,256]{1,0:T(8,128)} %get-tuple-element.26), channel_id=1, source_target_pairs={{8,0},{16,8},{24,16},{0,24},{9,1},{17,9},{25,17},{1,25},{10,2},{18... | collective-permute-start | bytes 786440 | tf_op jit(solution)/shard_map/ppermute | solution.py:618
  14.2 14.6 %collective-permute-start = (f32[128,256]{1,0:T(8,128)}, f32[128,256]{1,0:T(8,128)S(1)}, u32[]{:S(2)}, u32[]{:S(2)}) collective-permute-start(f32[128,256]{1,0:T(8,128)} %get-tuple-element.23), channel_id=1, source_target_pairs={{0,1},{1,2},{2,3},{3,4},{4,5},{5,6},{6,7},{7,0},{8,9},{9,10},{10,1... | collective-permute-start | bytes 393224 | tf_op jit(solution)/shard_map/ppermute | solution.py:614
  16.2 12.6 %collective-permute-start.1 = (f32[128,256]{1,0:T(8,128)}, f32[128,256]{1,0:T(8,128)S(1)}, u32[]{:S(2)}, u32[]{:S(2)}) collective-permute-start(f32[128,256]{1,0:T(8,128)} %get-tuple-element.24), channel_id=1, source_target_pairs={{1,0},{2,1},{3,2},{4,3},{5,4},{6,5},{7,6},{0,7},{9,8},{10,9},{11,1... | collective-permute-start | bytes 393224 | tf_op jit(solution)/shard_map/ppermute | solution.py:618
  30.1 9.4 %all-to-all-start.1 = ((f32[4,128,128]{2,1,0:T(8,128)}), f32[4,128,128]{2,1,0:T(8,128)S(1)}, u32[]{:S(2)}, u32[]{:S(2)}) async-start(f32[4,128,128]{2,1,0:T(8,128)} %bitcast.5), calls=%async_computation.1 | async-start | bytes 524288 | tf_op jit(solution)/shard_map/all_to_all | solution.py:661
  43.9 8.3 %all-to-all-start.2 = ((f32[4,80,128]{2,1,0:T(8,128)}), f32[4,80,128]{2,1,0:T(8,128)S(1)}, u32[]{:S(2)}, u32[]{:S(2)}) async-start(f32[4,80,128]{2,1,0:T(8,128)} %bitcast.7), calls=%async_computation.2 | async-start | bytes 327680 | tf_op jit(solution)/shard_map/all_to_all | solution.py:709
  53.6 13.5 %all-to-all-start.3 = ((f32[8,80,128]{2,1,0:T(8,128)}), f32[8,80,128]{2,1,0:T(8,128)S(1)}, u32[]{:S(2)}, u32[]{:S(2)}) async-start(f32[8,80,128]{2,1,0:T(8,128)} %bitcast.9), calls=%async_computation.3 | async-start | bytes 655360 | tf_op jit(solution)/shard_map/all_to_all | solution.py:743

commit v6 on v5

--- a/solution.py
+++ b/solution.py
@@ -725,7 +725,7 @@
             input_output_aliases={1: 0} if before else {},
         )
 
-    few = max(1, kz * 3 // 16)
+    few = max(1, kz * 7 // 16)
     grad_half = gradient(0, few)
 
     send = call(

time: 69.9 us -> 69.9 us (level)
    all_to_all x1, waiting for transfers between devices: 2.8 us -> 1.45 us  [per_device(): returned = exchange(send, 'gz')]
    all_to_all x1, waiting for transfers between devices: 4.37 us -> 5.67 us  [per_device(): arrived = exchange(send, 'gy')]
where the time goes in v6:
time: 69.9 us; the launch traced here: 69.4 us
  Pallas kernels  34.8 us (50%)
  starting transfers between devices  24.3 us (35%)
  waiting for transfers between devices  9.52 us (14%)
  between operations  0.72 us (1%)
    pallas_call x9, Pallas kernels, call(): pl.pallas_call(body, out_shape=outs, scratch_shapes=list(scratch), compil...  34.8 us
    all_to_all x1, starting transfers between devices, per_device(): lines = exchange(send, 'gy')  7.26 us
    all_to_all x1, waiting for transfers between devices, per_device(): arrived = exchange(send, 'gy')  5.67 us
    ppermute x2, starting transfers between devices, from_above(): lax.ppermute(values, axis, [((i + 1) % size, i) for i in range(size)])  4.44 us
    all_to_all x1, starting transfers between devices, per_device(): arrived = exchange(send, 'gy')  3.65 us
    all_to_all x1, starting transfers between devices, per_device(): owned = exchange(send, 'gz')  3.59 us
    all_to_all x1, starting transfers between devices, per_device(): returned = exchange(send, 'gz')  3.36 us
    ppermute x2, starting transfers between devices, from_below(): lax.ppermute(values, axis, [(i, (i + 1) % size) for i in range(size)])  2.02 us
  transfers between devices with their start and end apart: 8, of which 4 were waited for; matrix products, arithmetic and copies ran while one was open for 0% of the time, Pallas kernels for 30%

profile of v6, /device:TPU:0, one launch (start us, length us, event | category | flops | bytes accessed | tf_op | source)
XLA Modules:
  0.0 69.4 jit_solution(15064181960905779260)
XLA Ops:
  0.6 4.5 %shard_map.93 = (f32[1024,256]{1,0:T(8,128)S(1)}, f32[1024,128]{1,0:T(8,128)}, f32[128,256]{1,0:T(8,128)}, f32[128,256]{1,0:T(8,128)}, f32[256,256]{1,0:T(8,128)}, /*index=5*/f32[256,256]{1,0:T(8,128)}) custom-call(f32[1024,256]{1,0:T(8,128)} %bitcast.16, f32[1024,256]{1,0:T(8,128)} %bitcast.19, f32[1024,256]{1,0:T(8,128)} %bitcast.20), custom_call_target="tpu_custom_call" | custom-call | flops 67108864 | bytes 6291456 | tf_op jit(solution)/shard_map/pallas_call | solution.py:25
  5.2 7.3 %all-to-all-start = ((f32[8,128,128]{2,1,0:T(8,128)}), f32[8,128,128]{2,1,0:T(8,128)S(1)}, u32[]{:S(2)}, u32[]{:S(2)}) async-start(f32[8,128,128]{2,1,0:T(8,128)} %bitcast.3), calls=%async_computation | async-start | bytes 1048576 | tf_op jit(solution)/shard_map/all_to_all | solution.py:610
  12.4 0.0 collective-permute-start.2
  12.4 1.7 %collective-permute-start.3 = (f32[256,256]{1,0:T(8,128)}, f32[256,256]{1,0:T(8,128)S(1)}, u32[]{:S(2)}, u32[]{:S(2)}) collective-permute-start(f32[256,256]{1,0:T(8,128)} %get-tuple-element.26), channel_id=1, source_target_pairs={{8,0},{16,8},{24,16},{0,24},{9,1},{17,9},{25,17},{1,25},{10,2},{18... | collective-permute-start | bytes 786440 | tf_op jit(solution)/shard_map/ppermute | solution.py:618
  14.2 2.0 %collective-permute-start = (f32[128,256]{1,0:T(8,128)}, f32[128,256]{1,0:T(8,128)S(1)}, u32[]{:S(2)}, u32[]{:S(2)}) collective-permute-start(f32[128,256]{1,0:T(8,128)} %get-tuple-element.23), channel_id=1, source_target_pairs={{0,1},{1,2},{2,3},{3,4},{4,5},{5,6},{6,7},{7,0},{8,9},{9,10},{10,1... | collective-permute-start | bytes 393224 | tf_op jit(solution)/shard_map/ppermute | solution.py:614
  16.2 2.7 %collective-permute-start.1 = (f32[128,256]{1,0:T(8,128)}, f32[128,256]{1,0:T(8,128)S(1)}, u32[]{:S(2)}, u32[]{:S(2)}) collective-permute-start(f32[128,256]{1,0:T(8,128)} %get-tuple-element.24), channel_id=1, source_target_pairs={{1,0},{2,1},{3,2},{4,3},{5,4},{6,5},{7,6},{0,7},{9,8},{10,9},{11,1... | collective-permute-start | bytes 393224 | tf_op jit(solution)/shard_map/ppermute | solution.py:618
  18.9 9.2 %shard_map.94 = (f32[1024,256]{1,0:T(8,128)S(1)}, f32[256,256]{1,0:T(8,128)}, f32[256,8]{1,0:T(8,128)}, f32[256,256]{1,0:T(8,128)}, f32[2,8,16,32,128]{4,3,2,1,0:T(8,128)}) custom-call(f32[1024,256]{1,0:T(8,128)} %bitcast.17, f32[1024,256]{1,0:T(8,128)S(1)} %get-tuple-element.27.slope_ref, f32[32,32]{1,0:T(8,128)} %refs_0_.1, f32[5,32]{1,0:T(8,128)} %refs_1_.1, ...), custom_call_target="tpu_custom_call" | custom-call | flops 402653184 | bytes 33554432 | tf_op jit(solution)/shard_map/pallas_call | solution.py:25
  28.1 0.7 collective-permute-done.refs_0_.ybefore_ref
  28.8 0.0 collective-permute-done.1.refs_1_.yafter_ref
  28.8 0.0 collective-permute-done.2.refs_2_.zbefore_ref
  28.8 0.0 collective-permute-done.3.refs_3_.zafter_ref
  28.8 0.0 all-to-all-done
  28.8 1.2 %shard_map.95 = f32[512,128]{1,0:T(8,128)} custom-call(f32[1024,128]{1,0:T(8,128)S(1)} %bitcast.12, f32[128,256]{1,0:T(8,128)S(1)} %collective-permute-done.refs_0_.ybefore_ref, f32[128,256]{1,0:T(8,128)S(1)} %collective-permute-done.1.refs_1_.yafter_ref, f32[256,256]{1,0:T(8,128)S(1)} %collective-permute-done.2.refs_2_.zbefore_ref, ...), custom_call_target="tpu_custom_call" | custom-call | flops 16777216 | bytes 4194304 | tf_op jit(solution)/shard_map/pallas_call | solution.py:25
  30.1 3.6 %all-to-all-start.1 = ((f32[4,128,128]{2,1,0:T(8,128)}), f32[4,128,128]{2,1,0:T(8,128)S(1)}, u32[]{:S(2)}, u32[]{:S(2)}) async-start(f32[4,128,128]{2,1,0:T(8,128)} %bitcast.5), calls=%async_computation.1 | async-start | bytes 524288 | tf_op jit(solution)/shard_map/all_to_all | solution.py:661
  33.7 4.1 %shard_map.96 = (f32[768,256]{1,0:T(8,128)S(1)}, f32[16,128]{1,0:T(8,128)}) custom-call(f32[128,256]{1,0:T(8,128)S(1)} %collective-permute-done.refs_0_.ybefore_ref, f32[128,256]{1,0:T(8,128)S(1)} %collective-permute-done.1.refs_1_.yafter_ref, f32[256,256]{1,0:T(8,128)S(1)} %collective-permute-done.2.refs_2_.zbefore_ref, ...), custom_call_target="tpu_custom_call" | custom-call | flops 201326592 | bytes 3145728 | tf_op jit(solution)/shard_map/pallas_call | solution.py:25
  37.8 1.7 %all-to-all-done.1 = f32[4,128,128]{2,1,0:T(8,128)S(1)} async-done(((f32[4,128,128]{2,1,0:T(8,128)}), f32[4,128,128]{2,1,0:T(8,128)S(1)}, u32[]{:S(2)}, u32[]{:S(2)}) %all-to-all-start.1) | async-done | bytes 262176 | tf_op jit(solution)/shard_map/all_to_all | solution.py:661
  39.5 4.5 %shard_map.97 = (f32[320,128]{1,0:T(8,128)}, f32[512,128]{1,0:T(8,128)S(1)}) custom-call(f32[512,128]{1,0:T(8,128)S(1)} %bitcast.14, f32[2,8,16,32,128]{4,3,2,1,0:T(8,128)} %get-tuple-element.28.refs_4_.weights_hbm, f32[16,128]{1,0:T(8,128)} %get-tuple-element.32.part_hbm), custom_call_target="tpu_custom_call" | custom-call | flops 8388608 | bytes 6291456 | tf_op jit(solution)/shard_map/pallas_call | solution.py:25
  43.9 3.4 %all-to-all-start.2 = ((f32[4,80,128]{2,1,0:T(8,128)}), f32[4,80,128]{2,1,0:T(8,128)S(1)}, u32[]{:S(2)}, u32[]{:S(2)}) async-start(f32[4,80,128]{2,1,0:T(8,128)} %bitcast.7), calls=%async_computation.2 | async-start | bytes 327680 | tf_op jit(solution)/shard_map/all_to_all | solution.py:709
  47.3 3.5 %shard_map.98.refs_0_ = f32[2,16,8,4,32,32]{5,4,3,2,1,0:T(8,128)} custom-call(f32[512,128]{1,0:T(8,128)S(1)} %get-tuple-element.34.hat_ref), custom_call_target="tpu_custom_call" | custom-call | flops 3670016 | bytes 7340032 | tf_op jit(solution)/shard_map/pallas_call | solution.py:25
  50.8 1.4 %all-to-all-done.2 = f32[4,80,128]{2,1,0:T(8,128)S(1)} async-done(((f32[4,80,128]{2,1,0:T(8,128)}), f32[4,80,128]{2,1,0:T(8,128)S(1)}, u32[]{:S(2)}, u32[]{:S(2)}) %all-to-all-start.2) | async-done | bytes 163872 | tf_op jit(solution)/shard_map/all_to_all | solution.py:709
  52.3 1.3 %shard_map.99 = f32[640,128]{1,0:T(8,128)} custom-call(f32[320,128]{1,0:T(8,128)S(1)} %bitcast.15, f32[2,16,8,4,32,32]{5,4,3,2,1,0:T(8,128)} %shard_map.98.refs_0_), custom_call_target="tpu_custom_call" | custom-call | flops 8388608 | bytes 2097152 | tf_op jit(solution)/shard_map/pallas_call | solution.py:25
  53.6 3.7 %all-to-all-start.3 = ((f32[8,80,128]{2,1,0:T(8,128)}), f32[8,80,128]{2,1,0:T(8,128)S(1)}, u32[]{:S(2)}, u32[]{:S(2)}) async-start(f32[8,80,128]{2,1,0:T(8,128)} %bitcast.9), calls=%async_computation.3 | async-start | bytes 655360 | tf_op jit(solution)/shard_map/all_to_all | solution.py:743
  57.2 4.1 %shard_map.101 = f32[2,16,8,4,32,32]{5,4,3,2,1,0:T(8,128)} custom-call(f32[512,128]{1,0:T(8,128)S(1)} %get-tuple-element.34.hat_ref, f32[2,16,8,4,32,32]{5,4,3,2,1,0:T(8,128)} %shard_map.98.refs_0_), custom_call_target="tpu_custom_call", output_to_operand_aliasing={{}: (1, {})} | custom-call | flops 4718592 | bytes 9437184 | tf_op jit(solution)/shard_map/pallas_call | solution.py:25
  61.4 5.7 %all-to-all-done.3 = f32[8,80,128]{2,1,0:T(8,128)S(1)} async-done(((f32[8,80,128]{2,1,0:T(8,128)}), f32[8,80,128]{2,1,0:T(8,128)S(1)}, u32[]{:S(2)}, u32[]{:S(2)}) %all-to-all-start.3) | async-done | bytes 327712 | tf_op jit(solution)/shard_map/all_to_all | solution.py:743
  67.0 2.4 %shard_map.100 = (f32[1024,256]{1,0:T(8,128)}, f32[32,32]{1,0:T(8,128)}, f32[5,32]{1,0:T(8,128)}) custom-call(f32[640,128]{1,0:T(8,128)S(1)} %bitcast.13, f32[1024,256]{1,0:T(8,128)S(1)} %get-tuple-element.35.local_ref, f32[768,256]{1,0:T(8,128)S(1)} %get-tuple-element.36.fix_ref), custom_call_target="tpu_custom_call" | custom-call | flops 33554432 | bytes 3145728 | tf_op jit(solution)/shard_map/pallas_call | solution.py:25
Async XLA Ops:
  5.2 23.7 %all-to-all-start = ((f32[8,128,128]{2,1,0:T(8,128)}), f32[8,128,128]{2,1,0:T(8,128)S(1)}, u32[]{:S(2)}, u32[]{:S(2)}) async-start(f32[8,128,128]{2,1,0:T(8,128)} %bitcast.3), calls=%async_computation | async-start | bytes 1048576 | tf_op jit(solution)/shard_map/all_to_all | solution.py:610
  12.4 16.4 %collective-permute-start.2 = (f32[256,256]{1,0:T(8,128)}, f32[256,256]{1,0:T(8,128)S(1)}, u32[]{:S(2)}, u32[]{:S(2)}) collective-permute-start(f32[256,256]{1,0:T(8,128)} %get-tuple-element.25), channel_id=1, source_target_pairs={{0,8},{8,16},{16,24},{24,0},{1,9},{9,17},{17,25},{25,1},{2,10},{10... | collective-permute-start | bytes 786440 | tf_op jit(solution)/shard_map/ppermute | solution.py:614
  12.4 16.4 %collective-permute-start.3 = (f32[256,256]{1,0:T(8,128)}, f32[256,256]{1,0:T(8,128)S(1)}, u32[]{:S(2)}, u32[]{:S(2)}) collective-permute-start(f32[256,256]{1,0:T(8,128)} %get-tuple-element.26), channel_id=1, source_target_pairs={{8,0},{16,8},{24,16},{0,24},{9,1},{17,9},{25,17},{1,25},{10,2},{18... | collective-permute-start | bytes 786440 | tf_op jit(solution)/shard_map/ppermute | solution.py:618
  14.2 14.6 %collective-permute-start = (f32[128,256]{1,0:T(8,128)}, f32[128,256]{1,0:T(8,128)S(1)}, u32[]{:S(2)}, u32[]{:S(2)}) collective-permute-start(f32[128,256]{1,0:T(8,128)} %get-tuple-element.23), channel_id=1, source_target_pairs={{0,1},{1,2},{2,3},{3,4},{4,5},{5,6},{6,7},{7,0},{8,9},{9,10},{10,1... | collective-permute-start | bytes 393224 | tf_op jit(solution)/shard_map/ppermute | solution.py:614
  16.2 12.6 %collective-permute-start.1 = (f32[128,256]{1,0:T(8,128)}, f32[128,256]{1,0:T(8,128)S(1)}, u32[]{:S(2)}, u32[]{:S(2)}) collective-permute-start(f32[128,256]{1,0:T(8,128)} %get-tuple-element.24), channel_id=1, source_target_pairs={{1,0},{2,1},{3,2},{4,3},{5,4},{6,5},{7,6},{0,7},{9,8},{10,9},{11,1... | collective-permute-start | bytes 393224 | tf_op jit(solution)/shard_map/ppermute | solution.py:618
  30.1 9.4 %all-to-all-start.1 = ((f32[4,128,128]{2,1,0:T(8,128)}), f32[4,128,128]{2,1,0:T(8,128)S(1)}, u32[]{:S(2)}, u32[]{:S(2)}) async-start(f32[4,128,128]{2,1,0:T(8,128)} %bitcast.5), calls=%async_computation.1 | async-start | bytes 524288 | tf_op jit(solution)/shard_map/all_to_all | solution.py:661
  43.9 8.3 %all-to-all-start.2 = ((f32[4,80,128]{2,1,0:T(8,128)}), f32[4,80,128]{2,1,0:T(8,128)S(1)}, u32[]{:S(2)}, u32[]{:S(2)}) async-start(f32[4,80,128]{2,1,0:T(8,128)} %bitcast.7), calls=%async_computation.2 | async-start | bytes 327680 | tf_op jit(solution)/shard_map/all_to_all | solution.py:709
  53.6 13.5 %all-to-all-start.3 = ((f32[8,80,128]{2,1,0:T(8,128)}), f32[8,80,128]{2,1,0:T(8,128)S(1)}, u32[]{:S(2)}, u32[]{:S(2)}) async-start(f32[8,80,128]{2,1,0:T(8,128)} %bitcast.9), calls=%async_computation.3 | async-start | bytes 655360 | tf_op jit(solution)/shard_map/all_to_all | solution.py:743
